TPU v7x, 32 devices: a whole 2x2x4 slice. The times are simulated.
32 devices in a mesh: cluster: 4 (over x, core), shard: 8 (over z, y).
Axes of the slice: x: 2, y: 2, z: 4, core: 2. Of those that a mesh axis runs over, the one named last changes fastest.
Arguments:
- flow_start: float32 [512, 256], P(('cluster', 'shard')), may hold values from 0 to 1
- demand: float32 [512, 256], P(('cluster', 'shard')), may hold values from 0.25 to 2
- utility: float32 [512, 256], P(('cluster', 'shard')), may hold values from 1 to 16
- path_count: int32 [512], P(('cluster', 'shard')), may hold values from 1 to 256, as said below
- cluster_size: int32 [4], P('cluster'), may hold values from 1 to 16, as said below
- incidence: float32 [1024, 256, 128], P(('cluster', 'shard')), may hold values from 0 to 1, as said below
- inc_path: int32 [1024], P(('cluster', 'shard')), may hold values from 0 to 127, as said below
- inc_edge: int32 [1024], P(('cluster', 'shard')), may hold values from 0 to 6
- capacity: float32 [224, 128], P(('cluster', 'shard')), may hold values from 0.25 to 4
- dual_start: float32 [224, 128], P(('cluster', 'shard')), may hold values from 0 to 7
- partner: int32 [4, 3], P('cluster'), may hold values from 0 to 3, as said below
Outputs:
- flows: float32 [512, 256], P(('cluster', 'shard'))
- duals: float32 [224, 128], P(('cluster', 'shard'))
Inputs may be any that keep to these rules, and one draw needn't show every extreme that they name: `path_count`: some path block has 256 live paths. `cluster_size`: some cluster has 16. partner[c, k] = q implies partner[q, k] = c; the partners of a cluster are distinct and differ from it. `incidence`: every entry is 0 or 1. Among the 32 incidence blocks of one device, at most 8 have the same value of inc_path // 16, and on every device some value is taken by exactly 8.
All inputs are finite; a program needn't handle non-finite values.
Results may differ from a plain program's by a relative error of at most 0.0001.
Values sent between devices are 32-bit elements; how exact they have to be, the bound alone decides.
No kernel may reach another device: no remote copies, remote signals or barrier semaphores. Data moves between devices by JAX's collectives and lax.ppermute only.
A program may use at most 64 MiB of HBM per device.

v0:
```python
import jax
import jax.numpy as jnp
from jax import lax
from jax.sharding import PartitionSpec as P

ITERS = 3


def body(
    flow_start,
    demand,
    utility,
    path_count,
    cluster_size,
    incidence,
    inc_path,
    inc_edge,
    capacity,
    dual_start,
    partner,
):
    exact_mode = lax.Precision.HIGHEST
    block_count, path_width = flow_start.shape
    inc_count = incidence.shape[0]
    edge_width = incidence.shape[2]
    local_blocks = capacity.shape[0]
    slot_count = partner.shape[1]
    interior = local_blocks - slot_count
    clusters = lax.axis_size("cluster")
    norm_bound = max(
        2, inc_count * inc_count * path_width * edge_width // (1024 * local_blocks * block_count)
    )
    capacity_unit = float(max(1, inc_count * path_width // (160 * local_blocks)))
    step_size = 1.0 / (2.0 * norm_bound)
    block_ids = jnp.arange(block_count, dtype=jnp.int32)
    path_ids = jnp.arange(path_width, dtype=jnp.int32)
    live_mask = (
        (block_ids < cluster_size[0])[:, None] & (path_ids[None, :] < path_count[:, None])
    ).astype(jnp.float32)
    edge_pick = (jnp.arange(local_blocks, dtype=jnp.int32)[:, None] == inc_edge[None, :]).astype(
        jnp.float32
    )
    partner_pick = (jnp.arange(clusters, dtype=jnp.int32)[:, None] == partner[0][None, :]).astype(
        jnp.float32
    )

    def twin_of(border):
        outgoing = jnp.dot(partner_pick, border, precision=exact_mode)
        incoming = lax.all_to_all(outgoing, "cluster", split_axis=0, concat_axis=0, tiled=True)
        return jnp.dot(partner_pick.T, incoming, precision=exact_mode)

    cap_border = capacity[interior:]
    dual_border = dual_start[interior:]
    outgoing = jnp.einsum(
        "ck,mke->cme", partner_pick, jnp.stack([cap_border, dual_border]), precision=exact_mode
    )
    incoming = lax.all_to_all(outgoing, "cluster", split_axis=0, concat_axis=0, tiled=True)
    twins = jnp.einsum("ck,cme->mke", partner_pick, incoming, precision=exact_mode)
    limit = capacity_unit * jnp.concatenate(
        [capacity[:interior], 0.5 * (cap_border + twins[0])], axis=0
    )
    duals = jnp.concatenate([dual_start[:interior], 0.5 * (dual_border + twins[1])], axis=0)

    def load_of_rows(picked):
        terms = jnp.einsum("ipe,ip->ie", incidence, picked, precision=exact_mode)
        own_load = jnp.dot(edge_pick, terms, precision=exact_mode)
        border = own_load[interior:]
        return jnp.concatenate([own_load[:interior], border + twin_of(border)], axis=0)

    def total_load(gathered):
        return load_of_rows(jnp.take(gathered, inc_path, axis=0))

    def settle(load, duals_now):
        split = jnp.minimum(limit, load + duals_now)
        return (split, duals_now + load - split)

    flows = jnp.minimum(jnp.maximum(flow_start, 0.0), demand) * live_mask

    def shared_flows(flows_now):
        return lax.all_gather(flows_now, "shard", axis=0, tiled=True)

    load = total_load(shared_flows(flows))
    split, duals = settle(load, duals)
    for iteration in range(ITERS):
        residual = load - split + duals
        residual_picked = jnp.take(residual, inc_edge, axis=0)
        terms = jnp.einsum("ipe,ie->ip", incidence, residual_picked, precision=exact_mode)
        rows_pick = (
            jnp.arange(block_count * lax.axis_size("shard"), dtype=jnp.int32)[:, None]
            == inc_path[None, :]
        ).astype(jnp.float32)
        gradient = lax.psum_scatter(
            jnp.dot(rows_pick, terms, precision=exact_mode),
            "shard",
            scatter_dimension=0,
            tiled=True,
        )
        flows = (
            jnp.minimum(jnp.maximum(flows - step_size * (gradient - utility), 0.0), demand)
            * live_mask
        )
        load = total_load(shared_flows(flows))
        split, duals = settle(load, duals)
    return (flows, duals)


def solution(mesh):
    return jax.shard_map(
        body,
        mesh=mesh,
        in_specs=(
            P(("cluster", "shard"), None),
            P(("cluster", "shard"), None),
            P(("cluster", "shard"), None),
            P(("cluster", "shard")),
            P("cluster"),
            P(("cluster", "shard"), None, None),
            P(("cluster", "shard")),
            P(("cluster", "shard")),
            P(("cluster", "shard"), None),
            P(("cluster", "shard"), None),
            P("cluster", None),
        ),
        out_specs=(P(("cluster", "shard"), None), P(("cluster", "shard"), None)),
        check_vma=False,
    )
```

profile of v0, /device:TPU:0, one launch (start us, length us, event | category | flops | bytes accessed | tf_op | source)
XLA Modules:
  0.0 403.7 jit_solution(15539624812091651235)
XLA Ops:
  10.0 32.3 %all_gather.12 = f32[128,256]{1,0:T(8,128)S(1)} all-gather(f32[16,256]{1,0:T(8,128)S(1)} %minimum_select_fusion.3), channel_id=1, replica_groups=mesh['cluster'=4,'shard'=8] {'shard'}, dimensions={0}, use_global_device_ids=true | all-gather | bytes 147456 | tf_op jit(solution)/shard_map/all_gather | solution.py:80
  43.1 4.4 %fusion.15 = f32[32,1,128]{2,1,0:T(1,128)S(1)} fusion(f32[32,256,128]{2,1,0:T(8,128)} %param.20, f32[32,256,1]{1,0,2:T(8,128)S(1)} %select_bitcast_fusion.3), kind=kOutput, calls=%fused_computation.28 | convolution fusion | flops 12582912 | bytes 4243456 | tf_op jit(solution)/shard_map/ipe,ip->ie/dot_general | solution.py:65
  48.4 3.2 all-to-all-start
  52.6 2.7 all-to-all-done
  55.3 3.2 all-to-all-start.1
  58.8 3.5 all-to-all-done.1
  63.1 5.7 %fusion.61 = f32[32,1,256]{2,1,0:T(1,128)S(1)} fusion(f32[32,128,1]{1,2,0:T(1,128)S(1)} %bitcast.95, f32[32,256,128]{2,1,0:T(8,128)} %param.20), kind=kOutput, calls=%fused_computation.110 | convolution fusion | flops 12582912 | bytes 4243456 | tf_op jit(solution)/shard_map/ipe,ie->ip/dot_general | solution.py:87
  69.7 61.0 %reduce-scatter.4.cloned.1.call-done = f32[16,256]{1,0:T(8,128)} async-done(((f32[128,256]{1,0:T(8,128)}), f32[16,256]{1,0:T(8,128)}) %reduce-scatter.4.cloned.1.call-update) | async-done | bytes 16400 | tf_op jit(solution)/shard_map/reduce_scatter | solution.py:92
  131.5 30.6 %all_gather.13 = f32[128,256]{1,0:T(8,128)S(1)} all-gather(f32[16,256]{1,0:T(8,128)S(1)} %minimum_select_fusion.2), channel_id=1, replica_groups=mesh['cluster'=4,'shard'=8] {'shard'}, dimensions={0}, use_global_device_ids=true | all-gather | bytes 147456 | tf_op jit(solution)/shard_map/all_gather | solution.py:80
  162.8 4.3 %fusion.12 = f32[32,1,128]{2,1,0:T(1,128)S(1)} fusion(f32[32,256,128]{2,1,0:T(8,128)} %param.20, f32[32,256,1]{1,0,2:T(8,128)S(1)} %select_bitcast_fusion.2), kind=kOutput, calls=%fused_computation.25 | convolution fusion | flops 12582912 | bytes 4243456 | tf_op jit(solution)/shard_map/ipe,ip->ie/dot_general | solution.py:65
  168.1 3.2 all-to-all-start.2
  171.6 3.4 all-to-all-done.2
  175.8 5.7 %fusion.62 = f32[32,1,256]{2,1,0:T(1,128)S(1)} fusion(f32[32,128,1]{1,2,0:T(1,128)S(1)} %bitcast.97, f32[32,256,128]{2,1,0:T(8,128)} %param.20), kind=kOutput, calls=%fused_computation.111 | convolution fusion | flops 12582912 | bytes 4243456 | tf_op jit(solution)/shard_map/ipe,ie->ip/dot_general | solution.py:87
  182.4 59.1 %reduce-scatter.6.cloned.1.call-done = f32[16,256]{1,0:T(8,128)} async-done(((f32[128,256]{1,0:T(8,128)}), f32[16,256]{1,0:T(8,128)}) %reduce-scatter.6.cloned.1.call-update) | async-done | bytes 16400 | tf_op jit(solution)/shard_map/reduce_scatter | solution.py:92
  242.3 30.6 %all_gather.14 = f32[128,256]{1,0:T(8,128)S(1)} all-gather(f32[16,256]{1,0:T(8,128)S(1)} %minimum_select_fusion.1), channel_id=1, replica_groups=mesh['cluster'=4,'shard'=8] {'shard'}, dimensions={0}, use_global_device_ids=true | all-gather | bytes 147456 | tf_op jit(solution)/shard_map/all_gather | solution.py:80
  273.5 4.3 %fusion.9 = f32[32,1,128]{2,1,0:T(1,128)S(1)} fusion(f32[32,256,128]{2,1,0:T(8,128)} %param.20, f32[32,256,1]{1,0,2:T(8,128)S(1)} %select_bitcast_fusion.1), kind=kOutput, calls=%fused_computation.22 | convolution fusion | flops 12582912 | bytes 4243456 | tf_op jit(solution)/shard_map/ipe,ip->ie/dot_general | solution.py:65
  278.8 3.2 all-to-all-start.3
  282.1 3.6 all-to-all-done.3
  286.6 5.7 %fusion.63 = f32[32,1,256]{2,1,0:T(1,128)S(1)} fusion(f32[32,128,1]{1,2,0:T(1,128)S(1)} %bitcast.93, f32[32,256,128]{2,1,0:T(8,128)} %param.20), kind=kOutput, calls=%fused_computation.112 | convolution fusion | flops 12582912 | bytes 4243456 | tf_op jit(solution)/shard_map/ipe,ie->ip/dot_general | solution.py:87
  293.1 59.1 %reduce-scatter.8.cloned.1.call-done = f32[16,256]{1,0:T(8,128)} async-done(((f32[128,256]{1,0:T(8,128)}), f32[16,256]{1,0:T(8,128)}) %reduce-scatter.8.cloned.1.call-update) | async-done | bytes 16400 | tf_op jit(solution)/shard_map/reduce_scatter | solution.py:92
  353.0 30.6 %all_gather.15 = f32[128,256]{1,0:T(8,128)S(1)} all-gather(f32[16,256]{1,0:T(8,128)S(1)} %minimum_select_fusion), channel_id=1, replica_groups=mesh['cluster'=4,'shard'=8] {'shard'}, dimensions={0}, use_global_device_ids=true | all-gather | bytes 147456 | tf_op jit(solution)/shard_map/all_gather | solution.py:80
  384.2 4.3 %fusion.6 = f32[32,1,128]{2,1,0:T(1,128)S(1)} fusion(f32[32,256,128]{2,1,0:T(8,128)} %param.20, f32[32,256,1]{1,0,2:T(8,128)S(1)} %select_bitcast_fusion), kind=kOutput, calls=%fused_computation.19 | convolution fusion | flops 12582912 | bytes 4243456 | tf_op jit(solution)/shard_map/ipe,ip->ie/dot_general | solution.py:65
  389.5 3.2 all-to-all-start.4
  392.8 3.6 all-to-all-done.4
  (81 shorter events, 18.5 us)
Async XLA Ops:
  7.2 40.2 %copy-start.6 = (s32[32]{0:T(128)S(1)}, s32[32]{0:T(128)}, u32[]{:S(2)}) copy-start(s32[32]{0:T(128)} %param.22) | copy-start | bytes 388
  7.2 40.4 %copy-start.9 = (s32[1,3]{1,0:T(1,128)S(1)}, s32[1,3]{1,0:T(1,128)}, u32[]{:S(2)}) copy-start(s32[1,3]{1,0:T(1,128)} %param.25) | copy-start | bytes 40
  7.2 44.5 %copy-start.4 = (f32[7,128]{1,0:T(8,128)S(1)}, f32[7,128]{1,0:T(8,128)}, u32[]{:S(2)}) copy-start(f32[7,128]{1,0:T(8,128)} %param.24) | copy-start | bytes 10756
  7.2 44.5 %copy-start.5 = (f32[7,128]{1,0:T(8,128)S(1)}, f32[7,128]{1,0:T(8,128)}, u32[]{:S(2)}) copy-start(f32[7,128]{1,0:T(8,128)} %param.23) | copy-start | bytes 10756
  43.0 25.8 %copy-start.8 = (s32[32]{0:T(128)S(1)}, s32[32]{0:T(128)}, u32[]{:S(2)}) copy-start(s32[32]{0:T(128)} %param.21) | copy-start | bytes 388
  43.0 87.7 %copy-start = (f32[16,256]{1,0:T(8,128)S(1)}, f32[16,256]{1,0:T(8,128)}, u32[]{:S(2)}) copy-start(f32[16,256]{1,0:T(8,128)} %param.16) | copy-start | bytes 49156
  43.0 87.7 %copy-start.1 = (f32[16,256]{1,0:T(8,128)S(1)}, f32[16,256]{1,0:T(8,128)}, u32[]{:S(2)}) copy-start(f32[16,256]{1,0:T(8,128)} %param.17) | copy-start | bytes 49156
  43.0 87.7 %copy-start.2 = (f32[16,256]{1,0:T(8,128)S(1)}, f32[16,256]{1,0:T(8,128)}, u32[]{:S(2)}) copy-start(f32[16,256]{1,0:T(8,128)} %param.15) | copy-start | bytes 49156
  43.0 87.7 %copy-start.7 = (s32[16]{0:T(128)S(1)}, s32[16]{0:T(128)}, u32[]{:S(2)}) copy-start(s32[16]{0:T(128)} %param.18) | copy-start | bytes 196
  48.4 6.9 %all-to-all-start = ((f32[4,1,128]{2,1,0:T(1,128)}), f32[4,1,128]{2,1,0:T(1,128)S(1)}, u32[]{:S(2)}, u32[]{:S(2)}) async-start(f32[4,1,128]{2,1,0:T(1,128)} %bitcast.6), calls=%async_computation | async-start | bytes 4096 | tf_op jit(solution)/shard_map/all_to_all | solution.py:49
  55.3 7.0 %all-to-all-start.1 = ((f32[4,2,128]{2,1,0:T(2,128)}), f32[4,2,128]{2,1,0:T(2,128)S(1)}, u32[]{:S(2)}, u32[]{:S(2)}) async-start(f32[4,2,128]{2,1,0:T(2,128)} %copy.20), calls=%async_computation.1 | async-start | bytes 8192 | tf_op jit(solution)/shard_map/all_to_all | solution.py:57
  58.5 72.2 %reduce-scatter.4.cloned.1.call-start = ((), (), s32[]{:S(2)}) async-start(), calls=%async_computation.8 | async-start | bytes 147456 | tf_op jit(solution)/shard_map/reduce_scatter | solution.py:92
  168.1 6.9 %all-to-all-start.2 = ((f32[4,1,128]{2,1,0:T(1,128)}), f32[4,1,128]{2,1,0:T(1,128)S(1)}, u32[]{:S(2)}, u32[]{:S(2)}) async-start(f32[4,1,128]{2,1,0:T(1,128)} %bitcast.21), calls=%async_computation.3 | async-start | bytes 4096 | tf_op jit(solution)/shard_map/all_to_all | solution.py:49
  171.3 70.1 %reduce-scatter.6.cloned.1.call-start = ((), (), s32[]{:S(2)}) async-start(), calls=%async_computation.9 | async-start | bytes 147456 | tf_op jit(solution)/shard_map/reduce_scatter | solution.py:92
  278.8 6.9 %all-to-all-start.3 = ((f32[4,1,128]{2,1,0:T(1,128)}), f32[4,1,128]{2,1,0:T(1,128)S(1)}, u32[]{:S(2)}, u32[]{:S(2)}) async-start(f32[4,1,128]{2,1,0:T(1,128)} %bitcast.30), calls=%async_computation.5 | async-start | bytes 4096 | tf_op jit(solution)/shard_map/all_to_all | solution.py:49
  282.0 70.1 %reduce-scatter.8.cloned.1.call-start = ((), (), s32[]{:S(2)}) async-start(), calls=%async_computation.10 | async-start | bytes 147456 | tf_op jit(solution)/shard_map/reduce_scatter | solution.py:92
  353.0 44.2 %copy-start.3 = (f32[16,256]{1,0:T(8,128)}, f32[16,256]{1,0:T(8,128)S(1)}, u32[]{:S(2)}) copy-start(f32[16,256]{1,0:T(8,128)S(1)} %minimum_select_fusion) | copy-start | bytes 49156
  389.5 6.9 %all-to-all-start.4 = ((f32[4,1,128]{2,1,0:T(1,128)}), f32[4,1,128]{2,1,0:T(1,128)S(1)}, u32[]{:S(2)}, u32[]{:S(2)}) async-start(f32[4,1,128]{2,1,0:T(1,128)} %bitcast.39), calls=%async_computation.7 | async-start | bytes 4096 | tf_op jit(solution)/shard_map/all_to_all | solution.py:49
Sparse Core Ops, SparseCore 0:
  69.8 60.8 reduce-scatter.3
  182.5 58.9 reduce-scatter.5
  293.2 58.9 reduce-scatter.7
where the time goes:
time: 405 us; the launch traced here: 404 us
  waiting for transfers between devices  196 us (48%)
  blocking collectives  124 us (31%)
  matrix products  42 us (10%)
  starting transfers between devices  16.4 us (4%)
  between operations  14.7 us (4%)
  other arithmetic  5.78 us (1%)
  local copies, waits for them, and re-layouts  4.79 us (1%)
    reduce_scatter x3, waiting for transfers between devices, body(): lax.psum_scatter(jnp.dot(rows_pick, terms, precision=exact_mode), 'shard'...  179 us
    all_gather x4, blocking collectives, shared_flows(): return lax.all_gather(flows_now, 'shard', axis=0, tiled=True)  124 us
    dot_general x4, matrix products, load_of_rows(): terms = jnp.einsum('ipe,ip->ie', incidence, picked, precision=exact_mode)  17.3 us
    dot_general x3, matrix products, body(): jnp.einsum('ipe,ie->ip', incidence, residual_picked, precision=exact_mode)  17 us
    all_to_all x4, waiting for transfers between devices, twin_of(): lax.all_to_all(outgoing, 'cluster', split_axis=0, concat_axis=0, tiled=True)  13.3 us
    all_to_all x4, starting transfers between devices, twin_of(): lax.all_to_all(outgoing, 'cluster', split_axis=0, concat_axis=0, tiled=True)  12.9 us
  transfers between devices with their start and end apart: 8, of which 8 were waited for; matrix products, arithmetic and copies ran while one was open for 0% of the time, Pallas kernels for 0%

commit v1 on v0

v1 whole, which is shorter than its diff:
```python
import jax
import jax.numpy as jnp
from jax import lax
from jax.experimental import pallas as pl
from jax.experimental.pallas import tpu as pltpu
from jax.sharding import PartitionSpec as P

ITERS = 3
SUB = 8
VMEM = pl.BlockSpec(memory_space=pltpu.VMEM)
SMEM = pl.BlockSpec(memory_space=pltpu.SMEM)


def split3(x):
    high = x.astype(jnp.bfloat16)
    rest = x - high.astype(jnp.float32)
    middle = rest.astype(jnp.bfloat16)
    low = (rest - middle.astype(jnp.float32)).astype(jnp.bfloat16)
    return high, middle, low


def pick_rows(onehot, rows):
    total = None
    for part in split3(rows):
        term = jnp.dot(onehot, part, preferred_element_type=jnp.float32)
        total = term if total is None else total + term
    return total


def prep_kernel(
    start_ref, demand_ref, utility_ref, cap_ref, dual_ref, ids_ref, count_ref, size_ref,
    first_ref, second_ref, border_ref,
):
    blocks, width = start_ref.shape
    edges = cap_ref.shape[1]
    slots = border_ref.shape[0] // 2
    interior = cap_ref.shape[0] - slots
    lanes = lax.broadcasted_iota(jnp.int32, (1, width), 1)
    limits = []
    for j in range(blocks):
        count = jnp.where(j < size_ref[0], count_ref[j], 0)
        limits.append(jnp.where(lanes < count, demand_ref[j : j + 1, :], 0.0))
    limit = jnp.concatenate(limits, axis=0)
    first_ref[:blocks] = jnp.minimum(jnp.maximum(start_ref[...], 0.0), limit)
    ids = ids_ref[...].astype(jnp.float32)
    first_ref[blocks:] = jnp.zeros((SUB, width), jnp.float32)
    first_ref[blocks : blocks + 1, : ids.shape[1]] = ids
    second_ref[:blocks] = limit
    second_ref[blocks:] = utility_ref[...]
    border_ref[:slots] = cap_ref[interior:]
    border_ref[slots:] = dual_ref[interior:]


def load_of(flows, mask, inc_ref):
    count, _, edges = inc_ref.shape
    parts = [p.astype(jnp.float32) for p in split3(flows)]
    total = jnp.zeros((3 * SUB, edges), jnp.float32)
    for i in range(count):
        column = mask[:, i : i + 1]
        rows = jnp.concatenate([p[i : i + 1] * column for p in parts], axis=0)
        total += jnp.dot(rows.astype(jnp.bfloat16), inc_ref[i], preferred_element_type=jnp.float32)
    return total[:SUB] + total[SUB : 2 * SUB] + total[2 * SUB :]


def put_load(load, load_ref, border_ref):
    slots = border_ref.shape[0]
    interior = load_ref.shape[0] - slots
    load_ref[...] = load[: load_ref.shape[0]]
    border_ref[...] = load[interior : interior + slots]


def start_kernel(pieces, *refs):
    ins, (onehot_ref, mask_ref, inc_ref, flows_ref, load_ref, border_ref) = refs[:pieces], refs[pieces:]
    blocks = flows_ref.shape[0] - inc_ref.shape[0]
    group = blocks + SUB
    rows = jnp.concatenate(
        [ref[k : k + blocks] for ref in ins for k in range(0, ref.shape[0], group)], axis=0
    )
    flows = pick_rows(onehot_ref[...], rows)
    flows_ref[...] = flows
    put_load(load_of(flows[: inc_ref.shape[0]], mask_ref[...], inc_ref), load_ref, border_ref)


def pick_kernel(pieces, blocks, *refs):
    ins, (onehot_ref, limit_ref, utility_ref) = refs[:pieces], refs[pieces:]
    for offset, out in ((0, limit_ref), (blocks, utility_ref)):
        rows = jnp.concatenate(
            [
                ref[k : k + blocks]
                for ref in ins
                for k in range(offset, ref.shape[0], 2 * blocks)
            ],
            axis=0,
        )
        out[...] = pick_rows(onehot_ref[...], rows)


def flow_kernel(pieces, step_size, *refs):
    ins = refs[:pieces]
    (same_ref, flows_ref, limit_ref, utility_ref, mask_ref, inc_ref,
     out_ref, load_ref, border_ref) = refs[pieces:]
    terms = jnp.concatenate([ref[...] for ref in ins], axis=0)
    gradient = pick_rows(same_ref[...], terms)
    flows = flows_ref[...] - step_size * (gradient - utility_ref[...])
    flows = jnp.minimum(jnp.maximum(flows, 0.0), limit_ref[...])
    out_ref[...] = flows
    put_load(load_of(flows[: inc_ref.shape[0]], mask_ref[...], inc_ref), load_ref, border_ref)


def twin_of(ins, choice_ref):
    total = None
    for k, ref in enumerate(ins):
        term = jnp.where(choice_ref[k] > 0.5, ref[...], 0.0)
        total = term if total is None else total + term
    return total


def settle(ins, choice_ref, load_ref, limit, duals):
    load = load_ref[...]
    slots = ins[0].shape[0]
    interior = load.shape[0] - slots
    load = jnp.concatenate([load[:interior], load[interior:] + twin_of(ins, choice_ref)], axis=0)
    split = jnp.minimum(limit, load + duals)
    duals = (duals + load) - split
    return (load - split) + duals, duals


def back_terms(residual, mask, inc_ref, out_ref):
    rows = residual.shape[0]
    if rows < SUB:
        residual = jnp.concatenate(
            [residual, jnp.zeros((SUB - rows, residual.shape[1]), jnp.float32)], axis=0
        )
    parts = [p.astype(jnp.float32) for p in split3(residual)]
    left = jnp.concatenate(parts, axis=0).astype(jnp.bfloat16)
    for i in range(inc_ref.shape[0]):
        got = lax.dot_general(
            left, inc_ref[i], (((1,), (1,)), ((), ())), preferred_element_type=jnp.float32
        )
        got = got[:SUB] + got[SUB : 2 * SUB] + got[2 * SUB :]
        out_ref[i : i + 1, :] = jnp.sum(got * mask[:, i : i + 1], axis=0, keepdims=True)


def first_dual_kernel(others, unit, *refs):
    ins, starts = refs[:others], refs[others : 2 * others]
    (choice_ref, load_ref, cap_ref, dual_ref, mask_ref, inc_ref,
     limit_ref, out_ref, terms_ref) = refs[2 * others :]
    slots = ins[0].shape[0]
    interior = load_ref.shape[0] - slots
    cap_in = [r.at[:slots] for r in starts]
    dual_in = [r.at[slots:] for r in starts]

    def shared(ref, twins):
        mean = 0.5 * (ref[interior:] + twin_of(twins, choice_ref))
        return jnp.concatenate([ref[:interior], mean], axis=0)

    limit = unit * shared(cap_ref, cap_in)
    limit_ref[...] = limit
    residual, duals = settle(ins, choice_ref, load_ref, limit, shared(dual_ref, dual_in))
    out_ref[...] = duals
    back_terms(residual, mask_ref[...], inc_ref, terms_ref)


def dual_kernel(others, *refs):
    ins = refs[:others]
    (choice_ref, load_ref, limit_ref, dual_ref, mask_ref, inc_ref,
     out_ref, terms_ref) = refs[others:]
    residual, duals = settle(ins, choice_ref, load_ref, limit_ref[...], dual_ref[...])
    out_ref[...] = duals
    back_terms(residual, mask_ref[...], inc_ref, terms_ref)


def last_dual_kernel(others, *refs):
    ins = refs[:others]
    choice_ref, load_ref, limit_ref, dual_ref, out_ref = refs[others:]
    out_ref[...] = settle(ins, choice_ref, load_ref, limit_ref[...], dual_ref[...])[1]


def kernel_call(kernel, name, outs, operands, scalars=0, flops=0):
    shapes = tuple(jax.ShapeDtypeStruct(shape, jnp.float32) for shape in outs)
    size = sum(x.size * x.dtype.itemsize for x in operands)
    return pl.pallas_call(
        kernel,
        out_shape=shapes,
        in_specs=[VMEM] * (len(operands) - scalars) + [SMEM] * scalars,
        out_specs=tuple(VMEM for _ in outs),
        compiler_params=pltpu.CompilerParams(vmem_limit_bytes=16 * 1024 * 1024),
        cost_estimate=pl.CostEstimate(flops=flops, bytes_accessed=size, transcendentals=0),
        name=name,
    )(*operands)


def body(
    flow_start,
    demand,
    utility,
    path_count,
    cluster_size,
    incidence,
    inc_path,
    inc_edge,
    capacity,
    dual_start,
    partner,
):
    blocks, width = flow_start.shape
    incs = incidence.shape[0]
    edges = incidence.shape[2]
    locals_ = capacity.shape[0]
    slots = partner.shape[1]
    clusters, devices = lax.axis_size("cluster"), lax.axis_size("shard")
    cluster, shard = lax.axis_index("cluster"), lax.axis_index("shard")
    rows = incs + blocks
    norm_bound = max(2, incs * incs * width * edges // (1024 * locals_ * blocks))
    unit = float(max(1, incs * width // (160 * locals_)))
    step_size = 1.0 / (2.0 * norm_bound)
    bits = devices.bit_length() - 1
    assert devices == 1 << bits and clusters & (clusters - 1) == 0
    stages = [1] * (bits % 2) + [2] * (bits // 2)

    def share(x):
        pieces, shift = [x], 0
        for step in stages:
            now = pieces[0] if len(pieces) == 1 else jnp.concatenate(pieces, axis=0)
            pieces = [now]
            for k in range(1, 1 << step):
                pairs = [(i, i ^ (k << shift)) for i in range(devices)]
                pieces.append(lax.ppermute(now, "shard", pairs))
            shift += step
        return pieces

    def trade(x):
        return [
            lax.ppermute(x, "cluster", [(i, i ^ k) for i in range(clusters)])
            for k in range(1, clusters)
        ]

    inc = incidence.astype(jnp.bfloat16)
    first, second, border = kernel_call(
        prep_kernel,
        "prepare",
        [(blocks + SUB, width), (2 * blocks, width), (2 * slots, edges)],
        [flow_start, demand, utility, capacity, dual_start, inc_path[None, :], path_count, cluster_size],
        scalars=2,
    )
    own_rows = jnp.arange(blocks, dtype=jnp.int32)
    place = jnp.concatenate([((inc_path // blocks) ^ shard) * blocks + inc_path % blocks, own_rows])
    onehot = (place[:, None] == jnp.arange(blocks * devices, dtype=jnp.int32)).astype(jnp.bfloat16)
    mask = (jnp.arange(SUB, dtype=jnp.int32)[:, None] == inc_edge[None, :]).astype(jnp.float32)
    choice = (partner[0][None, :] == (cluster ^ jnp.arange(1, clusters, dtype=jnp.int32))[:, None])
    choice = jnp.broadcast_to(choice.astype(jnp.float32)[:, :, None], (clusters - 1, slots, edges))

    firsts = share(first)
    starts = trade(border)
    seconds = share(second)
    ids = jnp.concatenate([p.reshape(-1, blocks + SUB, width)[:, blocks, :incs] for p in firsts], axis=0)
    names = jnp.concatenate([inc_path, shard * blocks + own_rows]).astype(jnp.float32)
    same = (names[:, None] == ids.reshape(1, -1)).astype(jnp.bfloat16)

    pieces, others = len(firsts), clusters - 1
    flops = 2 * incs * width * edges * SUB
    load_shapes = [(rows, width), (locals_, edges), (slots, edges)]
    flows, load, out = kernel_call(
        lambda *refs: start_kernel(pieces, *refs), "first_load", load_shapes,
        [*firsts, onehot, mask, inc], flops=flops,
    )
    limits, utilities = kernel_call(
        lambda *refs: pick_kernel(pieces, blocks, *refs), "pick", [(rows, width)] * 2,
        [*seconds, onehot],
    )
    dual_shape, term_shape = (locals_, edges), (incs, width)
    limit, duals, terms = kernel_call(
        lambda *refs: first_dual_kernel(others, unit, *refs), "first_duals",
        [dual_shape, dual_shape, term_shape],
        [*trade(out), *starts, choice, load, capacity, dual_start, mask, inc], flops=flops,
    )
    for iteration in range(ITERS):
        flows, load, out = kernel_call(
            lambda *refs: flow_kernel(pieces, step_size, *refs), "flows", load_shapes,
            [*share(terms), same, flows, limits, utilities, mask, inc], flops=flops,
        )
        operands = [*trade(out), choice, load, limit, duals]
        if iteration < ITERS - 1:
            duals, terms = kernel_call(
                lambda *refs: dual_kernel(others, *refs), "duals", [dual_shape, term_shape],
                [*operands, mask, inc], flops=flops,
            )
    (duals,) = kernel_call(
        lambda *refs: last_dual_kernel(others, *refs), "last_duals", [dual_shape], operands
    )
    return flows[incs:], duals


def solution(mesh):
    whole = P(("cluster", "shard"))
    wide = P(("cluster", "shard"), None)
    return jax.shard_map(
        body,
        mesh=mesh,
        in_specs=(
            wide, wide, wide, whole, P("cluster"), P(("cluster", "shard"), None, None),
            whole, whole, wide, wide, P("cluster", None),
        ),
        out_specs=(wide, wide),
        check_vma=False,
    )
```

time: 405 us -> 86.7 us (0.21)
  waiting for transfers between devices: 196 us -> 27.2 us
  blocking collectives: 124 us -> 0 us
  matrix products: 42 us -> 0 us
  starting transfers between devices: 16.4 us -> 39.6 us
  between operations: 14.7 us -> 1.48 us
  Pallas kernels: 0 us -> 6.52 us
    reduce_scatter x3 -> x0, waiting for transfers between devices: 179 us -> none  [body(): lax.psum_scatter(jnp.dot(rows_pick, terms, precision=exact_mode), 'shard'...]
    all_gather x4 -> x0, blocking collectives: 124 us -> none  [shared_flows(): return lax.all_gather(flows_now, 'shard', axis=0, tiled=True)]
    dot_general x24 -> x0, matrix products: 42 us -> none  [the longest x4 17.3 us: load_of_rows(): terms = jnp.einsum('ipe,ip->ie', incidence, picked, precision=exact_mode)]
    ppermute x0 -> x35, starting transfers between devices: none -> 39.6 us  [the longest x20 28.8 us: share(): pieces.append(lax.ppermute(now, 'shard', pairs))]
    ppermute x0 -> x35, waiting for transfers between devices: none -> 27.2 us  [the longest x20 21.8 us: share(): pieces.append(lax.ppermute(now, 'shard', pairs))]
    all_to_all x5 -> x0, waiting for transfers between devices: 16.8 us -> none  [the longest x4 13.3 us: twin_of(): lax.all_to_all(outgoing, 'cluster', split_axis=0, concat_axis=0, tiled=True)]
    all_to_all x5 -> x0, starting transfers between devices: 16.1 us -> none  [the longest x4 12.9 us: twin_of(): lax.all_to_all(outgoing, 'cluster', split_axis=0, concat_axis=0, tiled=True)]
    pallas_call x0 -> x10, Pallas kernels: none -> 6.52 us  [kernel_call(): pl.pallas_call(kernel, out_shape=shapes, in_specs=[VMEM] * (len(operands)...]
  transfers between devices with their start and end apart: 8 -> 35, of which waited for: 8 -> 17; matrix products, arithmetic and copies ran while one was open for 0% -> 7% of each run, Pallas kernels for 0% -> 2%
where the time goes in v1:
time: 86.7 us; the launch traced here: 86 us
  starting transfers between devices  39.6 us (46%)
  waiting for transfers between devices  27.2 us (31%)
  Pallas kernels  6.52 us (8%)
  local copies, waits for them, and re-layouts  5.63 us (6%)
  other arithmetic  5.56 us (6%)
  between operations  1.48 us (2%)
    ppermute x20, starting transfers between devices, share(): pieces.append(lax.ppermute(now, 'shard', pairs))  28.8 us
    ppermute x20, waiting for transfers between devices, share(): pieces.append(lax.ppermute(now, 'shard', pairs))  21.8 us
    ppermute x15, starting transfers between devices, trade(): lax.ppermute(x, 'cluster', [(i, i ^ k) for i in range(clusters)])  10.8 us
    pallas_call x10, Pallas kernels, kernel_call(): pl.pallas_call(kernel, out_shape=shapes, in_specs=[VMEM] * (len(operands)...  6.52 us
    ppermute x15, waiting for transfers between devices, trade(): lax.ppermute(x, 'cluster', [(i, i ^ k) for i in range(clusters)])  5.44 us
    unnamed x23, local copies, waits for them, and re-layouts  4.85 us
    convert_element_type x1, other arithmetic, body(): inc = incidence.astype(jnp.bfloat16)  2.53 us
  transfers between devices with their start and end apart: 35, of which 17 were waited for; matrix products, arithmetic and copies ran while one was open for 7% of the time, Pallas kernels for 2%

profile of v1, /device:TPU:0, one launch (start us, length us, event | category | flops | bytes accessed | tf_op | source)
XLA Modules:
  0.0 86.0 jit_solution(12164810489222910543)
XLA Ops:
  6.7 2.4 %collective-permute-start.9 = (f32[6,128]{1,0:T(8,128)S(1)}, f32[6,128]{1,0:T(8,128)S(1)}, u32[]{:S(2)}, u32[]{:S(2)}) collective-permute-start(f32[6,128]{1,0:T(8,128)S(1)} %get-tuple-element.28), channel_id=1, source_target_pairs={{0,24},{8,16},{16,8},{24,0},{1,25},{9,17},{17,9},{25,1},{2,26},{10... | collective-permute-start | bytes 9224 | tf_op jit(solution)/shard_map/ppermute | solution.py:234
  9.8 1.5 %collective-permute-start = (f32[24,256]{1,0:T(8,128)S(1)}, f32[24,256]{1,0:T(8,128)S(1)}, u32[]{:S(2)}, u32[]{:S(2)}) collective-permute-start(f32[24,256]{1,0:T(8,128)S(1)} %get-tuple-element.26), channel_id=1, source_target_pairs={{0,1},{1,0},{2,3},{3,2},{4,5},{5,4},{6,7},{7,6},{8,9},{9,8},{10,11... | collective-permute-start | bytes 73736 | tf_op jit(solution)/shard_map/ppermute | solution.py:228
  14.8 2.5 %convert_element_type.28.refs_6_.refs_11_.refs_9_.refs_8_ = bf16[32,256,128]{2,1,0:T(8,128)(2,1)S(1)} convert(f32[32,256,128]{2,1,0:T(8,128)} %param.16) | non-fusion elementwise | flops 1048576 | bytes 6291456 | tf_op jit(solution)/shard_map/convert_element_type | solution.py:238
  17.3 3.7 %collective-permute-start.3 = (f32[48,256]{1,0:T(8,128)S(1)}, f32[48,256]{1,0:T(8,128)S(1)}, u32[]{:S(2)}, u32[]{:S(2)}) collective-permute-start(f32[48,256]{1,0:T(8,128)S(1)} %constant_dynamic-update-slice_fusion.refs_0_), channel_id=1, source_target_pairs={{0,6},{1,7},{2,4},{3,5},{4,2},{5,3},{6,0},{7,1},{8,14},{9,15},{10,... | collective-permute-start | bytes 147464 | tf_op jit(solution)/shard_map/ppermute | solution.py:228
  21.8 1.8 %collective-permute-done.3.refs_3_ = f32[48,256]{1,0:T(8,128)S(1)} collective-permute-done((f32[48,256]{1,0:T(8,128)S(1)}, f32[48,256]{1,0:T(8,128)S(1)}, u32[]{:S(2)}, u32[]{:S(2)}) %collective-permute-start.3) | collective-permute-done | bytes 49184 | tf_op jit(solution)/shard_map/ppermute | solution.py:228
  23.7 2.3 %collective-permute-done.2.refs_2_ = f32[48,256]{1,0:T(8,128)S(1)} collective-permute-done((f32[48,256]{1,0:T(8,128)S(1)}, f32[48,256]{1,0:T(8,128)S(1)}, u32[]{:S(2)}, u32[]{:S(2)}) %collective-permute-start.2) | collective-permute-done | bytes 49184 | tf_op jit(solution)/shard_map/ppermute | solution.py:228
  28.7 2.0 %collective-permute-start.17 = (f32[64,256]{1,0:T(8,128)S(1)}, f32[64,256]{1,0:T(8,128)S(1)}, u32[]{:S(2)}, u32[]{:S(2)}) collective-permute-start(f32[64,256]{1,0:T(8,128)S(1)} %constant_dynamic-update-slice_fusion.4.refs_0_), channel_id=1, source_target_pairs={{0,6},{1,7},{2,4},{3,5},{4,2},{5,3},{6,0},{7,1},{8,14},{9,15},{10,... | collective-permute-start | bytes 196616 | tf_op jit(solution)/shard_map/ppermute | solution.py:228
  30.8 2.3 %collective-permute-start.15 = (f32[64,256]{1,0:T(8,128)S(1)}, f32[64,256]{1,0:T(8,128)S(1)}, u32[]{:S(2)}, u32[]{:S(2)}) collective-permute-start(f32[64,256]{1,0:T(8,128)S(1)} %constant_dynamic-update-slice_fusion.4.refs_0_), channel_id=1, source_target_pairs={{0,2},{1,3},{2,0},{3,1},{4,6},{5,7},{6,4},{7,5},{8,10},{9,11},{10,... | collective-permute-start | bytes 196616 | tf_op jit(solution)/shard_map/ppermute | solution.py:228
  34.0 1.6 %collective-permute-start.10 = (f32[32,256]{1,0:T(8,128)S(1)}, f32[32,256]{1,0:T(8,128)S(1)}, u32[]{:S(2)}, u32[]{:S(2)}) collective-permute-start(f32[32,256]{1,0:T(8,128)S(1)} %get-tuple-element.30), channel_id=1, source_target_pairs={{0,1},{1,0},{2,3},{3,2},{4,5},{5,4},{6,7},{7,6},{8,9},{9,8},{10,11... | collective-permute-start | bytes 98312 | tf_op jit(solution)/shard_map/ppermute | solution.py:228
  35.6 2.4 %collective-permute-done.10 = f32[32,256]{1,0:T(8,128)S(1)} collective-permute-done((f32[32,256]{1,0:T(8,128)S(1)}, f32[32,256]{1,0:T(8,128)S(1)}, u32[]{:S(2)}, u32[]{:S(2)}) %collective-permute-start.10) | collective-permute-done | bytes 32800 | tf_op jit(solution)/shard_map/ppermute | solution.py:228
  38.0 2.0 %collective-permute-start.13 = (f32[64,256]{1,0:T(8,128)S(1)}, f32[64,256]{1,0:T(8,128)S(1)}, u32[]{:S(2)}, u32[]{:S(2)}) collective-permute-start(f32[64,256]{1,0:T(8,128)S(1)} %constant_dynamic-update-slice_fusion.2.refs_0_), channel_id=1, source_target_pairs={{0,6},{1,7},{2,4},{3,5},{4,2},{5,3},{6,0},{7,1},{8,14},{9,15},{10,... | collective-permute-start | bytes 196616 | tf_op jit(solution)/shard_map/ppermute | solution.py:228
  40.0 2.4 %collective-permute-start.11 = (f32[64,256]{1,0:T(8,128)S(1)}, f32[64,256]{1,0:T(8,128)S(1)}, u32[]{:S(2)}, u32[]{:S(2)}) collective-permute-start(f32[64,256]{1,0:T(8,128)S(1)} %constant_dynamic-update-slice_fusion.2.refs_0_), channel_id=1, source_target_pairs={{0,2},{1,3},{2,0},{3,1},{4,6},{5,7},{6,4},{7,5},{8,10},{9,11},{10,... | collective-permute-start | bytes 196616 | tf_op jit(solution)/shard_map/ppermute | solution.py:228
  42.7 1.7 %collective-permute-done.13.refs_3_ = f32[64,256]{1,0:T(8,128)S(1)} collective-permute-done((f32[64,256]{1,0:T(8,128)S(1)}, f32[64,256]{1,0:T(8,128)S(1)}, u32[]{:S(2)}, u32[]{:S(2)}) %collective-permute-start.13) | collective-permute-done | bytes 65568 | tf_op jit(solution)/shard_map/ppermute | solution.py:228
  51.0 1.6 %collective-permute-start.21 = (f32[32,256]{1,0:T(8,128)S(1)}, f32[32,256]{1,0:T(8,128)S(1)}, u32[]{:S(2)}, u32[]{:S(2)}) collective-permute-start(f32[32,256]{1,0:T(8,128)S(1)} %get-tuple-element.39), channel_id=1, source_target_pairs={{0,1},{1,0},{2,3},{3,2},{4,5},{5,4},{6,7},{7,6},{8,9},{9,8},{10,11... | collective-permute-start | bytes 98312 | tf_op jit(solution)/shard_map/ppermute | solution.py:228
  52.6 2.4 %collective-permute-done.21 = f32[32,256]{1,0:T(8,128)S(1)} collective-permute-done((f32[32,256]{1,0:T(8,128)S(1)}, f32[32,256]{1,0:T(8,128)S(1)}, u32[]{:S(2)}, u32[]{:S(2)}) %collective-permute-start.21) | collective-permute-done | bytes 32800 | tf_op jit(solution)/shard_map/ppermute | solution.py:228
  55.0 2.1 %collective-permute-start.24 = (f32[64,256]{1,0:T(8,128)S(1)}, f32[64,256]{1,0:T(8,128)S(1)}, u32[]{:S(2)}, u32[]{:S(2)}) collective-permute-start(f32[64,256]{1,0:T(8,128)S(1)} %constant_dynamic-update-slice_fusion.6.refs_0_), channel_id=1, source_target_pairs={{0,6},{1,7},{2,4},{3,5},{4,2},{5,3},{6,0},{7,1},{8,14},{9,15},{10,... | collective-permute-start | bytes 196616 | tf_op jit(solution)/shard_map/ppermute | solution.py:228
  57.4 2.0 %collective-permute-start.22 = (f32[64,256]{1,0:T(8,128)S(1)}, f32[64,256]{1,0:T(8,128)S(1)}, u32[]{:S(2)}, u32[]{:S(2)}) collective-permute-start(f32[64,256]{1,0:T(8,128)S(1)} %constant_dynamic-update-slice_fusion.6.refs_0_), channel_id=1, source_target_pairs={{0,2},{1,3},{2,0},{3,1},{4,6},{5,7},{6,4},{7,5},{8,10},{9,11},{10,... | collective-permute-start | bytes 196616 | tf_op jit(solution)/shard_map/ppermute | solution.py:228
  59.4 2.1 %collective-permute-done.24.refs_3_ = f32[64,256]{1,0:T(8,128)S(1)} collective-permute-done((f32[64,256]{1,0:T(8,128)S(1)}, f32[64,256]{1,0:T(8,128)S(1)}, u32[]{:S(2)}, u32[]{:S(2)}) %collective-permute-start.24) | collective-permute-done | bytes 65568 | tf_op jit(solution)/shard_map/ppermute | solution.py:228
  61.5 2.0 %collective-permute-done.23.refs_2_ = f32[64,256]{1,0:T(8,128)S(1)} collective-permute-done((f32[64,256]{1,0:T(8,128)S(1)}, f32[64,256]{1,0:T(8,128)S(1)}, u32[]{:S(2)}, u32[]{:S(2)}) %collective-permute-start.23) | collective-permute-done | bytes 65568 | tf_op jit(solution)/shard_map/ppermute | solution.py:228
  68.7 1.6 %collective-permute-start.28 = (f32[32,256]{1,0:T(8,128)S(1)}, f32[32,256]{1,0:T(8,128)S(1)}, u32[]{:S(2)}, u32[]{:S(2)}) collective-permute-start(f32[32,256]{1,0:T(8,128)S(1)} %get-tuple-element.44), channel_id=1, source_target_pairs={{0,1},{1,0},{2,3},{3,2},{4,5},{5,4},{6,7},{7,6},{8,9},{9,8},{10,11... | collective-permute-start | bytes 98312 | tf_op jit(solution)/shard_map/ppermute | solution.py:228
  70.3 2.4 %collective-permute-done.28 = f32[32,256]{1,0:T(8,128)S(1)} collective-permute-done((f32[32,256]{1,0:T(8,128)S(1)}, f32[32,256]{1,0:T(8,128)S(1)}, u32[]{:S(2)}, u32[]{:S(2)}) %collective-permute-start.28) | collective-permute-done | bytes 32800 | tf_op jit(solution)/shard_map/ppermute | solution.py:228
  72.7 2.1 %collective-permute-start.31 = (f32[64,256]{1,0:T(8,128)S(1)}, f32[64,256]{1,0:T(8,128)S(1)}, u32[]{:S(2)}, u32[]{:S(2)}) collective-permute-start(f32[64,256]{1,0:T(8,128)S(1)} %constant_dynamic-update-slice_fusion.8.refs_0_), channel_id=1, source_target_pairs={{0,6},{1,7},{2,4},{3,5},{4,2},{5,3},{6,0},{7,1},{8,14},{9,15},{10,... | collective-permute-start | bytes 196616 | tf_op jit(solution)/shard_map/ppermute | solution.py:228
  74.8 2.3 %collective-permute-start.29 = (f32[64,256]{1,0:T(8,128)S(1)}, f32[64,256]{1,0:T(8,128)S(1)}, u32[]{:S(2)}, u32[]{:S(2)}) collective-permute-start(f32[64,256]{1,0:T(8,128)S(1)} %constant_dynamic-update-slice_fusion.8.refs_0_), channel_id=1, source_target_pairs={{0,2},{1,3},{2,0},{3,1},{4,6},{5,7},{6,4},{7,5},{8,10},{9,11},{10,... | collective-permute-start | bytes 196616 | tf_op jit(solution)/shard_map/ppermute | solution.py:228
  77.1 1.9 %collective-permute-done.31.refs_3_ = f32[64,256]{1,0:T(8,128)S(1)} collective-permute-done((f32[64,256]{1,0:T(8,128)S(1)}, f32[64,256]{1,0:T(8,128)S(1)}, u32[]{:S(2)}, u32[]{:S(2)}) %collective-permute-start.31) | collective-permute-done | bytes 65568 | tf_op jit(solution)/shard_map/ppermute | solution.py:228
  (103 shorter events, 33.4 us)
Async XLA Ops:
  6.7 21.4 %collective-permute-start.9 = (f32[6,128]{1,0:T(8,128)S(1)}, f32[6,128]{1,0:T(8,128)S(1)}, u32[]{:S(2)}, u32[]{:S(2)}) collective-permute-start(f32[6,128]{1,0:T(8,128)S(1)} %get-tuple-element.28), channel_id=1, source_target_pairs={{0,24},{8,16},{16,8},{24,0},{1,25},{9,17},{17,9},{25,1},{2,26},{10... | collective-permute-start | bytes 9224 | tf_op jit(solution)/shard_map/ppermute | solution.py:234
  9.1 19.6 %collective-permute-start.8 = (f32[6,128]{1,0:T(8,128)S(1)}, f32[6,128]{1,0:T(8,128)S(1)}, u32[]{:S(2)}, u32[]{:S(2)}) collective-permute-start(f32[6,128]{1,0:T(8,128)S(1)} %get-tuple-element.28), channel_id=1, source_target_pairs={{0,16},{8,24},{16,0},{24,8},{1,17},{9,25},{17,1},{25,9},{2,18},{10... | collective-permute-start | bytes 9224 | tf_op jit(solution)/shard_map/ppermute | solution.py:234
  9.8 7.5 %collective-permute-start = (f32[24,256]{1,0:T(8,128)S(1)}, f32[24,256]{1,0:T(8,128)S(1)}, u32[]{:S(2)}, u32[]{:S(2)}) collective-permute-start(f32[24,256]{1,0:T(8,128)S(1)} %get-tuple-element.26), channel_id=1, source_target_pairs={{0,1},{1,0},{2,3},{3,2},{4,5},{5,4},{6,7},{7,6},{8,9},{9,8},{10,11... | collective-permute-start | bytes 73736 | tf_op jit(solution)/shard_map/ppermute | solution.py:228
  11.3 9.7 %collective-permute-start.14 = (f32[32,256]{1,0:T(8,128)S(1)}, f32[32,256]{1,0:T(8,128)S(1)}, u32[]{:S(2)}, u32[]{:S(2)}) collective-permute-start(f32[32,256]{1,0:T(8,128)S(1)} %get-tuple-element.32), channel_id=1, source_target_pairs={{0,1},{1,0},{2,3},{3,2},{4,5},{5,4},{6,7},{7,6},{8,9},{9,8},{10,11... | collective-permute-start | bytes 98312 | tf_op jit(solution)/shard_map/ppermute | solution.py:228
  17.3 6.3 %collective-permute-start.3 = (f32[48,256]{1,0:T(8,128)S(1)}, f32[48,256]{1,0:T(8,128)S(1)}, u32[]{:S(2)}, u32[]{:S(2)}) collective-permute-start(f32[48,256]{1,0:T(8,128)S(1)} %constant_dynamic-update-slice_fusion.refs_0_), channel_id=1, source_target_pairs={{0,6},{1,7},{2,4},{3,5},{4,2},{5,3},{6,0},{7,1},{8,14},{9,15},{10,... | collective-permute-start | bytes 147464 | tf_op jit(solution)/shard_map/ppermute | solution.py:228
  21.0 5.0 %collective-permute-start.2 = (f32[48,256]{1,0:T(8,128)S(1)}, f32[48,256]{1,0:T(8,128)S(1)}, u32[]{:S(2)}, u32[]{:S(2)}) collective-permute-start(f32[48,256]{1,0:T(8,128)S(1)} %constant_dynamic-update-slice_fusion.refs_0_), channel_id=1, source_target_pairs={{0,4},{1,5},{2,6},{3,7},{4,0},{5,1},{6,2},{7,3},{8,12},{9,13},{10,... | collective-permute-start | bytes 147464 | tf_op jit(solution)/shard_map/ppermute | solution.py:228
  21.0 5.0 %collective-permute-start.1 = (f32[48,256]{1,0:T(8,128)S(1)}, f32[48,256]{1,0:T(8,128)S(1)}, u32[]{:S(2)}, u32[]{:S(2)}) collective-permute-start(f32[48,256]{1,0:T(8,128)S(1)} %constant_dynamic-update-slice_fusion.refs_0_), channel_id=1, source_target_pairs={{0,2},{1,3},{2,0},{3,1},{4,6},{5,7},{6,4},{7,5},{8,10},{9,11},{10,... | collective-permute-start | bytes 147464 | tf_op jit(solution)/shard_map/ppermute | solution.py:228
  23.6 7.1 %collective-permute-start.7 = (f32[6,128]{1,0:T(8,128)S(1)}, f32[6,128]{1,0:T(8,128)S(1)}, u32[]{:S(2)}, u32[]{:S(2)}) collective-permute-start(f32[6,128]{1,0:T(8,128)S(1)} %get-tuple-element.28), channel_id=1, source_target_pairs={{0,8},{8,0},{16,24},{24,16},{1,9},{9,1},{17,25},{25,17},{2,10},{10... | collective-permute-start | bytes 9224 | tf_op jit(solution)/shard_map/ppermute | solution.py:234
  26.6 4.2 %collective-permute-start.6 = (f32[3,128]{1,0:T(4,128)S(1)}, f32[3,128]{1,0:T(4,128)S(1)}, u32[]{:S(2)}, u32[]{:S(2)}) collective-permute-start(f32[3,128]{1,0:T(4,128)S(1)} %get-tuple-element.27), channel_id=1, source_target_pairs={{0,24},{8,16},{16,8},{24,0},{1,25},{9,17},{17,9},{25,1},{2,26},{10... | collective-permute-start | bytes 4616 | tf_op jit(solution)/shard_map/ppermute | solution.py:234
  26.7 6.4 %collective-permute-start.5 = (f32[3,128]{1,0:T(4,128)S(1)}, f32[3,128]{1,0:T(4,128)S(1)}, u32[]{:S(2)}, u32[]{:S(2)}) collective-permute-start(f32[3,128]{1,0:T(4,128)S(1)} %get-tuple-element.27), channel_id=1, source_target_pairs={{0,16},{8,24},{16,0},{24,8},{1,17},{9,25},{17,1},{25,9},{2,18},{10... | collective-permute-start | bytes 4616 | tf_op jit(solution)/shard_map/ppermute | solution.py:234
  28.1 5.0 %collective-permute-start.4 = (f32[3,128]{1,0:T(4,128)S(1)}, f32[3,128]{1,0:T(4,128)S(1)}, u32[]{:S(2)}, u32[]{:S(2)}) collective-permute-start(f32[3,128]{1,0:T(4,128)S(1)} %get-tuple-element.27), channel_id=1, source_target_pairs={{0,8},{8,0},{16,24},{24,16},{1,9},{9,1},{17,25},{25,17},{2,10},{10... | collective-permute-start | bytes 4616 | tf_op jit(solution)/shard_map/ppermute | solution.py:234
  28.7 11.3 %collective-permute-start.17 = (f32[64,256]{1,0:T(8,128)S(1)}, f32[64,256]{1,0:T(8,128)S(1)}, u32[]{:S(2)}, u32[]{:S(2)}) collective-permute-start(f32[64,256]{1,0:T(8,128)S(1)} %constant_dynamic-update-slice_fusion.4.refs_0_), channel_id=1, source_target_pairs={{0,6},{1,7},{2,4},{3,5},{4,2},{5,3},{6,0},{7,1},{8,14},{9,15},{10,... | collective-permute-start | bytes 196616 | tf_op jit(solution)/shard_map/ppermute | solution.py:228
  30.7 11.8 %collective-permute-start.16 = (f32[64,256]{1,0:T(8,128)S(1)}, f32[64,256]{1,0:T(8,128)S(1)}, u32[]{:S(2)}, u32[]{:S(2)}) collective-permute-start(f32[64,256]{1,0:T(8,128)S(1)} %constant_dynamic-update-slice_fusion.4.refs_0_), channel_id=1, source_target_pairs={{0,4},{1,5},{2,6},{3,7},{4,0},{5,1},{6,2},{7,3},{8,12},{9,13},{10,... | collective-permute-start | bytes 196616 | tf_op jit(solution)/shard_map/ppermute | solution.py:228
  30.8 11.7 %collective-permute-start.15 = (f32[64,256]{1,0:T(8,128)S(1)}, f32[64,256]{1,0:T(8,128)S(1)}, u32[]{:S(2)}, u32[]{:S(2)}) collective-permute-start(f32[64,256]{1,0:T(8,128)S(1)} %constant_dynamic-update-slice_fusion.4.refs_0_), channel_id=1, source_target_pairs={{0,2},{1,3},{2,0},{3,1},{4,6},{5,7},{6,4},{7,5},{8,10},{9,11},{10,... | collective-permute-start | bytes 196616 | tf_op jit(solution)/shard_map/ppermute | solution.py:228
  34.0 4.0 %collective-permute-start.10 = (f32[32,256]{1,0:T(8,128)S(1)}, f32[32,256]{1,0:T(8,128)S(1)}, u32[]{:S(2)}, u32[]{:S(2)}) collective-permute-start(f32[32,256]{1,0:T(8,128)S(1)} %get-tuple-element.30), channel_id=1, source_target_pairs={{0,1},{1,0},{2,3},{3,2},{4,5},{5,4},{6,7},{7,6},{8,9},{9,8},{10,11... | collective-permute-start | bytes 98312 | tf_op jit(solution)/shard_map/ppermute | solution.py:228
  38.0 6.4 %collective-permute-start.13 = (f32[64,256]{1,0:T(8,128)S(1)}, f32[64,256]{1,0:T(8,128)S(1)}, u32[]{:S(2)}, u32[]{:S(2)}) collective-permute-start(f32[64,256]{1,0:T(8,128)S(1)} %constant_dynamic-update-slice_fusion.2.refs_0_), channel_id=1, source_target_pairs={{0,6},{1,7},{2,4},{3,5},{4,2},{5,3},{6,0},{7,1},{8,14},{9,15},{10,... | collective-permute-start | bytes 196616 | tf_op jit(solution)/shard_map/ppermute | solution.py:228
  40.0 5.8 %collective-permute-start.12 = (f32[64,256]{1,0:T(8,128)S(1)}, f32[64,256]{1,0:T(8,128)S(1)}, u32[]{:S(2)}, u32[]{:S(2)}) collective-permute-start(f32[64,256]{1,0:T(8,128)S(1)} %constant_dynamic-update-slice_fusion.2.refs_0_), channel_id=1, source_target_pairs={{0,4},{1,5},{2,6},{3,7},{4,0},{5,1},{6,2},{7,3},{8,12},{9,13},{10,... | collective-permute-start | bytes 196616 | tf_op jit(solution)/shard_map/ppermute | solution.py:228
  40.0 5.8 %collective-permute-start.11 = (f32[64,256]{1,0:T(8,128)S(1)}, f32[64,256]{1,0:T(8,128)S(1)}, u32[]{:S(2)}, u32[]{:S(2)}) collective-permute-start(f32[64,256]{1,0:T(8,128)S(1)} %constant_dynamic-update-slice_fusion.2.refs_0_), channel_id=1, source_target_pairs={{0,2},{1,3},{2,0},{3,1},{4,6},{5,7},{6,4},{7,5},{8,10},{9,11},{10,... | collective-permute-start | bytes 196616 | tf_op jit(solution)/shard_map/ppermute | solution.py:228
  55.0 6.5 %collective-permute-start.24 = (f32[64,256]{1,0:T(8,128)S(1)}, f32[64,256]{1,0:T(8,128)S(1)}, u32[]{:S(2)}, u32[]{:S(2)}) collective-permute-start(f32[64,256]{1,0:T(8,128)S(1)} %constant_dynamic-update-slice_fusion.6.refs_0_), channel_id=1, source_target_pairs={{0,6},{1,7},{2,4},{3,5},{4,2},{5,3},{6,0},{7,1},{8,14},{9,15},{10,... | collective-permute-start | bytes 196616 | tf_op jit(solution)/shard_map/ppermute | solution.py:228
  57.2 6.3 %collective-permute-start.23 = (f32[64,256]{1,0:T(8,128)S(1)}, f32[64,256]{1,0:T(8,128)S(1)}, u32[]{:S(2)}, u32[]{:S(2)}) collective-permute-start(f32[64,256]{1,0:T(8,128)S(1)} %constant_dynamic-update-slice_fusion.6.refs_0_), channel_id=1, source_target_pairs={{0,4},{1,5},{2,6},{3,7},{4,0},{5,1},{6,2},{7,3},{8,12},{9,13},{10,... | collective-permute-start | bytes 196616 | tf_op jit(solution)/shard_map/ppermute | solution.py:228
  57.4 6.1 %collective-permute-start.22 = (f32[64,256]{1,0:T(8,128)S(1)}, f32[64,256]{1,0:T(8,128)S(1)}, u32[]{:S(2)}, u32[]{:S(2)}) collective-permute-start(f32[64,256]{1,0:T(8,128)S(1)} %constant_dynamic-update-slice_fusion.6.refs_0_), channel_id=1, source_target_pairs={{0,2},{1,3},{2,0},{3,1},{4,6},{5,7},{6,4},{7,5},{8,10},{9,11},{10,... | collective-permute-start | bytes 196616 | tf_op jit(solution)/shard_map/ppermute | solution.py:228
  72.7 6.3 %collective-permute-start.31 = (f32[64,256]{1,0:T(8,128)S(1)}, f32[64,256]{1,0:T(8,128)S(1)}, u32[]{:S(2)}, u32[]{:S(2)}) collective-permute-start(f32[64,256]{1,0:T(8,128)S(1)} %constant_dynamic-update-slice_fusion.8.refs_0_), channel_id=1, source_target_pairs={{0,6},{1,7},{2,4},{3,5},{4,2},{5,3},{6,0},{7,1},{8,14},{9,15},{10,... | collective-permute-start | bytes 196616 | tf_op jit(solution)/shard_map/ppermute | solution.py:228
  74.8 5.6 %collective-permute-start.30 = (f32[64,256]{1,0:T(8,128)S(1)}, f32[64,256]{1,0:T(8,128)S(1)}, u32[]{:S(2)}, u32[]{:S(2)}) collective-permute-start(f32[64,256]{1,0:T(8,128)S(1)} %constant_dynamic-update-slice_fusion.8.refs_0_), channel_id=1, source_target_pairs={{0,4},{1,5},{2,6},{3,7},{4,0},{5,1},{6,2},{7,3},{8,12},{9,13},{10,... | collective-permute-start | bytes 196616 | tf_op jit(solution)/shard_map/ppermute | solution.py:228
  74.8 5.6 %collective-permute-start.29 = (f32[64,256]{1,0:T(8,128)S(1)}, f32[64,256]{1,0:T(8,128)S(1)}, u32[]{:S(2)}, u32[]{:S(2)}) collective-permute-start(f32[64,256]{1,0:T(8,128)S(1)} %constant_dynamic-update-slice_fusion.8.refs_0_), channel_id=1, source_target_pairs={{0,2},{1,3},{2,0},{3,1},{4,6},{5,7},{6,4},{7,5},{8,10},{9,11},{10,... | collective-permute-start | bytes 196616 | tf_op jit(solution)/shard_map/ppermute | solution.py:228
  (20 other events, 77.0 us)

commit v2 on v1

v2 whole, which is shorter than its diff:
```python
import jax
import jax.numpy as jnp
from jax import lax
from jax.experimental import pallas as pl
from jax.experimental.pallas import tpu as pltpu
from jax.sharding import PartitionSpec as P

ITERS = 3
SUB = 8
VMEM = pl.BlockSpec(memory_space=pltpu.VMEM)


def split3(x):
    high = x.astype(jnp.bfloat16)
    rest = x - high.astype(jnp.float32)
    middle = rest.astype(jnp.bfloat16)
    low = (rest - middle.astype(jnp.float32)).astype(jnp.bfloat16)
    return high, middle, low


def pick_rows(onehot, rows):
    total = None
    for part in split3(rows):
        term = jnp.dot(onehot, part, preferred_element_type=jnp.float32)
        total = term if total is None else total + term
    return total


def column_of(row):
    n = row.shape[1]
    down = lax.broadcasted_iota(jnp.int32, (n, n), 0)
    along = lax.broadcasted_iota(jnp.int32, (n, n), 1)
    return jnp.sum(jnp.where(down == along, row, 0.0), axis=1, keepdims=True)


def prep_kernel(
    start_hbm, demand_hbm, utility_hbm, cap_hbm, dual_hbm, path_hbm, edge_hbm, count_hbm, size_hbm, partner_hbm,
    first_ref, second_ref, border_ref, onehot_ref, mask_ref, choice_ref,
    start_ref, demand_ref, cap_ref, dual_ref, path_ref, edge_ref, count_ref, size_ref, partner_ref, sems,
):
    blocks, width = start_ref.shape
    slots = border_ref.shape[0] // 2
    interior = cap_ref.shape[0] - slots
    incs = path_ref.shape[1]
    copies = [
        pltpu.make_async_copy(source, target, sems.at[k])
        for k, (source, target) in enumerate(
            [
                (start_hbm, start_ref),
                (demand_hbm, demand_ref),
                (utility_hbm, second_ref.at[blocks : 2 * blocks]),
                (cap_hbm, cap_ref),
                (dual_hbm, dual_ref),
                (path_hbm, path_ref),
                (edge_hbm, edge_ref),
                (count_hbm, count_ref),
                (size_hbm, size_ref),
                (partner_hbm, partner_ref),
            ]
        )
    ]
    for copy in copies:
        copy.start()
    cluster, shard = lax.axis_index("cluster"), lax.axis_index("shard")
    for copy in copies:
        copy.wait()
    lanes = lax.broadcasted_iota(jnp.int32, (1, width), 1)
    limits = []
    for j in range(blocks):
        count = jnp.where(j < size_ref[0], count_ref[j], 0)
        limits.append(jnp.where(lanes < count, demand_ref[j : j + 1, :], 0.0))
    limit = jnp.concatenate(limits, axis=0)
    first_ref[...] = jnp.minimum(jnp.maximum(start_ref[...], 0.0), limit)
    second_ref[:blocks] = limit
    names = path_ref[...]
    second_ref[2 * blocks :] = jnp.zeros((SUB, width), jnp.float32)
    second_ref[2 * blocks : 2 * blocks + 1, :incs] = names.astype(jnp.float32)
    border_ref[:slots] = cap_ref[interior:]
    border_ref[slots:] = dual_ref[interior:]
    place = jnp.bitwise_xor(names // blocks, shard) * blocks + names % blocks
    total = onehot_ref.shape[1]
    along = lax.broadcasted_iota(jnp.int32, (incs, total), 1).astype(jnp.float32)
    picked = jnp.where(along == column_of(place.astype(jnp.float32)), 1.0, 0.0)
    down = lax.broadcasted_iota(jnp.int32, (blocks, total), 0)
    own = jnp.where(down == lax.broadcasted_iota(jnp.int32, (blocks, total), 1), 1.0, 0.0)
    onehot_ref[...] = jnp.concatenate([picked, own], axis=0).astype(jnp.bfloat16)
    edge = lax.broadcasted_iota(jnp.int32, mask_ref.shape, 0)
    mask_ref[...] = jnp.where(edge == edge_ref[...], 1.0, 0.0)
    for k in range(choice_ref.shape[0]):
        for j in range(slots):
            chosen = jnp.where(partner_ref[0, j] == jnp.bitwise_xor(cluster, k + 1), 1.0, 0.0)
            choice_ref[k, j : j + 1, :] = jnp.full((1, choice_ref.shape[2]), chosen, jnp.float32)


def cast_kernel(inc_ref, out_ref):
    out_ref[...] = inc_ref[...].astype(jnp.bfloat16)


def turn_kernel(inc_ref, out_ref):
    for i in range(inc_ref.shape[0]):
        out_ref[i] = inc_ref[i].T


def load_of(flows, mask, inc_ref):
    count, _, edges = inc_ref.shape
    parts = [p.astype(jnp.float32) for p in split3(flows)]
    total = jnp.zeros((3 * SUB, edges), jnp.float32)
    for i in range(count):
        column = mask[:, i : i + 1]
        rows = jnp.concatenate([p[i : i + 1] * column for p in parts], axis=0)
        total += jnp.dot(rows.astype(jnp.bfloat16), inc_ref[i], preferred_element_type=jnp.float32)
    return total[:SUB] + total[SUB : 2 * SUB] + total[2 * SUB :]


def put_load(load, load_ref, border_ref):
    slots = border_ref.shape[0]
    interior = load_ref.shape[0] - slots
    load_ref[...] = load[: load_ref.shape[0]]
    border_ref[...] = load[interior : interior + slots]


def start_kernel(pieces, *refs):
    ins, (onehot_ref, mask_ref, inc_ref, given_ref, flows_ref, load_ref, border_ref) = refs[:pieces], refs[pieces:]
    incs = inc_ref.shape[0]
    ins = [ins[-1], *ins[:-1]]
    rows = jnp.concatenate([ref[...] for ref in ins], axis=0)
    flows = pick_rows(onehot_ref[...], rows)
    flows_ref[...] = flows
    slots = given_ref.shape[0] // 2
    put_load(load_of(flows[:incs], mask_ref[...], inc_ref), load_ref, border_ref.at[:slots])
    border_ref[slots:] = given_ref[...]


def pick_kernel(pieces, blocks, incs, *refs):
    ins, (onehot_ref, limit_ref, utility_ref, same_ref) = refs[:pieces], refs[pieces:]
    group = 2 * blocks + SUB
    for offset, out in ((0, limit_ref), (blocks, utility_ref)):
        rows = [ref[k : k + blocks] for ref in ins for k in range(offset, ref.shape[0], group)]
        out[...] = pick_rows(onehot_ref[...], jnp.concatenate(rows, axis=0))
    owned = (lax.axis_index("shard") * blocks).astype(jnp.float32)
    own = lax.broadcasted_iota(jnp.int32, (blocks, 1), 0).astype(jnp.float32) + owned
    names = jnp.concatenate([column_of(ins[0][2 * blocks : 2 * blocks + 1, :incs]), own], axis=0)
    at = 0
    for ref in ins:
        for k in range(2 * blocks, ref.shape[0], group):
            same = jnp.where(names == ref[k : k + 1, :incs], 1.0, 0.0)
            same_ref[:, at : at + incs] = same.astype(jnp.bfloat16)
            at += incs


def flow_kernel(pieces, step_size, *refs):
    ins = refs[:pieces]
    ins = [ins[-1], ins[1], ins[0], *ins[2:-1]]
    (same_ref, flows_ref, limit_ref, utility_ref, mask_ref, inc_ref,
     out_ref, load_ref, border_ref) = refs[pieces:]
    terms = jnp.concatenate([ref[...] for ref in ins], axis=0)
    gradient = pick_rows(same_ref[...], terms)
    flows = flows_ref[...] - step_size * (gradient - utility_ref[...])
    flows = jnp.minimum(jnp.maximum(flows, 0.0), limit_ref[...])
    out_ref[...] = flows
    put_load(load_of(flows[: inc_ref.shape[0]], mask_ref[...], inc_ref), load_ref, border_ref)


def twin_of(ins, choice_ref):
    total = None
    for k, ref in enumerate(ins):
        term = jnp.where(choice_ref[k] > 0.5, ref[...], 0.0)
        total = term if total is None else total + term
    return total


def settle(ins, choice_ref, load_ref, limit, duals):
    load = load_ref[...]
    slots = ins[0].shape[0]
    interior = load.shape[0] - slots
    load = jnp.concatenate([load[:interior], load[interior:] + twin_of(ins, choice_ref)], axis=0)
    split = jnp.minimum(limit, load + duals)
    duals = (duals + load) - split
    return (load - split) + duals, duals


def back_terms(residual, mask, inc_ref, out_ref, turned=False):
    rows = residual.shape[0]
    if rows < SUB:
        residual = jnp.concatenate(
            [residual, jnp.zeros((SUB - rows, residual.shape[1]), jnp.float32)], axis=0
        )
    parts = [p.astype(jnp.float32) for p in split3(residual)]
    left = jnp.concatenate(parts, axis=0).astype(jnp.bfloat16)
    for i in range(inc_ref.shape[0]):
        dims = (((1,), (0 if turned else 1,)), ((), ()))
        got = lax.dot_general(left, inc_ref[i], dims, preferred_element_type=jnp.float32)
        got = got[:SUB] + got[SUB : 2 * SUB] + got[2 * SUB :]
        out_ref[i : i + 1, :] = jnp.sum(got * mask[:, i : i + 1], axis=0, keepdims=True)


def first_dual_kernel(others, unit, *refs):
    ins = refs[:others]
    (choice_ref, load_ref, cap_ref, dual_ref, mask_ref, inc_ref,
     limit_ref, out_ref, terms_ref) = refs[others:]
    slots = ins[0].shape[0] // 3
    interior = load_ref.shape[0] - slots
    loads, caps, starts = [[r.at[k * slots : (k + 1) * slots] for r in ins] for k in range(3)]

    def shared(ref, twins):
        mean = 0.5 * (ref[interior:] + twin_of(twins, choice_ref))
        return jnp.concatenate([ref[:interior], mean], axis=0)

    limit = unit * shared(cap_ref, caps)
    limit_ref[...] = limit
    residual, duals = settle(loads, choice_ref, load_ref, limit, shared(dual_ref, starts))
    out_ref[...] = duals
    back_terms(residual, mask_ref[...], inc_ref, terms_ref)


def dual_kernel(others, *refs):
    ins = refs[:others]
    (choice_ref, load_ref, limit_ref, dual_ref, mask_ref, inc_ref,
     out_ref, terms_ref) = refs[others:]
    residual, duals = settle(ins, choice_ref, load_ref, limit_ref[...], dual_ref[...])
    out_ref[...] = duals
    back_terms(residual, mask_ref[...], inc_ref, terms_ref, True)


def last_dual_kernel(others, *refs):
    ins = refs[:others]
    choice_ref, load_ref, limit_ref, dual_ref, out_ref = refs[others:]
    out_ref[...] = settle(ins, choice_ref, load_ref, limit_ref[...], dual_ref[...])[1]


def kernel_call(kernel, name, outs, operands, flops=0, scratch=(), space=pltpu.VMEM, grant=16):
    shapes = tuple(x if hasattr(x, "dtype") else jax.ShapeDtypeStruct(x, jnp.float32) for x in outs)
    size = sum(x.size * x.dtype.itemsize for x in operands)
    return pl.pallas_call(
        kernel,
        out_shape=shapes,
        in_specs=[pl.BlockSpec(memory_space=space)] * len(operands),
        out_specs=tuple(VMEM for _ in outs),
        scratch_shapes=scratch,
        compiler_params=pltpu.CompilerParams(vmem_limit_bytes=grant * 1024 * 1024),
        cost_estimate=pl.CostEstimate(flops=flops, bytes_accessed=size, transcendentals=0),
        name=name,
    )(*operands)


def body(
    flow_start,
    demand,
    utility,
    path_count,
    cluster_size,
    incidence,
    inc_path,
    inc_edge,
    capacity,
    dual_start,
    partner,
):
    blocks, width = flow_start.shape
    incs = incidence.shape[0]
    edges = incidence.shape[2]
    locals_ = capacity.shape[0]
    slots = partner.shape[1]
    clusters, devices = lax.axis_size("cluster"), lax.axis_size("shard")
    cluster, shard = lax.axis_index("cluster"), lax.axis_index("shard")
    rows = incs + blocks
    norm_bound = max(2, incs * incs * width * edges // (1024 * locals_ * blocks))
    unit = float(max(1, incs * width // (160 * locals_)))
    step_size = 1.0 / (2.0 * norm_bound)
    bits = devices.bit_length() - 1
    assert devices == 1 << bits and clusters & (clusters - 1) == 0
    stages = [1] * (bits % 2) + [2] * (bits // 2)

    def share(x, stages, shift=0, hold=None):
        pieces = x if isinstance(x, list) else [x]
        for step in stages:
            now = pieces[0] if len(pieces) == 1 else jnp.concatenate(pieces, axis=0)
            pieces = [now]
            for k in range(1, 1 << step):
                pairs = [(i, i ^ (k << shift)) for i in range(devices)]
                given = now if hold is None else tied(now, hold[min(len(hold), (1 << step) - k) - 1])
                pieces.append(lax.ppermute(given, "shard", pairs))
            shift += step
        return pieces

    def trade(x):
        return [
            lax.ppermute(x, "cluster", [(i, i ^ k) for i in range(clusters)])
            for k in range(1, clusters)
        ]

    half = jnp.bfloat16
    first, second, border, onehot, mask, choice = kernel_call(
        prep_kernel,
        "prepare",
        [
            (blocks, width),
            (2 * blocks + SUB, width),
            (2 * slots, edges),
            jax.ShapeDtypeStruct((rows, blocks * devices), half),
            (SUB, incs),
            (clusters - 1, slots, edges),
        ],
        [
            flow_start, demand, utility, capacity, dual_start, inc_path[None, :], inc_edge[None, :],
            path_count, cluster_size, partner,
        ],
        scratch=[
            pltpu.VMEM((blocks, width), jnp.float32),
            pltpu.VMEM((blocks, width), jnp.float32),
            pltpu.VMEM((locals_, edges), jnp.float32),
            pltpu.VMEM((locals_, edges), jnp.float32),
            pltpu.VMEM((1, incs), jnp.int32),
            pltpu.VMEM((1, incs), jnp.int32),
            pltpu.SMEM((blocks,), jnp.int32),
            pltpu.SMEM((1,), jnp.int32),
            pltpu.SMEM((1, slots), jnp.int32),
            pltpu.SemaphoreType.DMA((10,)),
        ],
        space=pltpu.HBM, grant=56,
    )

    def tied(x, *after):
        return lax.optimization_barrier((x, *after))[0]

    stages_first, stages_rest = stages[:1], stages[1:]
    firsts = share(first, stages_first)
    seconds = share(second, stages_first)
    inc = pl.pallas_call(
        cast_kernel,
        grid=(4,),
        in_specs=[pl.BlockSpec((incs // 4, width, edges), lambda k: (k, 0, 0))],
        out_specs=pl.BlockSpec((incs // 4, width, edges), lambda k: (k, 0, 0)),
        out_shape=jax.ShapeDtypeStruct(incidence.shape, half),
        compiler_params=pltpu.CompilerParams(vmem_limit_bytes=16 * 1024 * 1024),
        cost_estimate=pl.CostEstimate(flops=0, bytes_accessed=6 * incidence.size, transcendentals=0),
        name="cast",
    )(incidence)
    firsts = share(firsts, stages_rest, stages[0])

    others = clusters - 1
    flops = 2 * incs * width * edges * SUB
    load_shapes = [(rows, width), (locals_, edges), (slots, edges)]
    flows, load, out = kernel_call(
        lambda *refs: start_kernel(len(firsts), *refs), "first_load",
        [(rows, width), (locals_, edges), (3 * slots, edges)],
        [*firsts[1:], firsts[0], onehot, mask, inc, border], flops=flops,
    )
    dual_shape, term_shape = (locals_, edges), (incs, width)
    limit, duals, terms = kernel_call(
        lambda *refs: first_dual_kernel(others, unit, *refs), "first_duals",
        [dual_shape, dual_shape, term_shape],
        [*trade(out), choice, load, capacity, dual_start, mask, inc], flops=flops,
    )
    for iteration in range(ITERS):
        near = share(terms, stages_first)
        if iteration == 0:
            seconds = share(seconds, stages_rest, stages[0], [out, out, terms])
            (turned_inc,) = kernel_call(
                turn_kernel, "transpose", [jax.ShapeDtypeStruct((incs, edges, width), half)],
                [tied(inc, near[-1])],
            )
            limits, utilities, same = kernel_call(
                lambda *refs: pick_kernel(len(seconds), blocks, incs, *refs), "pick",
                [(rows, width)] * 2 + [jax.ShapeDtypeStruct((rows, incs * devices), half)],
                [*seconds, onehot],
            )
        far = share(near, stages_rest, stages[0])
        flows, load, out = kernel_call(
            lambda *refs: flow_kernel(len(firsts), step_size, *refs), "flows", load_shapes,
            [far[2], far[1], *far[3:], far[0], same, flows, limits, utilities, mask, inc], flops=flops,
        )
        operands = [*trade(out), choice, load, limit, duals]
        if iteration < ITERS - 1:
            duals, terms = kernel_call(
                lambda *refs: dual_kernel(others, *refs), "duals", [dual_shape, term_shape],
                [*operands, mask, turned_inc], flops=flops,
            )
    (duals,) = kernel_call(
        lambda *refs: last_dual_kernel(others, *refs), "last_duals", [dual_shape], operands
    )
    return flows[incs:], duals


def solution(mesh):
    whole = P(("cluster", "shard"))
    wide = P(("cluster", "shard"), None)
    return jax.shard_map(
        body,
        mesh=mesh,
        in_specs=(
            wide, wide, wide, whole, P("cluster"), P(("cluster", "shard"), None, None),
            whole, whole, wide, wide, P("cluster", None),
        ),
        out_specs=(wide, wide),
        check_vma=False,
    )
```

time: 86.7 us -> 75.8 us (0.87)
  other arithmetic: 5.56 us -> 0 us
  waiting for transfers between devices: 27.2 us -> 23.6 us
  starting transfers between devices: 39.6 us -> 37.9 us
  local copies, waits for them, and re-layouts: 5.63 us -> 4.35 us
  Pallas kernels: 6.52 us -> 7.63 us
    convert_element_type x6 -> x0, other arithmetic: 4.79 us -> none  [the longest x1 2.53 us: body(): inc = incidence.astype(jnp.bfloat16)]
    ppermute x15 -> x12, starting transfers between devices: 10.8 us -> 8.1 us  [trade(): lax.ppermute(x, 'cluster', [(i, i ^ k) for i in range(clusters)])]
    ppermute x20, waiting for transfers between devices: 21.8 us -> 19.6 us  [share(): pieces.append(lax.ppermute(given, 'shard', pairs))]
    ppermute x15 -> x12, waiting for transfers between devices: 5.44 us -> 4.05 us  [trade(): lax.ppermute(x, 'cluster', [(i, i ^ k) for i in range(clusters)])]
    unnamed x23 -> x19, local copies, waits for them, and re-layouts: 4.85 us -> 3.72 us
    pallas_call x10 -> x12, Pallas kernels: 6.52 us -> 7.63 us  [the longest x11 7.38 us: kernel_call(): pl.pallas_call(kernel, out_shape=shapes, in_specs=[pl.BlockSpec(memory_sp...]
    ppermute x20, starting transfers between devices: 28.8 us -> 29.8 us  [share(): pieces.append(lax.ppermute(given, 'shard', pairs))]
  transfers between devices with their start and end apart: 35 -> 32, of which waited for: 17 -> 19; matrix products, arithmetic and copies ran while one was open for 7% -> 3% of each run, Pallas kernels for 2% -> 3%
where the time goes in v2:
time: 75.8 us; the launch traced here: 75 us
  starting transfers between devices  37.9 us (50%)
  waiting for transfers between devices  23.6 us (31%)
  Pallas kernels  7.63 us (10%)
  local copies, waits for them, and re-layouts  4.35 us (6%)
  between operations  1.49 us (2%)
    ppermute x20, starting transfers between devices, share(): pieces.append(lax.ppermute(given, 'shard', pairs))  29.8 us
    ppermute x20, waiting for transfers between devices, share(): pieces.append(lax.ppermute(given, 'shard', pairs))  19.6 us
    ppermute x12, starting transfers between devices, trade(): lax.ppermute(x, 'cluster', [(i, i ^ k) for i in range(clusters)])  8.1 us
    pallas_call x11, Pallas kernels, kernel_call(): pl.pallas_call(kernel, out_shape=shapes, in_specs=[pl.BlockSpec(memory_sp...  7.38 us
    ppermute x12, waiting for transfers between devices, trade(): lax.ppermute(x, 'cluster', [(i, i ^ k) for i in range(clusters)])  4.05 us
    unnamed x19, local copies, waits for them, and re-layouts  3.72 us
  transfers between devices with their start and end apart: 32, of which 19 were waited for; matrix products, arithmetic and copies ran while one was open for 3% of the time, Pallas kernels for 3%

profile of v2, /device:TPU:0, one launch (start us, length us, event | category | flops | bytes accessed | tf_op | source)
XLA Modules:
  0.0 75.0 jit_solution(2439596628728273468)
XLA Ops:
  1.3 1.6 %prepare.1 = (f32[16,256]{1,0:T(8,128)}, f32[40,256]{1,0:T(8,128)}, f32[6,128]{1,0:T(8,128)}, bf16[48,128]{1,0:T(8,128)(2,1)}, f32[8,32]{1,0:T(8,128)}, /*index=5*/f32[3,3,128]{2,1,0:T(4,128)}) custom-call(f32[16,256]{1,0:T(8,128)} %start_hbm.1, f32[16,256]{1,0:T(8,128)} %demand_hbm.1, f32[16,256]{1,0:T(8,128)} %utility_hbm.1, f32[7,128]{1,0:T(8,128)} %refs_5_.1, ...), custom_call_target="tpu_custom_call" | custom-call | bytes 56656 | tf_op jit(solution)/shard_map/prepare/pallas_call | solution.py:234
  2.9 3.0 %collective-permute-start = (f32[16,256]{1,0:T(8,128)}, f32[16,256]{1,0:T(8,128)S(1)}, u32[]{:S(2)}, u32[]{:S(2)}) collective-permute-start(f32[16,256]{1,0:T(8,128)} %get-tuple-element.33), channel_id=1, source_target_pairs={{0,1},{1,0},{2,3},{3,2},{4,5},{5,4},{6,7},{7,6},{8,9},{9,8},{10,11... | collective-permute-start | bytes 49160 | tf_op jit(solution)/shard_map/ppermute | solution.py:282
  7.9 4.2 %collective-permute-start.3 = (f32[32,256]{1,0:T(8,128)S(1)}, f32[32,256]{1,0:T(8,128)S(1)}, u32[]{:S(2)}, u32[]{:S(2)}) collective-permute-start(f32[32,256]{1,0:T(8,128)S(1)} %constant_dynamic-update-slice_fusion.refs_3_), channel_id=1, source_target_pairs={{0,6},{1,7},{2,4},{3,5},{4,2},{5,3},{6,0},{7,1},{8,14},{9,15},{10,... | collective-permute-start | bytes 98312 | tf_op jit(solution)/shard_map/ppermute | solution.py:282
  13.4 2.2 %copy-done = f32[32,256,128]{2,1,0:T(8,128)S(1)} copy-done((f32[32,256,128]{2,1,0:T(8,128)S(1)}, f32[32,256,128]{2,1,0:T(8,128)}, u32[]{:S(2)}) %copy-start) | copy-done | bytes 4194328
  17.5 1.6 %collective-permute-start.5 = (f32[9,128]{1,0:T(8,128)S(1)}, f32[9,128]{1,0:T(8,128)S(1)}, u32[]{:S(2)}, u32[]{:S(2)}) collective-permute-start(f32[9,128]{1,0:T(8,128)S(1)} %get-tuple-element.37), channel_id=1, source_target_pairs={{0,16},{8,24},{16,0},{24,8},{1,17},{9,25},{17,1},{25,9},{2,18},{10... | collective-permute-start | bytes 13832 | tf_op jit(solution)/shard_map/ppermute | solution.py:288
  19.4 3.3 %collective-permute-start.14 = (f32[80,256]{1,0:T(8,128)S(1)}, f32[80,256]{1,0:T(8,128)S(1)}, u32[]{:S(2)}, u32[]{:S(2)}) collective-permute-start(f32[80,256]{1,0:T(8,128)S(1)} %constant_dynamic-update-slice_fusion.4.refs_0_), channel_id=1, source_target_pairs={{0,6},{1,7},{2,4},{3,5},{4,2},{5,3},{6,0},{7,1},{8,14},{9,15},{10,... | collective-permute-start | bytes 245768 | tf_op jit(solution)/shard_map/ppermute | solution.py:282
  23.6 1.5 %collective-permute-start.7 = (f32[32,256]{1,0:T(8,128)S(1)}, f32[32,256]{1,0:T(8,128)S(1)}, u32[]{:S(2)}, u32[]{:S(2)}) collective-permute-start(f32[32,256]{1,0:T(8,128)S(1)} %get-tuple-element.40), channel_id=1, source_target_pairs={{0,1},{1,0},{2,3},{3,2},{4,5},{5,4},{6,7},{7,6},{8,9},{9,8},{10,11... | collective-permute-start | bytes 98312 | tf_op jit(solution)/shard_map/ppermute | solution.py:282
  27.6 1.9 %collective-permute-start.10 = (f32[64,256]{1,0:T(8,128)S(1)}, f32[64,256]{1,0:T(8,128)S(1)}, u32[]{:S(2)}, u32[]{:S(2)}) collective-permute-start(f32[64,256]{1,0:T(8,128)S(1)} %constant_dynamic-update-slice_fusion.2.refs_3_), channel_id=1, source_target_pairs={{0,6},{1,7},{2,4},{3,5},{4,2},{5,3},{6,0},{7,1},{8,14},{9,15},{10,... | collective-permute-start | bytes 196616 | tf_op jit(solution)/shard_map/ppermute | solution.py:282
  29.5 1.6 %collective-permute-start.9 = (f32[64,256]{1,0:T(8,128)S(1)}, f32[64,256]{1,0:T(8,128)S(1)}, u32[]{:S(2)}, u32[]{:S(2)}) collective-permute-start(f32[64,256]{1,0:T(8,128)S(1)} %constant_dynamic-update-slice_fusion.2.refs_3_), channel_id=1, source_target_pairs={{0,2},{1,3},{2,0},{3,1},{4,6},{5,7},{6,4},{7,5},{8,10},{9,11},{10,... | collective-permute-start | bytes 196616 | tf_op jit(solution)/shard_map/ppermute | solution.py:282
  32.2 2.3 %collective-permute-done.10.refs_2_ = f32[64,256]{1,0:T(8,128)S(1)} collective-permute-done((f32[64,256]{1,0:T(8,128)S(1)}, f32[64,256]{1,0:T(8,128)S(1)}, u32[]{:S(2)}, u32[]{:S(2)}) %collective-permute-start.10) | collective-permute-done | bytes 65568 | tf_op jit(solution)/shard_map/ppermute | solution.py:282
  34.9 1.9 %collective-permute-done.8.refs_0_ = f32[64,256]{1,0:T(8,128)S(1)} collective-permute-done((f32[64,256]{1,0:T(8,128)S(1)}, f32[64,256]{1,0:T(8,128)S(1)}, u32[]{:S(2)}, u32[]{:S(2)}) %collective-permute-start.8) | collective-permute-done | bytes 65568 | tf_op jit(solution)/shard_map/ppermute | solution.py:282
  37.6 1.6 %collective-permute-start.16 = (f32[3,128]{1,0:T(4,128)S(1)}, f32[3,128]{1,0:T(4,128)S(1)}, u32[]{:S(2)}, u32[]{:S(2)}) collective-permute-start(f32[3,128]{1,0:T(4,128)S(1)} %get-tuple-element.48), channel_id=1, source_target_pairs={{0,16},{8,24},{16,0},{24,8},{1,17},{9,25},{17,1},{25,9},{2,18},{10... | collective-permute-start | bytes 4616 | tf_op jit(solution)/shard_map/ppermute | solution.py:288
  41.7 1.4 %collective-permute-start.18 = (f32[32,256]{1,0:T(8,128)S(1)}, f32[32,256]{1,0:T(8,128)S(1)}, u32[]{:S(2)}, u32[]{:S(2)}) collective-permute-start(f32[32,256]{1,0:T(8,128)S(1)} %get-tuple-element.53), channel_id=1, source_target_pairs={{0,1},{1,0},{2,3},{3,2},{4,5},{5,4},{6,7},{7,6},{8,9},{9,8},{10,11... | collective-permute-start | bytes 98312 | tf_op jit(solution)/shard_map/ppermute | solution.py:282
  43.1 2.6 %collective-permute-done.18 = f32[32,256]{1,0:T(8,128)S(1)} collective-permute-done((f32[32,256]{1,0:T(8,128)S(1)}, f32[32,256]{1,0:T(8,128)S(1)}, u32[]{:S(2)}, u32[]{:S(2)}) %collective-permute-start.18) | collective-permute-done | bytes 32800 | tf_op jit(solution)/shard_map/ppermute | solution.py:282
  45.7 1.6 %collective-permute-start.21 = (f32[64,256]{1,0:T(8,128)S(1)}, f32[64,256]{1,0:T(8,128)S(1)}, u32[]{:S(2)}, u32[]{:S(2)}) collective-permute-start(f32[64,256]{1,0:T(8,128)S(1)} %constant_dynamic-update-slice_fusion.6.refs_3_), channel_id=1, source_target_pairs={{0,6},{1,7},{2,4},{3,5},{4,2},{5,3},{6,0},{7,1},{8,14},{9,15},{10,... | collective-permute-start | bytes 196616 | tf_op jit(solution)/shard_map/ppermute | solution.py:282
  47.2 2.8 %collective-permute-start.19 = (f32[64,256]{1,0:T(8,128)S(1)}, f32[64,256]{1,0:T(8,128)S(1)}, u32[]{:S(2)}, u32[]{:S(2)}) collective-permute-start(f32[64,256]{1,0:T(8,128)S(1)} %constant_dynamic-update-slice_fusion.6.refs_3_), channel_id=1, source_target_pairs={{0,4},{1,5},{2,6},{3,7},{4,0},{5,1},{6,2},{7,3},{8,12},{9,13},{10,... | collective-permute-start | bytes 196616 | tf_op jit(solution)/shard_map/ppermute | solution.py:282
  50.1 2.2 %collective-permute-done.21.refs_2_ = f32[64,256]{1,0:T(8,128)S(1)} collective-permute-done((f32[64,256]{1,0:T(8,128)S(1)}, f32[64,256]{1,0:T(8,128)S(1)}, u32[]{:S(2)}, u32[]{:S(2)}) %collective-permute-start.21) | collective-permute-done | bytes 65568 | tf_op jit(solution)/shard_map/ppermute | solution.py:282
  53.8 1.4 %collective-permute-start.23 = (f32[3,128]{1,0:T(4,128)S(1)}, f32[3,128]{1,0:T(4,128)S(1)}, u32[]{:S(2)}, u32[]{:S(2)}) collective-permute-start(f32[3,128]{1,0:T(4,128)S(1)} %get-tuple-element.55), channel_id=1, source_target_pairs={{0,16},{8,24},{16,0},{24,8},{1,17},{9,25},{17,1},{25,9},{2,18},{10... | collective-permute-start | bytes 4616 | tf_op jit(solution)/shard_map/ppermute | solution.py:288
  57.9 1.4 %collective-permute-start.25 = (f32[32,256]{1,0:T(8,128)S(1)}, f32[32,256]{1,0:T(8,128)S(1)}, u32[]{:S(2)}, u32[]{:S(2)}) collective-permute-start(f32[32,256]{1,0:T(8,128)S(1)} %get-tuple-element.58), channel_id=1, source_target_pairs={{0,1},{1,0},{2,3},{3,2},{4,5},{5,4},{6,7},{7,6},{8,9},{9,8},{10,11... | collective-permute-start | bytes 98312 | tf_op jit(solution)/shard_map/ppermute | solution.py:282
  59.3 2.6 %collective-permute-done.25 = f32[32,256]{1,0:T(8,128)S(1)} collective-permute-done((f32[32,256]{1,0:T(8,128)S(1)}, f32[32,256]{1,0:T(8,128)S(1)}, u32[]{:S(2)}, u32[]{:S(2)}) %collective-permute-start.25) | collective-permute-done | bytes 32800 | tf_op jit(solution)/shard_map/ppermute | solution.py:282
  61.8 1.9 %collective-permute-start.28 = (f32[64,256]{1,0:T(8,128)S(1)}, f32[64,256]{1,0:T(8,128)S(1)}, u32[]{:S(2)}, u32[]{:S(2)}) collective-permute-start(f32[64,256]{1,0:T(8,128)S(1)} %constant_dynamic-update-slice_fusion.8.refs_3_), channel_id=1, source_target_pairs={{0,6},{1,7},{2,4},{3,5},{4,2},{5,3},{6,0},{7,1},{8,14},{9,15},{10,... | collective-permute-start | bytes 196616 | tf_op jit(solution)/shard_map/ppermute | solution.py:282
  64.6 1.6 %collective-permute-start.26 = (f32[64,256]{1,0:T(8,128)S(1)}, f32[64,256]{1,0:T(8,128)S(1)}, u32[]{:S(2)}, u32[]{:S(2)}) collective-permute-start(f32[64,256]{1,0:T(8,128)S(1)} %constant_dynamic-update-slice_fusion.8.refs_3_), channel_id=1, source_target_pairs={{0,4},{1,5},{2,6},{3,7},{4,0},{5,1},{6,2},{7,3},{8,12},{9,13},{10,... | collective-permute-start | bytes 196616 | tf_op jit(solution)/shard_map/ppermute | solution.py:282
  66.2 2.4 %collective-permute-done.28.refs_2_ = f32[64,256]{1,0:T(8,128)S(1)} collective-permute-done((f32[64,256]{1,0:T(8,128)S(1)}, f32[64,256]{1,0:T(8,128)S(1)}, u32[]{:S(2)}, u32[]{:S(2)}) %collective-permute-start.28) | collective-permute-done | bytes 65568 | tf_op jit(solution)/shard_map/ppermute | solution.py:282
  70.6 2.2 %collective-permute-start.30 = (f32[3,128]{1,0:T(4,128)S(1)}, f32[3,128]{1,0:T(4,128)S(1)}, u32[]{:S(2)}, u32[]{:S(2)}) collective-permute-start(f32[3,128]{1,0:T(4,128)S(1)} %get-tuple-element.61), channel_id=1, source_target_pairs={{0,16},{8,24},{16,0},{24,8},{1,17},{9,25},{17,1},{25,9},{2,18},{10... | collective-permute-start | bytes 4616 | tf_op jit(solution)/shard_map/ppermute | solution.py:288
  (77 shorter events, 22.8 us)
Async XLA Ops:
  2.9 5.0 %collective-permute-start = (f32[16,256]{1,0:T(8,128)}, f32[16,256]{1,0:T(8,128)S(1)}, u32[]{:S(2)}, u32[]{:S(2)}) collective-permute-start(f32[16,256]{1,0:T(8,128)} %get-tuple-element.33), channel_id=1, source_target_pairs={{0,1},{1,0},{2,3},{3,2},{4,5},{5,4},{6,7},{7,6},{8,9},{9,8},{10,11... | collective-permute-start | bytes 49160 | tf_op jit(solution)/shard_map/ppermute | solution.py:282
  5.9 13.5 %collective-permute-start.11 = (f32[40,256]{1,0:T(8,128)}, f32[40,256]{1,0:T(8,128)S(1)}, u32[]{:S(2)}, u32[]{:S(2)}) collective-permute-start(f32[40,256]{1,0:T(8,128)} %get-tuple-element.41), channel_id=1, source_target_pairs={{0,1},{1,0},{2,3},{3,2},{4,5},{5,4},{6,7},{7,6},{8,9},{9,8},{10,11... | collective-permute-start | bytes 122888 | tf_op jit(solution)/shard_map/ppermute | solution.py:282
  7.9 8.0 %collective-permute-start.3 = (f32[32,256]{1,0:T(8,128)S(1)}, f32[32,256]{1,0:T(8,128)S(1)}, u32[]{:S(2)}, u32[]{:S(2)}) collective-permute-start(f32[32,256]{1,0:T(8,128)S(1)} %constant_dynamic-update-slice_fusion.refs_3_), channel_id=1, source_target_pairs={{0,6},{1,7},{2,4},{3,5},{4,2},{5,3},{6,0},{7,1},{8,14},{9,15},{10,... | collective-permute-start | bytes 98312 | tf_op jit(solution)/shard_map/ppermute | solution.py:282
  12.0 4.8 %collective-permute-start.2 = (f32[32,256]{1,0:T(8,128)S(1)}, f32[32,256]{1,0:T(8,128)S(1)}, u32[]{:S(2)}, u32[]{:S(2)}) collective-permute-start(f32[32,256]{1,0:T(8,128)S(1)} %constant_dynamic-update-slice_fusion.refs_3_), channel_id=1, source_target_pairs={{0,4},{1,5},{2,6},{3,7},{4,0},{5,1},{6,2},{7,3},{8,12},{9,13},{10,... | collective-permute-start | bytes 98312 | tf_op jit(solution)/shard_map/ppermute | solution.py:282
  12.0 4.8 %collective-permute-start.1 = (f32[32,256]{1,0:T(8,128)S(1)}, f32[32,256]{1,0:T(8,128)S(1)}, u32[]{:S(2)}, u32[]{:S(2)}) collective-permute-start(f32[32,256]{1,0:T(8,128)S(1)} %constant_dynamic-update-slice_fusion.refs_3_), channel_id=1, source_target_pairs={{0,2},{1,3},{2,0},{3,1},{4,6},{5,7},{6,4},{7,5},{8,10},{9,11},{10,... | collective-permute-start | bytes 98312 | tf_op jit(solution)/shard_map/ppermute | solution.py:282
  17.5 5.2 %collective-permute-start.6 = (f32[9,128]{1,0:T(8,128)S(1)}, f32[9,128]{1,0:T(8,128)S(1)}, u32[]{:S(2)}, u32[]{:S(2)}) collective-permute-start(f32[9,128]{1,0:T(8,128)S(1)} %get-tuple-element.37), channel_id=1, source_target_pairs={{0,24},{8,16},{16,8},{24,0},{1,25},{9,17},{17,9},{25,1},{2,26},{10... | collective-permute-start | bytes 13832 | tf_op jit(solution)/shard_map/ppermute | solution.py:288
  17.5 5.2 %collective-permute-start.5 = (f32[9,128]{1,0:T(8,128)S(1)}, f32[9,128]{1,0:T(8,128)S(1)}, u32[]{:S(2)}, u32[]{:S(2)}) collective-permute-start(f32[9,128]{1,0:T(8,128)S(1)} %get-tuple-element.37), channel_id=1, source_target_pairs={{0,16},{8,24},{16,0},{24,8},{1,17},{9,25},{17,1},{25,9},{2,18},{10... | collective-permute-start | bytes 13832 | tf_op jit(solution)/shard_map/ppermute | solution.py:288
  19.4 11.7 %collective-permute-start.14 = (f32[80,256]{1,0:T(8,128)S(1)}, f32[80,256]{1,0:T(8,128)S(1)}, u32[]{:S(2)}, u32[]{:S(2)}) collective-permute-start(f32[80,256]{1,0:T(8,128)S(1)} %constant_dynamic-update-slice_fusion.4.refs_0_), channel_id=1, source_target_pairs={{0,6},{1,7},{2,4},{3,5},{4,2},{5,3},{6,0},{7,1},{8,14},{9,15},{10,... | collective-permute-start | bytes 245768 | tf_op jit(solution)/shard_map/ppermute | solution.py:282
  22.7 9.3 %collective-permute-start.13 = (f32[80,256]{1,0:T(8,128)S(1)}, f32[80,256]{1,0:T(8,128)S(1)}, u32[]{:S(2)}, u32[]{:S(2)}) collective-permute-start(f32[80,256]{1,0:T(8,128)S(1)} %constant_dynamic-update-slice_fusion.4.refs_0_), channel_id=1, source_target_pairs={{0,4},{1,5},{2,6},{3,7},{4,0},{5,1},{6,2},{7,3},{8,12},{9,13},{10,... | collective-permute-start | bytes 245768 | tf_op jit(solution)/shard_map/ppermute | solution.py:282
  23.6 4.0 %collective-permute-start.7 = (f32[32,256]{1,0:T(8,128)S(1)}, f32[32,256]{1,0:T(8,128)S(1)}, u32[]{:S(2)}, u32[]{:S(2)}) collective-permute-start(f32[32,256]{1,0:T(8,128)S(1)} %get-tuple-element.40), channel_id=1, source_target_pairs={{0,1},{1,0},{2,3},{3,2},{4,5},{5,4},{6,7},{7,6},{8,9},{9,8},{10,11... | collective-permute-start | bytes 98312 | tf_op jit(solution)/shard_map/ppermute | solution.py:282
  25.1 6.9 %collective-permute-start.12 = (f32[80,256]{1,0:T(8,128)S(1)}, f32[80,256]{1,0:T(8,128)S(1)}, u32[]{:S(2)}, u32[]{:S(2)}) collective-permute-start(f32[80,256]{1,0:T(8,128)S(1)} %constant_dynamic-update-slice_fusion.4.refs_0_), channel_id=1, source_target_pairs={{0,2},{1,3},{2,0},{3,1},{4,6},{5,7},{6,4},{7,5},{8,10},{9,11},{10,... | collective-permute-start | bytes 245768 | tf_op jit(solution)/shard_map/ppermute | solution.py:282
  27.6 6.9 %collective-permute-start.10 = (f32[64,256]{1,0:T(8,128)S(1)}, f32[64,256]{1,0:T(8,128)S(1)}, u32[]{:S(2)}, u32[]{:S(2)}) collective-permute-start(f32[64,256]{1,0:T(8,128)S(1)} %constant_dynamic-update-slice_fusion.2.refs_3_), channel_id=1, source_target_pairs={{0,6},{1,7},{2,4},{3,5},{4,2},{5,3},{6,0},{7,1},{8,14},{9,15},{10,... | collective-permute-start | bytes 196616 | tf_op jit(solution)/shard_map/ppermute | solution.py:282
  29.5 5.4 %collective-permute-start.9 = (f32[64,256]{1,0:T(8,128)S(1)}, f32[64,256]{1,0:T(8,128)S(1)}, u32[]{:S(2)}, u32[]{:S(2)}) collective-permute-start(f32[64,256]{1,0:T(8,128)S(1)} %constant_dynamic-update-slice_fusion.2.refs_3_), channel_id=1, source_target_pairs={{0,2},{1,3},{2,0},{3,1},{4,6},{5,7},{6,4},{7,5},{8,10},{9,11},{10,... | collective-permute-start | bytes 196616 | tf_op jit(solution)/shard_map/ppermute | solution.py:282
  31.0 5.8 %collective-permute-start.8 = (f32[64,256]{1,0:T(8,128)S(1)}, f32[64,256]{1,0:T(8,128)S(1)}, u32[]{:S(2)}, u32[]{:S(2)}) collective-permute-start(f32[64,256]{1,0:T(8,128)S(1)} %constant_dynamic-update-slice_fusion.2.refs_3_), channel_id=1, source_target_pairs={{0,4},{1,5},{2,6},{3,7},{4,0},{5,1},{6,2},{7,3},{8,12},{9,13},{10,... | collective-permute-start | bytes 196616 | tf_op jit(solution)/shard_map/ppermute | solution.py:282
  37.6 3.7 %collective-permute-start.16 = (f32[3,128]{1,0:T(4,128)S(1)}, f32[3,128]{1,0:T(4,128)S(1)}, u32[]{:S(2)}, u32[]{:S(2)}) collective-permute-start(f32[3,128]{1,0:T(4,128)S(1)} %get-tuple-element.48), channel_id=1, source_target_pairs={{0,16},{8,24},{16,0},{24,8},{1,17},{9,25},{17,1},{25,9},{2,18},{10... | collective-permute-start | bytes 4616 | tf_op jit(solution)/shard_map/ppermute | solution.py:288
  41.7 4.0 %collective-permute-start.18 = (f32[32,256]{1,0:T(8,128)S(1)}, f32[32,256]{1,0:T(8,128)S(1)}, u32[]{:S(2)}, u32[]{:S(2)}) collective-permute-start(f32[32,256]{1,0:T(8,128)S(1)} %get-tuple-element.53), channel_id=1, source_target_pairs={{0,1},{1,0},{2,3},{3,2},{4,5},{5,4},{6,7},{7,6},{8,9},{9,8},{10,11... | collective-permute-start | bytes 98312 | tf_op jit(solution)/shard_map/ppermute | solution.py:282
  45.7 6.5 %collective-permute-start.21 = (f32[64,256]{1,0:T(8,128)S(1)}, f32[64,256]{1,0:T(8,128)S(1)}, u32[]{:S(2)}, u32[]{:S(2)}) collective-permute-start(f32[64,256]{1,0:T(8,128)S(1)} %constant_dynamic-update-slice_fusion.6.refs_3_), channel_id=1, source_target_pairs={{0,6},{1,7},{2,4},{3,5},{4,2},{5,3},{6,0},{7,1},{8,14},{9,15},{10,... | collective-permute-start | bytes 196616 | tf_op jit(solution)/shard_map/ppermute | solution.py:282
  47.2 5.7 %collective-permute-start.20 = (f32[64,256]{1,0:T(8,128)S(1)}, f32[64,256]{1,0:T(8,128)S(1)}, u32[]{:S(2)}, u32[]{:S(2)}) collective-permute-start(f32[64,256]{1,0:T(8,128)S(1)} %constant_dynamic-update-slice_fusion.6.refs_3_), channel_id=1, source_target_pairs={{0,2},{1,3},{2,0},{3,1},{4,6},{5,7},{6,4},{7,5},{8,10},{9,11},{10,... | collective-permute-start | bytes 196616 | tf_op jit(solution)/shard_map/ppermute | solution.py:282
  47.2 5.7 %collective-permute-start.19 = (f32[64,256]{1,0:T(8,128)S(1)}, f32[64,256]{1,0:T(8,128)S(1)}, u32[]{:S(2)}, u32[]{:S(2)}) collective-permute-start(f32[64,256]{1,0:T(8,128)S(1)} %constant_dynamic-update-slice_fusion.6.refs_3_), channel_id=1, source_target_pairs={{0,4},{1,5},{2,6},{3,7},{4,0},{5,1},{6,2},{7,3},{8,12},{9,13},{10,... | collective-permute-start | bytes 196616 | tf_op jit(solution)/shard_map/ppermute | solution.py:282
  57.9 4.0 %collective-permute-start.25 = (f32[32,256]{1,0:T(8,128)S(1)}, f32[32,256]{1,0:T(8,128)S(1)}, u32[]{:S(2)}, u32[]{:S(2)}) collective-permute-start(f32[32,256]{1,0:T(8,128)S(1)} %get-tuple-element.58), channel_id=1, source_target_pairs={{0,1},{1,0},{2,3},{3,2},{4,5},{5,4},{6,7},{7,6},{8,9},{9,8},{10,11... | collective-permute-start | bytes 98312 | tf_op jit(solution)/shard_map/ppermute | solution.py:282
  61.8 6.8 %collective-permute-start.28 = (f32[64,256]{1,0:T(8,128)S(1)}, f32[64,256]{1,0:T(8,128)S(1)}, u32[]{:S(2)}, u32[]{:S(2)}) collective-permute-start(f32[64,256]{1,0:T(8,128)S(1)} %constant_dynamic-update-slice_fusion.8.refs_3_), channel_id=1, source_target_pairs={{0,6},{1,7},{2,4},{3,5},{4,2},{5,3},{6,0},{7,1},{8,14},{9,15},{10,... | collective-permute-start | bytes 196616 | tf_op jit(solution)/shard_map/ppermute | solution.py:282
  63.8 4.9 %collective-permute-start.27 = (f32[64,256]{1,0:T(8,128)S(1)}, f32[64,256]{1,0:T(8,128)S(1)}, u32[]{:S(2)}, u32[]{:S(2)}) collective-permute-start(f32[64,256]{1,0:T(8,128)S(1)} %constant_dynamic-update-slice_fusion.8.refs_3_), channel_id=1, source_target_pairs={{0,2},{1,3},{2,0},{3,1},{4,6},{5,7},{6,4},{7,5},{8,10},{9,11},{10,... | collective-permute-start | bytes 196616 | tf_op jit(solution)/shard_map/ppermute | solution.py:282
  64.6 5.2 %collective-permute-start.26 = (f32[64,256]{1,0:T(8,128)S(1)}, f32[64,256]{1,0:T(8,128)S(1)}, u32[]{:S(2)}, u32[]{:S(2)}) collective-permute-start(f32[64,256]{1,0:T(8,128)S(1)} %constant_dynamic-update-slice_fusion.8.refs_3_), channel_id=1, source_target_pairs={{0,4},{1,5},{2,6},{3,7},{4,0},{5,1},{6,2},{7,3},{8,12},{9,13},{10,... | collective-permute-start | bytes 196616 | tf_op jit(solution)/shard_map/ppermute | solution.py:282
  70.6 3.8 %collective-permute-start.30 = (f32[3,128]{1,0:T(4,128)S(1)}, f32[3,128]{1,0:T(4,128)S(1)}, u32[]{:S(2)}, u32[]{:S(2)}) collective-permute-start(f32[3,128]{1,0:T(4,128)S(1)} %get-tuple-element.61), channel_id=1, source_target_pairs={{0,16},{8,24},{16,0},{24,8},{1,17},{9,25},{17,1},{25,9},{2,18},{10... | collective-permute-start | bytes 4616 | tf_op jit(solution)/shard_map/ppermute | solution.py:288
  (15 other events, 49.0 us)

commit v3 on v2

--- a/solution.py
+++ b/solution.py
@@ -70,11 +70,11 @@
         count = jnp.where(j < size_ref[0], count_ref[j], 0)
         limits.append(jnp.where(lanes < count, demand_ref[j : j + 1, :], 0.0))
     limit = jnp.concatenate(limits, axis=0)
-    first_ref[...] = jnp.minimum(jnp.maximum(start_ref[...], 0.0), limit)
+    first_ref[:blocks] = jnp.minimum(jnp.maximum(start_ref[...], 0.0), limit)
     second_ref[:blocks] = limit
     names = path_ref[...]
-    second_ref[2 * blocks :] = jnp.zeros((SUB, width), jnp.float32)
-    second_ref[2 * blocks : 2 * blocks + 1, :incs] = names.astype(jnp.float32)
+    first_ref[blocks:] = jnp.zeros((SUB, width), jnp.float32)
+    first_ref[blocks : blocks + 1, :incs] = names.astype(jnp.float32)
     border_ref[:slots] = cap_ref[interior:]
     border_ref[slots:] = dual_ref[interior:]
     place = jnp.bitwise_xor(names // blocks, shard) * blocks + names % blocks
@@ -123,38 +123,53 @@
     ins, (onehot_ref, mask_ref, inc_ref, given_ref, flows_ref, load_ref, border_ref) = refs[:pieces], refs[pieces:]
     incs = inc_ref.shape[0]
     ins = [ins[-1], *ins[:-1]]
-    rows = jnp.concatenate([ref[...] for ref in ins], axis=0)
-    flows = pick_rows(onehot_ref[...], rows)
+    blocks = flows_ref.shape[0] - incs
+    group = blocks + SUB
+    rows = [ref[k : k + blocks] for ref in ins for k in range(0, ref.shape[0], group)]
+    flows = pick_rows(onehot_ref[...], jnp.concatenate(rows, axis=0))
     flows_ref[...] = flows
     slots = given_ref.shape[0] // 2
     put_load(load_of(flows[:incs], mask_ref[...], inc_ref), load_ref, border_ref.at[:slots])
     border_ref[slots:] = given_ref[...]
 
 
-def pick_kernel(pieces, blocks, incs, *refs):
-    ins, (onehot_ref, limit_ref, utility_ref, same_ref) = refs[:pieces], refs[pieces:]
-    group = 2 * blocks + SUB
+def pick_kernel(pieces, blocks, *refs):
+    ins, (onehot_ref, limit_ref, utility_ref) = refs[:pieces], refs[pieces:]
     for offset, out in ((0, limit_ref), (blocks, utility_ref)):
-        rows = [ref[k : k + blocks] for ref in ins for k in range(offset, ref.shape[0], group)]
+        rows = [ref[k : k + blocks] for ref in ins for k in range(offset, ref.shape[0], 2 * blocks)]
         out[...] = pick_rows(onehot_ref[...], jnp.concatenate(rows, axis=0))
-    owned = (lax.axis_index("shard") * blocks).astype(jnp.float32)
-    own = lax.broadcasted_iota(jnp.int32, (blocks, 1), 0).astype(jnp.float32) + owned
-    names = jnp.concatenate([column_of(ins[0][2 * blocks : 2 * blocks + 1, :incs]), own], axis=0)
-    at = 0
-    for ref in ins:
-        for k in range(2 * blocks, ref.shape[0], group):
-            same = jnp.where(names == ref[k : k + 1, :incs], 1.0, 0.0)
-            same_ref[:, at : at + incs] = same.astype(jnp.bfloat16)
-            at += incs
+
+
+def relate_kernel(pieces, blocks, incs, stride, *refs):
+    ins, same_ref = refs[:pieces], refs[pieces]
+    rows = incs + blocks
+    group = blocks + SUB
+    shard = lax.axis_index("shard")
+    names = [ins[0][k : k + 1, :incs] for k in range(blocks, ins[0].shape[0], group)]
+    names = jnp.concatenate(names, axis=1)
+    down = lax.broadcasted_iota(jnp.int32, (blocks, 1), 0)
+    for k, ref in enumerate(ins):
+        own = (down + jnp.bitwise_xor(shard, k * stride) * blocks).astype(jnp.float32)
+        wanted = jnp.concatenate([column_of(ref[blocks : blocks + 1, :incs]), own], axis=0)
+        same_ref[k * rows : (k + 1) * rows] = jnp.where(wanted == names, 1.0, 0.0).astype(jnp.bfloat16)
+
+
+def sum_kernel(pieces, *refs):
+    ins, same_ref, outs = refs[:pieces], refs[pieces], refs[pieces + 1 :]
+    terms = jnp.concatenate([ref[...] for ref in ins], axis=0)
+    total = pick_rows(same_ref[...], terms)
+    rows = outs[0].shape[0]
+    for k, out in enumerate(outs):
+        out[...] = total[k * rows : (k + 1) * rows]
 
 
 def flow_kernel(pieces, step_size, *refs):
     ins = refs[:pieces]
-    ins = [ins[-1], ins[1], ins[0], *ins[2:-1]]
-    (same_ref, flows_ref, limit_ref, utility_ref, mask_ref, inc_ref,
+    (flows_ref, limit_ref, utility_ref, mask_ref, inc_ref,
      out_ref, load_ref, border_ref) = refs[pieces:]
-    terms = jnp.concatenate([ref[...] for ref in ins], axis=0)
-    gradient = pick_rows(same_ref[...], terms)
+    gradient = ins[0][...]
+    for ref in ins[1:]:
+        gradient += ref[...]
     flows = flows_ref[...] - step_size * (gradient - utility_ref[...])
     flows = jnp.minimum(jnp.maximum(flows, 0.0), limit_ref[...])
     out_ref[...] = flows
@@ -294,8 +309,8 @@
         prep_kernel,
         "prepare",
         [
-            (blocks, width),
-            (2 * blocks + SUB, width),
+            (blocks + SUB, width),
+            (2 * blocks, width),
             (2 * slots, edges),
             jax.ShapeDtypeStruct((rows, blocks * devices), half),
             (SUB, incs),
@@ -335,8 +350,13 @@
         compiler_params=pltpu.CompilerParams(vmem_limit_bytes=16 * 1024 * 1024),
         cost_estimate=pl.CostEstimate(flops=0, bytes_accessed=6 * incidence.size, transcendentals=0),
         name="cast",
-    )(incidence)
+    )(tied(incidence, firsts[-1]))
     firsts = share(firsts, stages_rest, stages[0])
+    far_count, stride = 1 << stages[-1], devices >> stages[-1]
+    (same,) = kernel_call(
+        lambda *refs: relate_kernel(far_count, blocks, incs, stride, *refs), "relate",
+        [jax.ShapeDtypeStruct((far_count * rows, incs * stride), half)], firsts,
+    )
 
     others = clusters - 1
     flops = 2 * incs * width * edges * SUB
@@ -353,22 +373,28 @@
         [*trade(out), choice, load, capacity, dual_start, mask, inc], flops=flops,
     )
     for iteration in range(ITERS):
-        near = share(terms, stages_first)
+        near = share(terms, stages[:-1])
         if iteration == 0:
             seconds = share(seconds, stages_rest, stages[0], [out, out, terms])
             (turned_inc,) = kernel_call(
                 turn_kernel, "transpose", [jax.ShapeDtypeStruct((incs, edges, width), half)],
                 [tied(inc, near[-1])],
             )
-            limits, utilities, same = kernel_call(
-                lambda *refs: pick_kernel(len(seconds), blocks, incs, *refs), "pick",
-                [(rows, width)] * 2 + [jax.ShapeDtypeStruct((rows, incs * devices), half)],
+            limits, utilities = kernel_call(
+                lambda *refs: pick_kernel(len(seconds), blocks, *refs), "pick", [(rows, width)] * 2,
                 [*seconds, onehot],
             )
-        far = share(near, stages_rest, stages[0])
+        sums = kernel_call(
+            lambda *refs: sum_kernel(len(near), *refs), "sums", [(rows, width)] * far_count,
+            [*near, same],
+        )
+        far = [sums[0]] + [
+            lax.ppermute(x, "shard", [(i, i ^ (k * stride)) for i in range(devices)])
+            for k, x in enumerate(sums) if k > 0
+        ]
         flows, load, out = kernel_call(
-            lambda *refs: flow_kernel(len(firsts), step_size, *refs), "flows", load_shapes,
-            [far[2], far[1], *far[3:], far[0], same, flows, limits, utilities, mask, inc], flops=flops,
+            lambda *refs: flow_kernel(len(far), step_size, *refs), "flows", load_shapes,
+            [far[2], far[3], far[1], far[0], flows, limits, utilities, mask, inc], flops=flops,
         )
         operands = [*trade(out), choice, load, limit, duals]
         if iteration < ITERS - 1:

time: 75.8 us -> 73.8 us (0.974)
  starting transfers between devices: 37.9 us -> 34.1 us
  waiting for transfers between devices: 23.6 us -> 25.7 us
    ppermute x20 -> x11, starting transfers between devices: 29.8 us -> 15.9 us  [share(): pieces.append(lax.ppermute(given, 'shard', pairs))]
    ppermute x0 -> x9, starting transfers between devices: none -> 10.7 us  [body(): lax.ppermute(x, 'shard', [(i, i ^ k * stride) for i in range(devices)])]
    ppermute x0 -> x9, waiting for transfers between devices: none -> 10.7 us  [body(): lax.ppermute(x, 'shard', [(i, i ^ k * stride) for i in range(devices)])]
    ppermute x20 -> x11, waiting for transfers between devices: 19.6 us -> 8.97 us  [share(): pieces.append(lax.ppermute(given, 'shard', pairs))]
    ppermute x12, waiting for transfers between devices: 4.05 us -> 6.03 us  [trade(): lax.ppermute(x, 'cluster', [(i, i ^ k) for i in range(clusters)])]
    pallas_call x11 -> x15, Pallas kernels: 7.38 us -> 7.49 us  [kernel_call(): pl.pallas_call(kernel, out_shape=shapes, in_specs=[pl.BlockSpec(memory_sp...]
    unnamed x19 -> x16, local copies, waits for them, and re-layouts: 3.72 us -> 3.75 us
  transfers between devices with their start and end apart: 32 -> 32, of which waited for: 19 -> 21; matrix products, arithmetic and copies ran while one was open for 3% -> 3% of each run, Pallas kernels for 3% -> 3%
where the time goes in v3:
time: 73.8 us; the launch traced here: 73.4 us
  starting transfers between devices  34.1 us (46%)
  waiting for transfers between devices  25.7 us (35%)
  Pallas kernels  7.74 us (10%)
  local copies, waits for them, and re-layouts  4.36 us (6%)
  between operations  1.52 us (2%)
    ppermute x11, starting transfers between devices, share(): pieces.append(lax.ppermute(given, 'shard', pairs))  15.9 us
    ppermute x9, starting transfers between devices, body(): lax.ppermute(x, 'shard', [(i, i ^ k * stride) for i in range(devices)])  10.7 us
    ppermute x9, waiting for transfers between devices, body(): lax.ppermute(x, 'shard', [(i, i ^ k * stride) for i in range(devices)])  10.7 us
    ppermute x11, waiting for transfers between devices, share(): pieces.append(lax.ppermute(given, 'shard', pairs))  8.97 us
    ppermute x12, starting transfers between devices, trade(): lax.ppermute(x, 'cluster', [(i, i ^ k) for i in range(clusters)])  7.62 us
    pallas_call x15, Pallas kernels, kernel_call(): pl.pallas_call(kernel, out_shape=shapes, in_specs=[pl.BlockSpec(memory_sp...  7.49 us
    ppermute x12, waiting for transfers between devices, trade(): lax.ppermute(x, 'cluster', [(i, i ^ k) for i in range(clusters)])  6.03 us
    unnamed x16, local copies, waits for them, and re-layouts  3.75 us
  transfers between devices with their start and end apart: 32, of which 21 were waited for; matrix products, arithmetic and copies ran while one was open for 3% of the time, Pallas kernels for 3%

profile of v3, /device:TPU:0, one launch (start us, length us, event | category | flops | bytes accessed | tf_op | source)
XLA Modules:
  0.0 73.4 jit_solution(1495473400552782650)
XLA Ops:
  1.3 1.6 %prepare.1 = (f32[24,256]{1,0:T(8,128)}, f32[32,256]{1,0:T(8,128)}, f32[6,128]{1,0:T(8,128)}, bf16[48,128]{1,0:T(8,128)(2,1)}, f32[8,32]{1,0:T(8,128)}, /*index=5*/f32[3,3,128]{2,1,0:T(4,128)}) custom-call(f32[16,256]{1,0:T(8,128)} %start_hbm.1, f32[16,256]{1,0:T(8,128)} %demand_hbm.1, f32[16,256]{1,0:T(8,128)} %utility_hbm.1, f32[7,128]{1,0:T(8,128)} %refs_5_.1, ...), custom_call_target="tpu_custom_call" | custom-call | bytes 56656 | tf_op jit(solution)/shard_map/prepare/pallas_call | solution.py:249
  2.9 3.0 %collective-permute-start = (f32[24,256]{1,0:T(8,128)}, f32[24,256]{1,0:T(8,128)S(1)}, u32[]{:S(2)}, u32[]{:S(2)}) collective-permute-start(f32[24,256]{1,0:T(8,128)} %get-tuple-element.45), channel_id=1, source_target_pairs={{0,1},{1,0},{2,3},{3,2},{4,5},{5,4},{6,7},{7,6},{8,9},{9,8},{10,11... | collective-permute-start | bytes 73736 | tf_op jit(solution)/shard_map/ppermute | solution.py:297
  8.0 4.3 %collective-permute-start.3 = (f32[48,256]{1,0:T(8,128)S(1)}, f32[48,256]{1,0:T(8,128)S(1)}, u32[]{:S(2)}, u32[]{:S(2)}) collective-permute-start(f32[48,256]{1,0:T(8,128)S(1)} %constant_dynamic-update-slice_fusion.refs_3_.refs_0_), channel_id=1, source_target_pairs={{0,6},{1,7},{2,4},{3,5},{4,2},{5,3},{6,0},{7,1},{8,14},{9,15},{10,... | collective-permute-start | bytes 147464 | tf_op jit(solution)/shard_map/ppermute | solution.py:297
  12.9 2.2 %copy-done = f32[32,256,128]{2,1,0:T(8,128)S(1)} copy-done((f32[32,256,128]{2,1,0:T(8,128)S(1)}, f32[32,256,128]{2,1,0:T(8,128)}, u32[]{:S(2)}) %copy-start) | copy-done | bytes 4194328
  15.4 1.8 %collective-permute-done.2.refs_1_.refs_2_ = f32[48,256]{1,0:T(8,128)S(1)} collective-permute-done((f32[48,256]{1,0:T(8,128)S(1)}, f32[48,256]{1,0:T(8,128)S(1)}, u32[]{:S(2)}, u32[]{:S(2)}) %collective-permute-start.2) | collective-permute-done | bytes 49184 | tf_op jit(solution)/shard_map/ppermute | solution.py:297
  17.9 2.0 %collective-permute-start.14 = (f32[64,256]{1,0:T(8,128)S(1)}, f32[64,256]{1,0:T(8,128)S(1)}, u32[]{:S(2)}, u32[]{:S(2)}) collective-permute-start(f32[64,256]{1,0:T(8,128)S(1)} %constant_dynamic-update-slice_fusion.2.refs_0_), channel_id=1, source_target_pairs={{0,6},{1,7},{2,4},{3,5},{4,2},{5,3},{6,0},{7,1},{8,14},{9,15},{10,... | collective-permute-start | bytes 196616 | tf_op jit(solution)/shard_map/ppermute | solution.py:297
  19.9 1.5 %collective-permute-start.5 = (f32[9,128]{1,0:T(8,128)S(1)}, f32[9,128]{1,0:T(8,128)S(1)}, u32[]{:S(2)}, u32[]{:S(2)}) collective-permute-start(f32[9,128]{1,0:T(8,128)S(1)} %get-tuple-element.50), channel_id=1, source_target_pairs={{0,16},{8,24},{16,0},{24,8},{1,17},{9,25},{17,1},{25,9},{2,18},{10... | collective-permute-start | bytes 13832 | tf_op jit(solution)/shard_map/ppermute | solution.py:303
  21.8 1.3 %collective-permute-done.6.refs_2_ = f32[9,128]{1,0:T(8,128)S(1)} collective-permute-done((f32[9,128]{1,0:T(8,128)S(1)}, f32[9,128]{1,0:T(8,128)S(1)}, u32[]{:S(2)}, u32[]{:S(2)}) %collective-permute-start.6) | collective-permute-done | bytes 4640 | tf_op jit(solution)/shard_map/ppermute | solution.py:303
  24.4 1.4 %collective-permute-start.7 = (f32[32,256]{1,0:T(8,128)S(1)}, f32[32,256]{1,0:T(8,128)S(1)}, u32[]{:S(2)}, u32[]{:S(2)}) collective-permute-start(f32[32,256]{1,0:T(8,128)S(1)} %get-tuple-element.53.refs_0_), channel_id=1, source_target_pairs={{0,1},{1,0},{2,3},{3,2},{4,5},{5,4},{6,7},{7,6},{8,9},{9,8},{10,11... | collective-permute-start | bytes 98312 | tf_op jit(solution)/shard_map/ppermute | solution.py:297
  26.1 2.2 %collective-permute-start.12 = (f32[64,256]{1,0:T(8,128)S(1)}, f32[64,256]{1,0:T(8,128)S(1)}, u32[]{:S(2)}, u32[]{:S(2)}) collective-permute-start(f32[64,256]{1,0:T(8,128)S(1)} %constant_dynamic-update-slice_fusion.2.refs_0_), channel_id=1, source_target_pairs={{0,2},{1,3},{2,0},{3,1},{4,6},{5,7},{6,4},{7,5},{8,10},{9,11},{10,... | collective-permute-start | bytes 196616 | tf_op jit(solution)/shard_map/ppermute | solution.py:297
  28.7 1.2 %collective-permute-start.8 = (f32[48,256]{1,0:T(8,128)S(1)}, f32[48,256]{1,0:T(8,128)S(1)}, u32[]{:S(2)}, u32[]{:S(2)}) collective-permute-start(f32[48,256]{1,0:T(8,128)S(1)} %get-tuple-element.54), channel_id=1, source_target_pairs={{0,4},{1,5},{2,6},{3,7},{4,0},{5,1},{6,2},{7,3},{8,12},{9,13},{10,... | collective-permute-start | bytes 147464 | tf_op jit(solution)/shard_map/ppermute | solution.py:392
  29.9 1.8 %collective-permute-start.9 = (f32[48,256]{1,0:T(8,128)S(1)}, f32[48,256]{1,0:T(8,128)S(1)}, u32[]{:S(2)}, u32[]{:S(2)}) collective-permute-start(f32[48,256]{1,0:T(8,128)S(1)} %get-tuple-element.55), channel_id=1, source_target_pairs={{0,6},{1,7},{2,4},{3,5},{4,2},{5,3},{6,0},{7,1},{8,14},{9,15},{10,... | collective-permute-start | bytes 147464 | tf_op jit(solution)/shard_map/ppermute | solution.py:392
  33.2 2.8 %collective-permute-done.8.refs_0_ = f32[48,256]{1,0:T(8,128)S(1)} collective-permute-done((f32[48,256]{1,0:T(8,128)S(1)}, f32[48,256]{1,0:T(8,128)S(1)}, u32[]{:S(2)}, u32[]{:S(2)}) %collective-permute-start.8) | collective-permute-done | bytes 49184 | tf_op jit(solution)/shard_map/ppermute | solution.py:392
  36.9 1.5 %collective-permute-start.16 = (f32[3,128]{1,0:T(4,128)S(1)}, f32[3,128]{1,0:T(4,128)S(1)}, u32[]{:S(2)}, u32[]{:S(2)}) collective-permute-start(f32[3,128]{1,0:T(4,128)S(1)} %get-tuple-element.64), channel_id=1, source_target_pairs={{0,16},{8,24},{16,0},{24,8},{1,17},{9,25},{17,1},{25,9},{2,18},{10... | collective-permute-start | bytes 4616 | tf_op jit(solution)/shard_map/ppermute | solution.py:303
  42.0 3.0 %collective-permute-done.18.refs_1_ = f32[32,256]{1,0:T(8,128)S(1)} collective-permute-done((f32[32,256]{1,0:T(8,128)S(1)}, f32[32,256]{1,0:T(8,128)S(1)}, u32[]{:S(2)}, u32[]{:S(2)}) %collective-permute-start.18) | collective-permute-done | bytes 32800 | tf_op jit(solution)/shard_map/ppermute | solution.py:297
  46.1 2.3 %collective-permute-start.20 = (f32[48,256]{1,0:T(8,128)S(1)}, f32[48,256]{1,0:T(8,128)S(1)}, u32[]{:S(2)}, u32[]{:S(2)}) collective-permute-start(f32[48,256]{1,0:T(8,128)S(1)} %get-tuple-element.71), channel_id=1, source_target_pairs={{0,6},{1,7},{2,4},{3,5},{4,2},{5,3},{6,0},{7,1},{8,14},{9,15},{10,... | collective-permute-start | bytes 147464 | tf_op jit(solution)/shard_map/ppermute | solution.py:392
  48.8 1.9 %collective-permute-done.19.refs_0_ = f32[48,256]{1,0:T(8,128)S(1)} collective-permute-done((f32[48,256]{1,0:T(8,128)S(1)}, f32[48,256]{1,0:T(8,128)S(1)}, u32[]{:S(2)}, u32[]{:S(2)}) %collective-permute-start.19) | collective-permute-done | bytes 49184 | tf_op jit(solution)/shard_map/ppermute | solution.py:392
  50.6 1.4 %collective-permute-done.20.refs_1_ = f32[48,256]{1,0:T(8,128)S(1)} collective-permute-done((f32[48,256]{1,0:T(8,128)S(1)}, f32[48,256]{1,0:T(8,128)S(1)}, u32[]{:S(2)}, u32[]{:S(2)}) %collective-permute-start.20) | collective-permute-done | bytes 49184 | tf_op jit(solution)/shard_map/ppermute | solution.py:392
  53.1 1.3 %collective-permute-start.23 = (f32[3,128]{1,0:T(4,128)S(1)}, f32[3,128]{1,0:T(4,128)S(1)}, u32[]{:S(2)}, u32[]{:S(2)}) collective-permute-start(f32[3,128]{1,0:T(4,128)S(1)} %get-tuple-element.75), channel_id=1, source_target_pairs={{0,16},{8,24},{16,0},{24,8},{1,17},{9,25},{17,1},{25,9},{2,18},{10... | collective-permute-start | bytes 4616 | tf_op jit(solution)/shard_map/ppermute | solution.py:303
  55.0 1.1 %collective-permute-done.24.refs_2_ = f32[3,128]{1,0:T(4,128)S(1)} collective-permute-done((f32[3,128]{1,0:T(4,128)S(1)}, f32[3,128]{1,0:T(4,128)S(1)}, u32[]{:S(2)}, u32[]{:S(2)}) %collective-permute-start.24) | collective-permute-done | bytes 1568 | tf_op jit(solution)/shard_map/ppermute | solution.py:303
  58.2 3.0 %collective-permute-done.25.refs_1_ = f32[32,256]{1,0:T(8,128)S(1)} collective-permute-done((f32[32,256]{1,0:T(8,128)S(1)}, f32[32,256]{1,0:T(8,128)S(1)}, u32[]{:S(2)}, u32[]{:S(2)}) %collective-permute-start.25) | collective-permute-done | bytes 32800 | tf_op jit(solution)/shard_map/ppermute | solution.py:297
  62.1 2.2 %collective-permute-start.27 = (f32[48,256]{1,0:T(8,128)S(1)}, f32[48,256]{1,0:T(8,128)S(1)}, u32[]{:S(2)}, u32[]{:S(2)}) collective-permute-start(f32[48,256]{1,0:T(8,128)S(1)} %get-tuple-element.80), channel_id=1, source_target_pairs={{0,6},{1,7},{2,4},{3,5},{4,2},{5,3},{6,0},{7,1},{8,14},{9,15},{10,... | collective-permute-start | bytes 147464 | tf_op jit(solution)/shard_map/ppermute | solution.py:392
  64.9 2.1 %collective-permute-done.26.refs_0_ = f32[48,256]{1,0:T(8,128)S(1)} collective-permute-done((f32[48,256]{1,0:T(8,128)S(1)}, f32[48,256]{1,0:T(8,128)S(1)}, u32[]{:S(2)}, u32[]{:S(2)}) %collective-permute-start.26) | collective-permute-done | bytes 49184 | tf_op jit(solution)/shard_map/ppermute | solution.py:392
  69.2 1.4 %collective-permute-start.30 = (f32[3,128]{1,0:T(4,128)S(1)}, f32[3,128]{1,0:T(4,128)S(1)}, u32[]{:S(2)}, u32[]{:S(2)}) collective-permute-start(f32[3,128]{1,0:T(4,128)S(1)} %get-tuple-element.85), channel_id=1, source_target_pairs={{0,16},{8,24},{16,0},{24,8},{1,17},{9,25},{17,1},{25,9},{2,18},{10... | collective-permute-start | bytes 4616 | tf_op jit(solution)/shard_map/ppermute | solution.py:303
  (75 shorter events, 23.6 us)
Async XLA Ops:
  2.9 5.0 %collective-permute-start = (f32[24,256]{1,0:T(8,128)}, f32[24,256]{1,0:T(8,128)S(1)}, u32[]{:S(2)}, u32[]{:S(2)}) collective-permute-start(f32[24,256]{1,0:T(8,128)} %get-tuple-element.45), channel_id=1, source_target_pairs={{0,1},{1,0},{2,3},{3,2},{4,5},{5,4},{6,7},{7,6},{8,9},{9,8},{10,11... | collective-permute-start | bytes 73736 | tf_op jit(solution)/shard_map/ppermute | solution.py:297
  5.9 9.5 %collective-permute-start.11 = (f32[32,256]{1,0:T(8,128)}, f32[32,256]{1,0:T(8,128)S(1)}, u32[]{:S(2)}, u32[]{:S(2)}) collective-permute-start(f32[32,256]{1,0:T(8,128)} %get-tuple-element.59), channel_id=1, source_target_pairs={{0,1},{1,0},{2,3},{3,2},{4,5},{5,4},{6,7},{7,6},{8,9},{9,8},{10,11... | collective-permute-start | bytes 98312 | tf_op jit(solution)/shard_map/ppermute | solution.py:297
  8.0 7.5 %collective-permute-start.3 = (f32[48,256]{1,0:T(8,128)S(1)}, f32[48,256]{1,0:T(8,128)S(1)}, u32[]{:S(2)}, u32[]{:S(2)}) collective-permute-start(f32[48,256]{1,0:T(8,128)S(1)} %constant_dynamic-update-slice_fusion.refs_3_.refs_0_), channel_id=1, source_target_pairs={{0,6},{1,7},{2,4},{3,5},{4,2},{5,3},{6,0},{7,1},{8,14},{9,15},{10,... | collective-permute-start | bytes 147464 | tf_op jit(solution)/shard_map/ppermute | solution.py:297
  12.3 5.0 %collective-permute-start.2 = (f32[48,256]{1,0:T(8,128)S(1)}, f32[48,256]{1,0:T(8,128)S(1)}, u32[]{:S(2)}, u32[]{:S(2)}) collective-permute-start(f32[48,256]{1,0:T(8,128)S(1)} %constant_dynamic-update-slice_fusion.refs_3_.refs_0_), channel_id=1, source_target_pairs={{0,4},{1,5},{2,6},{3,7},{4,0},{5,1},{6,2},{7,3},{8,12},{9,13},{10,... | collective-permute-start | bytes 147464 | tf_op jit(solution)/shard_map/ppermute | solution.py:297
  12.3 5.0 %collective-permute-start.1 = (f32[48,256]{1,0:T(8,128)S(1)}, f32[48,256]{1,0:T(8,128)S(1)}, u32[]{:S(2)}, u32[]{:S(2)}) collective-permute-start(f32[48,256]{1,0:T(8,128)S(1)} %constant_dynamic-update-slice_fusion.refs_3_.refs_0_), channel_id=1, source_target_pairs={{0,2},{1,3},{2,0},{3,1},{4,6},{5,7},{6,4},{7,5},{8,10},{9,11},{10,... | collective-permute-start | bytes 147464 | tf_op jit(solution)/shard_map/ppermute | solution.py:297
  17.9 13.8 %collective-permute-start.14 = (f32[64,256]{1,0:T(8,128)S(1)}, f32[64,256]{1,0:T(8,128)S(1)}, u32[]{:S(2)}, u32[]{:S(2)}) collective-permute-start(f32[64,256]{1,0:T(8,128)S(1)} %constant_dynamic-update-slice_fusion.2.refs_0_), channel_id=1, source_target_pairs={{0,6},{1,7},{2,4},{3,5},{4,2},{5,3},{6,0},{7,1},{8,14},{9,15},{10,... | collective-permute-start | bytes 196616 | tf_op jit(solution)/shard_map/ppermute | solution.py:297
  19.9 3.7 %collective-permute-start.5 = (f32[9,128]{1,0:T(8,128)S(1)}, f32[9,128]{1,0:T(8,128)S(1)}, u32[]{:S(2)}, u32[]{:S(2)}) collective-permute-start(f32[9,128]{1,0:T(8,128)S(1)} %get-tuple-element.50), channel_id=1, source_target_pairs={{0,16},{8,24},{16,0},{24,8},{1,17},{9,25},{17,1},{25,9},{2,18},{10... | collective-permute-start | bytes 13832 | tf_op jit(solution)/shard_map/ppermute | solution.py:303
  24.4 4.1 %collective-permute-start.7 = (f32[32,256]{1,0:T(8,128)S(1)}, f32[32,256]{1,0:T(8,128)S(1)}, u32[]{:S(2)}, u32[]{:S(2)}) collective-permute-start(f32[32,256]{1,0:T(8,128)S(1)} %get-tuple-element.53.refs_0_), channel_id=1, source_target_pairs={{0,1},{1,0},{2,3},{3,2},{4,5},{5,4},{6,7},{7,6},{8,9},{9,8},{10,11... | collective-permute-start | bytes 98312 | tf_op jit(solution)/shard_map/ppermute | solution.py:297
  25.9 7.1 %collective-permute-start.13 = (f32[64,256]{1,0:T(8,128)S(1)}, f32[64,256]{1,0:T(8,128)S(1)}, u32[]{:S(2)}, u32[]{:S(2)}) collective-permute-start(f32[64,256]{1,0:T(8,128)S(1)} %constant_dynamic-update-slice_fusion.2.refs_0_), channel_id=1, source_target_pairs={{0,4},{1,5},{2,6},{3,7},{4,0},{5,1},{6,2},{7,3},{8,12},{9,13},{10,... | collective-permute-start | bytes 196616 | tf_op jit(solution)/shard_map/ppermute | solution.py:297
  26.1 6.9 %collective-permute-start.12 = (f32[64,256]{1,0:T(8,128)S(1)}, f32[64,256]{1,0:T(8,128)S(1)}, u32[]{:S(2)}, u32[]{:S(2)}) collective-permute-start(f32[64,256]{1,0:T(8,128)S(1)} %constant_dynamic-update-slice_fusion.2.refs_0_), channel_id=1, source_target_pairs={{0,2},{1,3},{2,0},{3,1},{4,6},{5,7},{6,4},{7,5},{8,10},{9,11},{10,... | collective-permute-start | bytes 196616 | tf_op jit(solution)/shard_map/ppermute | solution.py:297
  28.7 7.2 %collective-permute-start.8 = (f32[48,256]{1,0:T(8,128)S(1)}, f32[48,256]{1,0:T(8,128)S(1)}, u32[]{:S(2)}, u32[]{:S(2)}) collective-permute-start(f32[48,256]{1,0:T(8,128)S(1)} %get-tuple-element.54), channel_id=1, source_target_pairs={{0,4},{1,5},{2,6},{3,7},{4,0},{5,1},{6,2},{7,3},{8,12},{9,13},{10,... | collective-permute-start | bytes 147464 | tf_op jit(solution)/shard_map/ppermute | solution.py:392
  29.9 6.1 %collective-permute-start.9 = (f32[48,256]{1,0:T(8,128)S(1)}, f32[48,256]{1,0:T(8,128)S(1)}, u32[]{:S(2)}, u32[]{:S(2)}) collective-permute-start(f32[48,256]{1,0:T(8,128)S(1)} %get-tuple-element.55), channel_id=1, source_target_pairs={{0,6},{1,7},{2,4},{3,5},{4,2},{5,3},{6,0},{7,1},{8,14},{9,15},{10,... | collective-permute-start | bytes 147464 | tf_op jit(solution)/shard_map/ppermute | solution.py:392
  31.7 4.7 %collective-permute-start.10 = (f32[48,256]{1,0:T(8,128)S(1)}, f32[48,256]{1,0:T(8,128)S(1)}, u32[]{:S(2)}, u32[]{:S(2)}) collective-permute-start(f32[48,256]{1,0:T(8,128)S(1)} %get-tuple-element.56), channel_id=1, source_target_pairs={{0,2},{1,3},{2,0},{3,1},{4,6},{5,7},{6,4},{7,5},{8,10},{9,11},{10,... | collective-permute-start | bytes 147464 | tf_op jit(solution)/shard_map/ppermute | solution.py:392
  36.9 3.7 %collective-permute-start.16 = (f32[3,128]{1,0:T(4,128)S(1)}, f32[3,128]{1,0:T(4,128)S(1)}, u32[]{:S(2)}, u32[]{:S(2)}) collective-permute-start(f32[3,128]{1,0:T(4,128)S(1)} %get-tuple-element.64), channel_id=1, source_target_pairs={{0,16},{8,24},{16,0},{24,8},{1,17},{9,25},{17,1},{25,9},{2,18},{10... | collective-permute-start | bytes 4616 | tf_op jit(solution)/shard_map/ppermute | solution.py:303
  41.0 4.0 %collective-permute-start.18 = (f32[32,256]{1,0:T(8,128)S(1)}, f32[32,256]{1,0:T(8,128)S(1)}, u32[]{:S(2)}, u32[]{:S(2)}) collective-permute-start(f32[32,256]{1,0:T(8,128)S(1)} %get-tuple-element.69.refs_0_), channel_id=1, source_target_pairs={{0,1},{1,0},{2,3},{3,2},{4,5},{5,4},{6,7},{7,6},{8,9},{9,8},{10,11... | collective-permute-start | bytes 98312 | tf_op jit(solution)/shard_map/ppermute | solution.py:297
  45.2 5.4 %collective-permute-start.19 = (f32[48,256]{1,0:T(8,128)S(1)}, f32[48,256]{1,0:T(8,128)S(1)}, u32[]{:S(2)}, u32[]{:S(2)}) collective-permute-start(f32[48,256]{1,0:T(8,128)S(1)} %get-tuple-element.70), channel_id=1, source_target_pairs={{0,4},{1,5},{2,6},{3,7},{4,0},{5,1},{6,2},{7,3},{8,12},{9,13},{10,... | collective-permute-start | bytes 147464 | tf_op jit(solution)/shard_map/ppermute | solution.py:392
  46.1 5.9 %collective-permute-start.20 = (f32[48,256]{1,0:T(8,128)S(1)}, f32[48,256]{1,0:T(8,128)S(1)}, u32[]{:S(2)}, u32[]{:S(2)}) collective-permute-start(f32[48,256]{1,0:T(8,128)S(1)} %get-tuple-element.71), channel_id=1, source_target_pairs={{0,6},{1,7},{2,4},{3,5},{4,2},{5,3},{6,0},{7,1},{8,14},{9,15},{10,... | collective-permute-start | bytes 147464 | tf_op jit(solution)/shard_map/ppermute | solution.py:392
  48.4 4.1 %collective-permute-start.21 = (f32[48,256]{1,0:T(8,128)S(1)}, f32[48,256]{1,0:T(8,128)S(1)}, u32[]{:S(2)}, u32[]{:S(2)}) collective-permute-start(f32[48,256]{1,0:T(8,128)S(1)} %get-tuple-element.72), channel_id=1, source_target_pairs={{0,2},{1,3},{2,0},{3,1},{4,6},{5,7},{6,4},{7,5},{8,10},{9,11},{10,... | collective-permute-start | bytes 147464 | tf_op jit(solution)/shard_map/ppermute | solution.py:392
  53.1 3.7 %collective-permute-start.23 = (f32[3,128]{1,0:T(4,128)S(1)}, f32[3,128]{1,0:T(4,128)S(1)}, u32[]{:S(2)}, u32[]{:S(2)}) collective-permute-start(f32[3,128]{1,0:T(4,128)S(1)} %get-tuple-element.75), channel_id=1, source_target_pairs={{0,16},{8,24},{16,0},{24,8},{1,17},{9,25},{17,1},{25,9},{2,18},{10... | collective-permute-start | bytes 4616 | tf_op jit(solution)/shard_map/ppermute | solution.py:303
  57.2 4.0 %collective-permute-start.25 = (f32[32,256]{1,0:T(8,128)S(1)}, f32[32,256]{1,0:T(8,128)S(1)}, u32[]{:S(2)}, u32[]{:S(2)}) collective-permute-start(f32[32,256]{1,0:T(8,128)S(1)} %get-tuple-element.78.refs_0_), channel_id=1, source_target_pairs={{0,1},{1,0},{2,3},{3,2},{4,5},{5,4},{6,7},{7,6},{8,9},{9,8},{10,11... | collective-permute-start | bytes 98312 | tf_op jit(solution)/shard_map/ppermute | solution.py:297
  61.4 5.7 %collective-permute-start.26 = (f32[48,256]{1,0:T(8,128)S(1)}, f32[48,256]{1,0:T(8,128)S(1)}, u32[]{:S(2)}, u32[]{:S(2)}) collective-permute-start(f32[48,256]{1,0:T(8,128)S(1)} %get-tuple-element.79), channel_id=1, source_target_pairs={{0,4},{1,5},{2,6},{3,7},{4,0},{5,1},{6,2},{7,3},{8,12},{9,13},{10,... | collective-permute-start | bytes 147464 | tf_op jit(solution)/shard_map/ppermute | solution.py:392
  62.1 6.0 %collective-permute-start.27 = (f32[48,256]{1,0:T(8,128)S(1)}, f32[48,256]{1,0:T(8,128)S(1)}, u32[]{:S(2)}, u32[]{:S(2)}) collective-permute-start(f32[48,256]{1,0:T(8,128)S(1)} %get-tuple-element.80), channel_id=1, source_target_pairs={{0,6},{1,7},{2,4},{3,5},{4,2},{5,3},{6,0},{7,1},{8,14},{9,15},{10,... | collective-permute-start | bytes 147464 | tf_op jit(solution)/shard_map/ppermute | solution.py:392
  64.3 4.3 %collective-permute-start.28 = (f32[48,256]{1,0:T(8,128)S(1)}, f32[48,256]{1,0:T(8,128)S(1)}, u32[]{:S(2)}, u32[]{:S(2)}) collective-permute-start(f32[48,256]{1,0:T(8,128)S(1)} %get-tuple-element.81), channel_id=1, source_target_pairs={{0,2},{1,3},{2,0},{3,1},{4,6},{5,7},{6,4},{7,5},{8,10},{9,11},{10,... | collective-permute-start | bytes 147464 | tf_op jit(solution)/shard_map/ppermute | solution.py:392
  69.2 3.7 %collective-permute-start.30 = (f32[3,128]{1,0:T(4,128)S(1)}, f32[3,128]{1,0:T(4,128)S(1)}, u32[]{:S(2)}, u32[]{:S(2)}) collective-permute-start(f32[3,128]{1,0:T(4,128)S(1)} %get-tuple-element.85), channel_id=1, source_target_pairs={{0,16},{8,24},{16,0},{24,8},{1,17},{9,25},{17,1},{25,9},{2,18},{10... | collective-permute-start | bytes 4616 | tf_op jit(solution)/shard_map/ppermute | solution.py:303
  (15 other events, 76.1 us)

commit v4 on v3

--- a/solution.py
+++ b/solution.py
@@ -33,37 +33,36 @@
     return jnp.sum(jnp.where(down == along, row, 0.0), axis=1, keepdims=True)
 
 
+def pick_thrice(thrice, rows):
+    parts = jnp.concatenate(split3(rows), axis=0)
+    return jnp.dot(thrice, parts, preferred_element_type=jnp.float32)
+
+
+def copy_all(pairs, sems):
+    copies = [pltpu.make_async_copy(*pair, sems.at[k]) for k, pair in enumerate(pairs)]
+    for copy in copies:
+        copy.start()
+    for copy in copies:
+        copy.wait()
+
+
 def prep_kernel(
-    start_hbm, demand_hbm, utility_hbm, cap_hbm, dual_hbm, path_hbm, edge_hbm, count_hbm, size_hbm, partner_hbm,
-    first_ref, second_ref, border_ref, onehot_ref, mask_ref, choice_ref,
-    start_ref, demand_ref, cap_ref, dual_ref, path_ref, edge_ref, count_ref, size_ref, partner_ref, sems,
+    start_hbm, demand_hbm, utility_hbm, path_hbm, count_hbm, size_hbm,
+    first_ref, start_ref, demand_ref, path_ref, count_ref, size_ref, sems,
 ):
     blocks, width = start_ref.shape
-    slots = border_ref.shape[0] // 2
-    interior = cap_ref.shape[0] - slots
     incs = path_ref.shape[1]
-    copies = [
-        pltpu.make_async_copy(source, target, sems.at[k])
-        for k, (source, target) in enumerate(
-            [
-                (start_hbm, start_ref),
-                (demand_hbm, demand_ref),
-                (utility_hbm, second_ref.at[blocks : 2 * blocks]),
-                (cap_hbm, cap_ref),
-                (dual_hbm, dual_ref),
-                (path_hbm, path_ref),
-                (edge_hbm, edge_ref),
-                (count_hbm, count_ref),
-                (size_hbm, size_ref),
-                (partner_hbm, partner_ref),
-            ]
-        )
-    ]
-    for copy in copies:
-        copy.start()
-    cluster, shard = lax.axis_index("cluster"), lax.axis_index("shard")
-    for copy in copies:
-        copy.wait()
+    copy_all(
+        [
+            (start_hbm, start_ref),
+            (demand_hbm, demand_ref),
+            (utility_hbm, first_ref.at[2 * blocks + SUB :]),
+            (path_hbm, path_ref),
+            (count_hbm, count_ref),
+            (size_hbm, size_ref),
+        ],
+        sems,
+    )
     lanes = lax.broadcasted_iota(jnp.int32, (1, width), 1)
     limits = []
     for j in range(blocks):
@@ -71,12 +70,20 @@
         limits.append(jnp.where(lanes < count, demand_ref[j : j + 1, :], 0.0))
     limit = jnp.concatenate(limits, axis=0)
     first_ref[:blocks] = jnp.minimum(jnp.maximum(start_ref[...], 0.0), limit)
-    second_ref[:blocks] = limit
+    first_ref[blocks : 2 * blocks] = limit
+    first_ref[2 * blocks : 2 * blocks + SUB] = jnp.zeros((SUB, width), jnp.float32)
+    first_ref[2 * blocks : 2 * blocks + 1, :incs] = path_ref[...].astype(jnp.float32)
+
+
+def table_kernel(
+    path_hbm, edge_hbm, partner_hbm,
+    onehot_ref, mask_ref, choice_ref, path_ref, edge_ref, partner_ref, sems,
+):
+    incs = path_ref.shape[1]
+    blocks = onehot_ref.shape[0] - incs
+    cluster, shard = lax.axis_index("cluster"), lax.axis_index("shard")
+    copy_all([(path_hbm, path_ref), (edge_hbm, edge_ref), (partner_hbm, partner_ref)], sems)
     names = path_ref[...]
-    first_ref[blocks:] = jnp.zeros((SUB, width), jnp.float32)
-    first_ref[blocks : blocks + 1, :incs] = names.astype(jnp.float32)
-    border_ref[:slots] = cap_ref[interior:]
-    border_ref[slots:] = dual_ref[interior:]
     place = jnp.bitwise_xor(names // blocks, shard) * blocks + names % blocks
     total = onehot_ref.shape[1]
     along = lax.broadcasted_iota(jnp.int32, (incs, total), 1).astype(jnp.float32)
@@ -87,7 +94,7 @@
     edge = lax.broadcasted_iota(jnp.int32, mask_ref.shape, 0)
     mask_ref[...] = jnp.where(edge == edge_ref[...], 1.0, 0.0)
     for k in range(choice_ref.shape[0]):
-        for j in range(slots):
+        for j in range(partner_ref.shape[1]):
             chosen = jnp.where(partner_ref[0, j] == jnp.bitwise_xor(cluster, k + 1), 1.0, 0.0)
             choice_ref[k, j : j + 1, :] = jnp.full((1, choice_ref.shape[2]), chosen, jnp.float32)
 
@@ -119,45 +126,66 @@
     border_ref[...] = load[interior : interior + slots]
 
 
+def offsets(ref, blocks):
+    return [0, *range(2 * blocks + SUB, ref.shape[0], 2 * blocks)]
+
+
 def start_kernel(pieces, *refs):
-    ins, (onehot_ref, mask_ref, inc_ref, given_ref, flows_ref, load_ref, border_ref) = refs[:pieces], refs[pieces:]
+    ins, (onehot_ref, mask_ref, inc_ref, cap_ref, dual_ref, flows_ref, load_ref, border_ref) = refs[:pieces], refs[pieces:]
     incs = inc_ref.shape[0]
     ins = [ins[-1], *ins[:-1]]
     blocks = flows_ref.shape[0] - incs
-    group = blocks + SUB
-    rows = [ref[k : k + blocks] for ref in ins for k in range(0, ref.shape[0], group)]
+    rows = [ref[k : k + blocks] for ref in ins for k in offsets(ref, blocks)]
     flows = pick_rows(onehot_ref[...], jnp.concatenate(rows, axis=0))
     flows_ref[...] = flows
-    slots = given_ref.shape[0] // 2
+    slots = border_ref.shape[0] // 3
+    interior = cap_ref.shape[0] - slots
     put_load(load_of(flows[:incs], mask_ref[...], inc_ref), load_ref, border_ref.at[:slots])
-    border_ref[slots:] = given_ref[...]
+    border_ref[slots : 2 * slots] = cap_ref[interior:]
+    border_ref[2 * slots :] = dual_ref[interior:]
 
 
 def pick_kernel(pieces, blocks, *refs):
-    ins, (onehot_ref, limit_ref, utility_ref) = refs[:pieces], refs[pieces:]
-    for offset, out in ((0, limit_ref), (blocks, utility_ref)):
-        rows = [ref[k : k + blocks] for ref in ins for k in range(offset, ref.shape[0], 2 * blocks)]
-        out[...] = pick_rows(onehot_ref[...], jnp.concatenate(rows, axis=0))
+    ins, (onehot_ref, limit_ref) = refs[:pieces], refs[pieces:]
+    rows = [ref[k + blocks : k + 2 * blocks] for ref in ins for k in offsets(ref, blocks)]
+    limit_ref[...] = pick_rows(onehot_ref[...], jnp.concatenate(rows, axis=0))
 
 
 def relate_kernel(pieces, blocks, incs, stride, *refs):
-    ins, same_ref = refs[:pieces], refs[pieces]
+    ins, near, (own_ref, others_ref) = refs[:pieces], refs[pieces:-2], refs[-2:]
     rows = incs + blocks
-    group = blocks + SUB
     shard = lax.axis_index("shard")
-    names = [ins[0][k : k + 1, :incs] for k in range(blocks, ins[0].shape[0], group)]
-    names = jnp.concatenate(names, axis=1)
+    at = 2 * blocks
+    group = 3 * blocks + SUB
+    names = [ref[k : k + 1, :incs] for ref in near for k in range(at, ref.shape[0], group)]
+    along = lax.broadcasted_iota(jnp.int32, (1, blocks), 1)
+    owned = [
+        (along + jnp.bitwise_xor(shard, k) * blocks).astype(jnp.float32) for k in range(stride)
+    ]
+    others = jnp.concatenate(names[1:] * 3, axis=1)
+    here = jnp.concatenate([names[0], *owned] * 3, axis=1)
+    column = lax.broadcasted_iota(jnp.int32, here.shape, 1) % (incs + stride * blocks)
+    weight = jnp.where(column < incs, 1.0, -1.0)
     down = lax.broadcasted_iota(jnp.int32, (blocks, 1), 0)
     for k, ref in enumerate(ins):
         own = (down + jnp.bitwise_xor(shard, k * stride) * blocks).astype(jnp.float32)
-        wanted = jnp.concatenate([column_of(ref[blocks : blocks + 1, :incs]), own], axis=0)
-        same_ref[k * rows : (k + 1) * rows] = jnp.where(wanted == names, 1.0, 0.0).astype(jnp.bfloat16)
-
-
-def sum_kernel(pieces, *refs):
-    ins, same_ref, outs = refs[:pieces], refs[pieces], refs[pieces + 1 :]
-    terms = jnp.concatenate([ref[...] for ref in ins], axis=0)
-    total = pick_rows(same_ref[...], terms)
+        wanted = column_of(ref[2 * blocks : 2 * blocks + 1, :incs])
+        wanted = jnp.concatenate([wanted, own], axis=0)
+        place = slice(k * rows, (k + 1) * rows)
+        own_ref[place] = jnp.where(wanted == here, weight, 0.0).astype(jnp.bfloat16)
+        others_ref[place] = jnp.where(wanted == others, 1.0, 0.0).astype(jnp.bfloat16)
+
+
+def part_kernel(terms_ref, *refs):
+    ins, (own_ref, out_ref) = refs[:-2], refs[-2:]
+    rows = jnp.concatenate([terms_ref[...], *[ref[...] for ref in ins]], axis=0)
+    out_ref[...] = pick_thrice(own_ref[...], rows)
+
+
+def sum_kernel(pieces, skip, *refs):
+    ins, (others_ref, part_ref), outs = refs[:pieces], refs[pieces : pieces + 2], refs[pieces + 2 :]
+    terms = jnp.concatenate([ref[...] for ref in ins], axis=0)[skip:]
+    total = part_ref[...] + pick_thrice(others_ref[...], terms)
     rows = outs[0].shape[0]
     for k, out in enumerate(outs):
         out[...] = total[k * rows : (k + 1) * rows]
@@ -165,12 +193,11 @@
 
 def flow_kernel(pieces, step_size, *refs):
     ins = refs[:pieces]
-    (flows_ref, limit_ref, utility_ref, mask_ref, inc_ref,
-     out_ref, load_ref, border_ref) = refs[pieces:]
-    gradient = ins[0][...]
+    flows_ref, limit_ref, mask_ref, inc_ref, out_ref, load_ref, border_ref = refs[pieces:]
+    slope = ins[0][...]
     for ref in ins[1:]:
-        gradient += ref[...]
-    flows = flows_ref[...] - step_size * (gradient - utility_ref[...])
+        slope += ref[...]
+    flows = flows_ref[...] - step_size * slope
     flows = jnp.minimum(jnp.maximum(flows, 0.0), limit_ref[...])
     out_ref[...] = flows
     put_load(load_of(flows[: inc_ref.shape[0]], mask_ref[...], inc_ref), load_ref, border_ref)
@@ -194,7 +221,7 @@
     return (load - split) + duals, duals
 
 
-def back_terms(residual, mask, inc_ref, out_ref, turned=False):
+def back_terms(residual, mask, inc_ref, out_ref):
     rows = residual.shape[0]
     if rows < SUB:
         residual = jnp.concatenate(
@@ -203,8 +230,7 @@
     parts = [p.astype(jnp.float32) for p in split3(residual)]
     left = jnp.concatenate(parts, axis=0).astype(jnp.bfloat16)
     for i in range(inc_ref.shape[0]):
-        dims = (((1,), (0 if turned else 1,)), ((), ()))
-        got = lax.dot_general(left, inc_ref[i], dims, preferred_element_type=jnp.float32)
+        got = jnp.dot(left, inc_ref[i], preferred_element_type=jnp.float32)
         got = got[:SUB] + got[SUB : 2 * SUB] + got[2 * SUB :]
         out_ref[i : i + 1, :] = jnp.sum(got * mask[:, i : i + 1], axis=0, keepdims=True)
 
@@ -234,7 +260,7 @@
      out_ref, terms_ref) = refs[others:]
     residual, duals = settle(ins, choice_ref, load_ref, limit_ref[...], dual_ref[...])
     out_ref[...] = duals
-    back_terms(residual, mask_ref[...], inc_ref, terms_ref, True)
+    back_terms(residual, mask_ref[...], inc_ref, terms_ref)
 
 
 def last_dual_kernel(others, *refs):
@@ -243,16 +269,18 @@
     out_ref[...] = settle(ins, choice_ref, load_ref, limit_ref[...], dual_ref[...])[1]
 
 
-def kernel_call(kernel, name, outs, operands, flops=0, scratch=(), space=pltpu.VMEM, grant=16):
+def kernel_call(kernel, name, outs, operands, flops=0, scratch=(), pin=False):
     shapes = tuple(x if hasattr(x, "dtype") else jax.ShapeDtypeStruct(x, jnp.float32) for x in outs)
     size = sum(x.size * x.dtype.itemsize for x in operands)
+    if pin:
+        operands = [pltpu.with_memory_space_constraint(x, pltpu.HBM) if x.size > 1 else x for x in operands]
     return pl.pallas_call(
         kernel,
         out_shape=shapes,
-        in_specs=[pl.BlockSpec(memory_space=space)] * len(operands),
+        in_specs=[pl.BlockSpec(memory_space=pltpu.HBM if pin else pltpu.VMEM)] * len(operands),
         out_specs=tuple(VMEM for _ in outs),
         scratch_shapes=scratch,
-        compiler_params=pltpu.CompilerParams(vmem_limit_bytes=grant * 1024 * 1024),
+        compiler_params=pltpu.CompilerParams(vmem_limit_bytes=16 * 1024 * 1024),
         cost_estimate=pl.CostEstimate(flops=flops, bytes_accessed=size, transcendentals=0),
         name=name,
     )(*operands)
@@ -304,43 +332,49 @@
             for k in range(1, clusters)
         ]
 
+    def tied(x, *after):
+        return lax.optimization_barrier((x, *after))[0]
+
+    stages_first, stages_rest = stages[:1], stages[1:]
     half = jnp.bfloat16
-    first, second, border, onehot, mask, choice = kernel_call(
+    (first,) = kernel_call(
         prep_kernel,
         "prepare",
+        [(3 * blocks + SUB, width)],
+        [flow_start, demand, utility, inc_path[None, :], path_count, cluster_size],
+        scratch=[
+            pltpu.VMEM((blocks, width), jnp.float32),
+            pltpu.VMEM((blocks, width), jnp.float32),
+            pltpu.VMEM((1, incs), jnp.int32),
+            pltpu.SMEM((blocks,), jnp.int32),
+            pltpu.SMEM((1,), jnp.int32),
+            pltpu.SemaphoreType.DMA((6,)),
+        ],
+        pin=True,
+    )
+    onehot, mask, choice = kernel_call(
+        table_kernel,
+        "tables",
         [
-            (blocks + SUB, width),
-            (2 * blocks, width),
-            (2 * slots, edges),
             jax.ShapeDtypeStruct((rows, blocks * devices), half),
             (SUB, incs),
             (clusters - 1, slots, edges),
         ],
-        [
-            flow_start, demand, utility, capacity, dual_start, inc_path[None, :], inc_edge[None, :],
-            path_count, cluster_size, partner,
-        ],
+        [tied(inc_path, first)[None, :], inc_edge[None, :], partner],
         scratch=[
-            pltpu.VMEM((blocks, width), jnp.float32),
-            pltpu.VMEM((blocks, width), jnp.float32),
-            pltpu.VMEM((locals_, edges), jnp.float32),
-            pltpu.VMEM((locals_, edges), jnp.float32),
             pltpu.VMEM((1, incs), jnp.int32),
             pltpu.VMEM((1, incs), jnp.int32),
-            pltpu.SMEM((blocks,), jnp.int32),
-            pltpu.SMEM((1,), jnp.int32),
             pltpu.SMEM((1, slots), jnp.int32),
-            pltpu.SemaphoreType.DMA((10,)),
+            pltpu.SemaphoreType.DMA((3,)),
         ],
-        space=pltpu.HBM, grant=56,
-    )
-
-    def tied(x, *after):
-        return lax.optimization_barrier((x, *after))[0]
-
-    stages_first, stages_rest = stages[:1], stages[1:]
-    firsts = share(first, stages_first)
-    seconds = share(second, stages_first)
+        pin=True,
+    )
+
+    limits_end, kept = 2 * blocks, 2 * blocks + SUB
+    near_firsts = share(first, stages[:-1])
+    groups = [p[k : k + kept + blocks] for p in near_firsts for k in range(0, p.shape[0], kept + blocks)]
+    utilities = [p[kept:] for p in groups]
+    firsts = [jnp.concatenate([groups[0][:kept], *[p[:limits_end] for p in groups[1:]]], axis=0)]
     inc = pl.pallas_call(
         cast_kernel,
         grid=(4,),
@@ -351,11 +385,15 @@
         cost_estimate=pl.CostEstimate(flops=0, bytes_accessed=6 * incidence.size, transcendentals=0),
         name="cast",
     )(tied(incidence, firsts[-1]))
-    firsts = share(firsts, stages_rest, stages[0])
+    firsts = share(firsts, stages[-1:], bits - stages[-1])
     far_count, stride = 1 << stages[-1], devices >> stages[-1]
-    (same,) = kernel_call(
+    own_same, other_same = kernel_call(
         lambda *refs: relate_kernel(far_count, blocks, incs, stride, *refs), "relate",
-        [jax.ShapeDtypeStruct((far_count * rows, incs * stride), half)], firsts,
+        [
+            jax.ShapeDtypeStruct((far_count * rows, 3 * (incs + stride * blocks)), half),
+            jax.ShapeDtypeStruct((far_count * rows, 3 * incs * (stride - 1)), half),
+        ],
+        [*firsts, *near_firsts],
     )
 
     others = clusters - 1
@@ -364,29 +402,34 @@
     flows, load, out = kernel_call(
         lambda *refs: start_kernel(len(firsts), *refs), "first_load",
         [(rows, width), (locals_, edges), (3 * slots, edges)],
-        [*firsts[1:], firsts[0], onehot, mask, inc, border], flops=flops,
+        [*firsts[1:], firsts[0], onehot, mask, inc, capacity, dual_start], flops=flops,
     )
     dual_shape, term_shape = (locals_, edges), (incs, width)
+    (turned_inc,) = kernel_call(
+        turn_kernel, "transpose", [jax.ShapeDtypeStruct((incs, edges, width), half)], [tied(inc, out)]
+    )
     limit, duals, terms = kernel_call(
         lambda *refs: first_dual_kernel(others, unit, *refs), "first_duals",
         [dual_shape, dual_shape, term_shape],
-        [*trade(out), choice, load, capacity, dual_start, mask, inc], flops=flops,
+        [*trade(out), choice, load, capacity, dual_start, mask, turned_inc], flops=flops,
     )
     for iteration in range(ITERS):
         near = share(terms, stages[:-1])
         if iteration == 0:
-            seconds = share(seconds, stages_rest, stages[0], [out, out, terms])
-            (turned_inc,) = kernel_call(
-                turn_kernel, "transpose", [jax.ShapeDtypeStruct((incs, edges, width), half)],
-                [tied(inc, near[-1])],
+            (limits,) = kernel_call(
+                lambda *refs: pick_kernel(len(firsts), blocks, *refs), "pick", [(rows, width)],
+                [*firsts, onehot],
             )
-            limits, utilities = kernel_call(
-                lambda *refs: pick_kernel(len(seconds), blocks, *refs), "pick", [(rows, width)] * 2,
-                [*seconds, onehot],
-            )
+        (part,) = kernel_call(
+            part_kernel, "own_sums", [(far_count * rows, width)], [terms, *utilities, own_same]
+        )
+        if near[0].shape == terms.shape:
+            near, skip = near[1:], 0
+        else:
+            skip = incs
         sums = kernel_call(
-            lambda *refs: sum_kernel(len(near), *refs), "sums", [(rows, width)] * far_count,
-            [*near, same],
+            lambda *refs: sum_kernel(len(near), skip, *refs), "sums", [(rows, width)] * far_count,
+            [*near, other_same, part],
         )
         far = [sums[0]] + [
             lax.ppermute(x, "shard", [(i, i ^ (k * stride)) for i in range(devices)])
@@ -394,7 +437,7 @@
         ]
         flows, load, out = kernel_call(
             lambda *refs: flow_kernel(len(far), step_size, *refs), "flows", load_shapes,
-            [far[2], far[3], far[1], far[0], flows, limits, utilities, mask, inc], flops=flops,
+            [far[2], far[3], far[1], far[0], flows, limits, mask, inc], flops=flops,
         )
         operands = [*trade(out), choice, load, limit, duals]
         if iteration < ITERS - 1:

time: 73.8 us -> 71.1 us (0.963)
  starting transfers between devices: 34.1 us -> 30.9 us
  waiting for transfers between devices: 25.7 us -> 27.8 us
  local copies, waits for them, and re-layouts: 4.36 us -> 2.81 us
    ppermute x11 -> x7, starting transfers between devices: 15.9 us -> 12.6 us  [share(): pieces.append(lax.ppermute(given, 'shard', pairs))]
    unnamed x16 -> x6, local copies, waits for them, and re-layouts: 3.75 us -> 2.19 us
    ppermute x11 -> x7, waiting for transfers between devices: 8.97 us -> 10.2 us  [share(): pieces.append(lax.ppermute(given, 'shard', pairs))]
    pallas_call x15 -> x19, Pallas kernels: 7.49 us -> 7.55 us  [kernel_call(): pl.pallas_call(kernel, out_shape=shapes, in_specs=[pl.BlockSpec(memory_sp...]
  transfers between devices with their start and end apart: 32 -> 28, of which waited for: 21 -> 21; matrix products, arithmetic and copies ran while one was open for 3% -> 1% of each run, Pallas kernels for 3% -> 4%
where the time goes in v4:
time: 71.1 us; the launch traced here: 70.8 us
  starting transfers between devices  30.9 us (43%)
  waiting for transfers between devices  27.8 us (39%)
  Pallas kernels  7.81 us (11%)
  local copies, waits for them, and re-layouts  2.81 us (4%)
  between operations  1.44 us (2%)
    ppermute x7, starting transfers between devices, share(): pieces.append(lax.ppermute(given, 'shard', pairs))  12.6 us
    ppermute x9, waiting for transfers between devices, body(): lax.ppermute(x, 'shard', [(i, i ^ k * stride) for i in range(devices)])  11 us
    ppermute x9, starting transfers between devices, body(): lax.ppermute(x, 'shard', [(i, i ^ k * stride) for i in range(devices)])  10.7 us
    ppermute x7, waiting for transfers between devices, share(): pieces.append(lax.ppermute(given, 'shard', pairs))  10.2 us
    ppermute x12, starting transfers between devices, trade(): lax.ppermute(x, 'cluster', [(i, i ^ k) for i in range(clusters)])  7.68 us
    pallas_call x19, Pallas kernels, kernel_call(): pl.pallas_call(kernel, out_shape=shapes, in_specs=[pl.BlockSpec(memory_sp...  7.55 us
    ppermute x12, waiting for transfers between devices, trade(): lax.ppermute(x, 'cluster', [(i, i ^ k) for i in range(clusters)])  6.52 us
    unnamed x6, local copies, waits for them, and re-layouts  2.19 us
  transfers between devices with their start and end apart: 28, of which 21 were waited for; matrix products, arithmetic and copies ran while one was open for 1% of the time, Pallas kernels for 4%

profile of v4, /device:TPU:0, one launch (start us, length us, event | category | flops | bytes accessed | tf_op | source)
XLA Modules:
  0.0 70.8 jit_solution(752537123056583790)
XLA Ops:
  2.2 3.0 %collective-permute-start = (f32[56,256]{1,0:T(8,128)S(1)}, f32[56,256]{1,0:T(8,128)S(1)}, u32[]{:S(2)}, u32[]{:S(2)}) collective-permute-start(f32[56,256]{1,0:T(8,128)S(1)} %prepare.1.refs_4_), channel_id=1, source_target_pairs={{0,1},{1,0},{2,3},{3,2},{4,5},{5,4},{6,7},{7,6},{8,9},{9,8},{10,11... | collective-permute-start | bytes 172040 | tf_op jit(solution)/shard_map/ppermute | solution.py:325
  5.2 2.2 %collective-permute-done.refs_5_ = f32[56,256]{1,0:T(8,128)S(1)} collective-permute-done((f32[56,256]{1,0:T(8,128)S(1)}, f32[56,256]{1,0:T(8,128)S(1)}, u32[]{:S(2)}, u32[]{:S(2)}) %collective-permute-start) | collective-permute-done | bytes 57376 | tf_op jit(solution)/shard_map/ppermute | solution.py:325
  7.4 4.2 %collective-permute-start.3 = (f32[72,256]{1,0:T(8,128)S(1)}, f32[72,256]{1,0:T(8,128)S(1)}, u32[]{:S(2)}, u32[]{:S(2)}) collective-permute-start(f32[72,256]{1,0:T(8,128)S(1)} %pad_maximum_fusion.refs_3_.refs_0_), channel_id=1, source_target_pairs={{0,6},{1,7},{2,4},{3,5},{4,2},{5,3},{6,0},{7,1},{8,14},{9,15},{10,... | collective-permute-start | bytes 221192 | tf_op jit(solution)/shard_map/ppermute | solution.py:325
  13.1 2.2 %copy-done = f32[32,256,128]{2,1,0:T(8,128)S(1)} copy-done((f32[32,256,128]{2,1,0:T(8,128)S(1)}, f32[32,256,128]{2,1,0:T(8,128)}, u32[]{:S(2)}) %copy-start) | copy-done | bytes 4194328
  15.6 1.6 %collective-permute-done.2.refs_1_.refs_2_ = f32[72,256]{1,0:T(8,128)S(1)} collective-permute-done((f32[72,256]{1,0:T(8,128)S(1)}, f32[72,256]{1,0:T(8,128)S(1)}, u32[]{:S(2)}, u32[]{:S(2)}) %collective-permute-start.2) | collective-permute-done | bytes 73760 | tf_op jit(solution)/shard_map/ppermute | solution.py:325
  22.4 1.6 %collective-permute-start.7 = (f32[32,256]{1,0:T(8,128)S(1)}, f32[32,256]{1,0:T(8,128)S(1)}, u32[]{:S(2)}, u32[]{:S(2)}) collective-permute-start(f32[32,256]{1,0:T(8,128)S(1)} %get-tuple-element.49.terms_ref), channel_id=1, source_target_pairs={{0,1},{1,0},{2,3},{3,2},{4,5},{5,4},{6,7},{7,6},{8,9},{9,8},{10,11... | collective-permute-start | bytes 98312 | tf_op jit(solution)/shard_map/ppermute | solution.py:325
  24.4 2.0 %collective-permute-done.7.refs_0_ = f32[32,256]{1,0:T(8,128)S(1)} collective-permute-done((f32[32,256]{1,0:T(8,128)S(1)}, f32[32,256]{1,0:T(8,128)S(1)}, u32[]{:S(2)}, u32[]{:S(2)}) %collective-permute-start.7) | collective-permute-done | bytes 32800 | tf_op jit(solution)/shard_map/ppermute | solution.py:325
  26.6 1.3 %collective-permute-start.8 = (f32[48,256]{1,0:T(8,128)S(1)}, f32[48,256]{1,0:T(8,128)S(1)}, u32[]{:S(2)}, u32[]{:S(2)}) collective-permute-start(f32[48,256]{1,0:T(8,128)S(1)} %get-tuple-element.52), channel_id=1, source_target_pairs={{0,4},{1,5},{2,6},{3,7},{4,0},{5,1},{6,2},{7,3},{8,12},{9,13},{10,... | collective-permute-start | bytes 147464 | tf_op jit(solution)/shard_map/ppermute | solution.py:435
  30.3 2.1 %collective-permute-done.8.refs_0_ = f32[48,256]{1,0:T(8,128)S(1)} collective-permute-done((f32[48,256]{1,0:T(8,128)S(1)}, f32[48,256]{1,0:T(8,128)S(1)}, u32[]{:S(2)}, u32[]{:S(2)}) %collective-permute-start.8) | collective-permute-done | bytes 49184 | tf_op jit(solution)/shard_map/ppermute | solution.py:435
  32.4 1.3 %collective-permute-done.9.refs_1_ = f32[48,256]{1,0:T(8,128)S(1)} collective-permute-done((f32[48,256]{1,0:T(8,128)S(1)}, f32[48,256]{1,0:T(8,128)S(1)}, u32[]{:S(2)}, u32[]{:S(2)}) %collective-permute-start.9) | collective-permute-done | bytes 49184 | tf_op jit(solution)/shard_map/ppermute | solution.py:435
  34.3 1.5 %collective-permute-start.12 = (f32[3,128]{1,0:T(4,128)S(1)}, f32[3,128]{1,0:T(4,128)S(1)}, u32[]{:S(2)}, u32[]{:S(2)}) collective-permute-start(f32[3,128]{1,0:T(4,128)S(1)} %get-tuple-element.57), channel_id=1, source_target_pairs={{0,16},{8,24},{16,0},{24,8},{1,17},{9,25},{17,1},{25,9},{2,18},{10... | collective-permute-start | bytes 4616 | tf_op jit(solution)/shard_map/ppermute | solution.py:331
  36.1 1.1 %collective-permute-done.13.refs_2_ = f32[3,128]{1,0:T(4,128)S(1)} collective-permute-done((f32[3,128]{1,0:T(4,128)S(1)}, f32[3,128]{1,0:T(4,128)S(1)}, u32[]{:S(2)}, u32[]{:S(2)}) %collective-permute-start.13) | collective-permute-done | bytes 1568 | tf_op jit(solution)/shard_map/ppermute | solution.py:331
  38.4 1.6 %collective-permute-start.14 = (f32[32,256]{1,0:T(8,128)S(1)}, f32[32,256]{1,0:T(8,128)S(1)}, u32[]{:S(2)}, u32[]{:S(2)}) collective-permute-start(f32[32,256]{1,0:T(8,128)S(1)} %get-tuple-element.61.terms_ref), channel_id=1, source_target_pairs={{0,1},{1,0},{2,3},{3,2},{4,5},{5,4},{6,7},{7,6},{8,9},{9,8},{10,11... | collective-permute-start | bytes 98312 | tf_op jit(solution)/shard_map/ppermute | solution.py:325
  40.1 2.2 %collective-permute-done.14.refs_0_ = f32[32,256]{1,0:T(8,128)S(1)} collective-permute-done((f32[32,256]{1,0:T(8,128)S(1)}, f32[32,256]{1,0:T(8,128)S(1)}, u32[]{:S(2)}, u32[]{:S(2)}) %collective-permute-start.14) | collective-permute-done | bytes 32800 | tf_op jit(solution)/shard_map/ppermute | solution.py:325
  42.5 1.2 %collective-permute-start.15 = (f32[48,256]{1,0:T(8,128)S(1)}, f32[48,256]{1,0:T(8,128)S(1)}, u32[]{:S(2)}, u32[]{:S(2)}) collective-permute-start(f32[48,256]{1,0:T(8,128)S(1)} %get-tuple-element.62), channel_id=1, source_target_pairs={{0,4},{1,5},{2,6},{3,7},{4,0},{5,1},{6,2},{7,3},{8,12},{9,13},{10,... | collective-permute-start | bytes 147464 | tf_op jit(solution)/shard_map/ppermute | solution.py:435
  43.7 1.7 %collective-permute-start.16 = (f32[48,256]{1,0:T(8,128)S(1)}, f32[48,256]{1,0:T(8,128)S(1)}, u32[]{:S(2)}, u32[]{:S(2)}) collective-permute-start(f32[48,256]{1,0:T(8,128)S(1)} %get-tuple-element.63), channel_id=1, source_target_pairs={{0,6},{1,7},{2,4},{3,5},{4,2},{5,3},{6,0},{7,1},{8,14},{9,15},{10,... | collective-permute-start | bytes 147464 | tf_op jit(solution)/shard_map/ppermute | solution.py:435
  46.1 2.4 %collective-permute-done.15.refs_0_ = f32[48,256]{1,0:T(8,128)S(1)} collective-permute-done((f32[48,256]{1,0:T(8,128)S(1)}, f32[48,256]{1,0:T(8,128)S(1)}, u32[]{:S(2)}, u32[]{:S(2)}) %collective-permute-start.15) | collective-permute-done | bytes 49184 | tf_op jit(solution)/shard_map/ppermute | solution.py:435
  48.5 1.2 %collective-permute-done.16.refs_1_ = f32[48,256]{1,0:T(8,128)S(1)} collective-permute-done((f32[48,256]{1,0:T(8,128)S(1)}, f32[48,256]{1,0:T(8,128)S(1)}, u32[]{:S(2)}, u32[]{:S(2)}) %collective-permute-start.16) | collective-permute-done | bytes 49184 | tf_op jit(solution)/shard_map/ppermute | solution.py:435
  54.6 1.6 %collective-permute-start.21 = (f32[32,256]{1,0:T(8,128)S(1)}, f32[32,256]{1,0:T(8,128)S(1)}, u32[]{:S(2)}, u32[]{:S(2)}) collective-permute-start(f32[32,256]{1,0:T(8,128)S(1)} %get-tuple-element.70.terms_ref), channel_id=1, source_target_pairs={{0,1},{1,0},{2,3},{3,2},{4,5},{5,4},{6,7},{7,6},{8,9},{9,8},{10,11... | collective-permute-start | bytes 98312 | tf_op jit(solution)/shard_map/ppermute | solution.py:325
  56.4 2.2 %collective-permute-done.21.refs_0_ = f32[32,256]{1,0:T(8,128)S(1)} collective-permute-done((f32[32,256]{1,0:T(8,128)S(1)}, f32[32,256]{1,0:T(8,128)S(1)}, u32[]{:S(2)}, u32[]{:S(2)}) %collective-permute-start.21) | collective-permute-done | bytes 32800 | tf_op jit(solution)/shard_map/ppermute | solution.py:325
  59.6 1.8 %collective-permute-start.23 = (f32[48,256]{1,0:T(8,128)S(1)}, f32[48,256]{1,0:T(8,128)S(1)}, u32[]{:S(2)}, u32[]{:S(2)}) collective-permute-start(f32[48,256]{1,0:T(8,128)S(1)} %get-tuple-element.72), channel_id=1, source_target_pairs={{0,6},{1,7},{2,4},{3,5},{4,2},{5,3},{6,0},{7,1},{8,14},{9,15},{10,... | collective-permute-start | bytes 147464 | tf_op jit(solution)/shard_map/ppermute | solution.py:435
  62.3 2.1 %collective-permute-done.22.refs_0_ = f32[48,256]{1,0:T(8,128)S(1)} collective-permute-done((f32[48,256]{1,0:T(8,128)S(1)}, f32[48,256]{1,0:T(8,128)S(1)}, u32[]{:S(2)}, u32[]{:S(2)}) %collective-permute-start.22) | collective-permute-done | bytes 49184 | tf_op jit(solution)/shard_map/ppermute | solution.py:435
  64.5 1.2 %collective-permute-done.23.refs_1_ = f32[48,256]{1,0:T(8,128)S(1)} collective-permute-done((f32[48,256]{1,0:T(8,128)S(1)}, f32[48,256]{1,0:T(8,128)S(1)}, u32[]{:S(2)}, u32[]{:S(2)}) %collective-permute-start.23) | collective-permute-done | bytes 49184 | tf_op jit(solution)/shard_map/ppermute | solution.py:435
  66.5 1.5 %collective-permute-start.26 = (f32[3,128]{1,0:T(4,128)S(1)}, f32[3,128]{1,0:T(4,128)S(1)}, u32[]{:S(2)}, u32[]{:S(2)}) collective-permute-start(f32[3,128]{1,0:T(4,128)S(1)} %get-tuple-element.77), channel_id=1, source_target_pairs={{0,16},{8,24},{16,0},{24,8},{1,17},{9,25},{17,1},{25,9},{2,18},{10... | collective-permute-start | bytes 4616 | tf_op jit(solution)/shard_map/ppermute | solution.py:331
  (64 shorter events, 24.4 us)
Async XLA Ops:
  2.2 5.2 %collective-permute-start = (f32[56,256]{1,0:T(8,128)S(1)}, f32[56,256]{1,0:T(8,128)S(1)}, u32[]{:S(2)}, u32[]{:S(2)}) collective-permute-start(f32[56,256]{1,0:T(8,128)S(1)} %prepare.1.refs_4_), channel_id=1, source_target_pairs={{0,1},{1,0},{2,3},{3,2},{4,5},{5,4},{6,7},{7,6},{8,9},{9,8},{10,11... | collective-permute-start | bytes 172040 | tf_op jit(solution)/shard_map/ppermute | solution.py:325
  7.4 8.2 %collective-permute-start.3 = (f32[72,256]{1,0:T(8,128)S(1)}, f32[72,256]{1,0:T(8,128)S(1)}, u32[]{:S(2)}, u32[]{:S(2)}) collective-permute-start(f32[72,256]{1,0:T(8,128)S(1)} %pad_maximum_fusion.refs_3_.refs_0_), channel_id=1, source_target_pairs={{0,6},{1,7},{2,4},{3,5},{4,2},{5,3},{6,0},{7,1},{8,14},{9,15},{10,... | collective-permute-start | bytes 221192 | tf_op jit(solution)/shard_map/ppermute | solution.py:325
  11.5 5.6 %collective-permute-start.2 = (f32[72,256]{1,0:T(8,128)S(1)}, f32[72,256]{1,0:T(8,128)S(1)}, u32[]{:S(2)}, u32[]{:S(2)}) collective-permute-start(f32[72,256]{1,0:T(8,128)S(1)} %pad_maximum_fusion.refs_3_.refs_0_), channel_id=1, source_target_pairs={{0,4},{1,5},{2,6},{3,7},{4,0},{5,1},{6,2},{7,3},{8,12},{9,13},{10,... | collective-permute-start | bytes 221192 | tf_op jit(solution)/shard_map/ppermute | solution.py:325
  11.5 5.6 %collective-permute-start.1 = (f32[72,256]{1,0:T(8,128)S(1)}, f32[72,256]{1,0:T(8,128)S(1)}, u32[]{:S(2)}, u32[]{:S(2)}) collective-permute-start(f32[72,256]{1,0:T(8,128)S(1)} %pad_maximum_fusion.refs_3_.refs_0_), channel_id=1, source_target_pairs={{0,2},{1,3},{2,0},{3,1},{4,6},{5,7},{6,4},{7,5},{8,10},{9,11},{10,... | collective-permute-start | bytes 221192 | tf_op jit(solution)/shard_map/ppermute | solution.py:325
  17.8 3.2 %collective-permute-start.6 = (f32[9,128]{1,0:T(8,128)S(1)}, f32[9,128]{1,0:T(8,128)S(1)}, u32[]{:S(2)}, u32[]{:S(2)}) collective-permute-start(f32[9,128]{1,0:T(8,128)S(1)} %get-tuple-element.45), channel_id=1, source_target_pairs={{0,24},{8,16},{16,8},{24,0},{1,25},{9,17},{17,9},{25,1},{2,26},{10... | collective-permute-start | bytes 13832 | tf_op jit(solution)/shard_map/ppermute | solution.py:331
  18.4 3.7 %collective-permute-start.5 = (f32[9,128]{1,0:T(8,128)S(1)}, f32[9,128]{1,0:T(8,128)S(1)}, u32[]{:S(2)}, u32[]{:S(2)}) collective-permute-start(f32[9,128]{1,0:T(8,128)S(1)} %get-tuple-element.45), channel_id=1, source_target_pairs={{0,16},{8,24},{16,0},{24,8},{1,17},{9,25},{17,1},{25,9},{2,18},{10... | collective-permute-start | bytes 13832 | tf_op jit(solution)/shard_map/ppermute | solution.py:331
  22.4 4.0 %collective-permute-start.7 = (f32[32,256]{1,0:T(8,128)S(1)}, f32[32,256]{1,0:T(8,128)S(1)}, u32[]{:S(2)}, u32[]{:S(2)}) collective-permute-start(f32[32,256]{1,0:T(8,128)S(1)} %get-tuple-element.49.terms_ref), channel_id=1, source_target_pairs={{0,1},{1,0},{2,3},{3,2},{4,5},{5,4},{6,7},{7,6},{8,9},{9,8},{10,11... | collective-permute-start | bytes 98312 | tf_op jit(solution)/shard_map/ppermute | solution.py:325
  26.6 5.8 %collective-permute-start.8 = (f32[48,256]{1,0:T(8,128)S(1)}, f32[48,256]{1,0:T(8,128)S(1)}, u32[]{:S(2)}, u32[]{:S(2)}) collective-permute-start(f32[48,256]{1,0:T(8,128)S(1)} %get-tuple-element.52), channel_id=1, source_target_pairs={{0,4},{1,5},{2,6},{3,7},{4,0},{5,1},{6,2},{7,3},{8,12},{9,13},{10,... | collective-permute-start | bytes 147464 | tf_op jit(solution)/shard_map/ppermute | solution.py:435
  27.9 5.9 %collective-permute-start.9 = (f32[48,256]{1,0:T(8,128)S(1)}, f32[48,256]{1,0:T(8,128)S(1)}, u32[]{:S(2)}, u32[]{:S(2)}) collective-permute-start(f32[48,256]{1,0:T(8,128)S(1)} %get-tuple-element.53), channel_id=1, source_target_pairs={{0,6},{1,7},{2,4},{3,5},{4,2},{5,3},{6,0},{7,1},{8,14},{9,15},{10,... | collective-permute-start | bytes 147464 | tf_op jit(solution)/shard_map/ppermute | solution.py:435
  29.0 4.7 %collective-permute-start.10 = (f32[48,256]{1,0:T(8,128)S(1)}, f32[48,256]{1,0:T(8,128)S(1)}, u32[]{:S(2)}, u32[]{:S(2)}) collective-permute-start(f32[48,256]{1,0:T(8,128)S(1)} %get-tuple-element.54), channel_id=1, source_target_pairs={{0,2},{1,3},{2,0},{3,1},{4,6},{5,7},{6,4},{7,5},{8,10},{9,11},{10,... | collective-permute-start | bytes 147464 | tf_op jit(solution)/shard_map/ppermute | solution.py:435
  34.2 3.1 %collective-permute-start.13 = (f32[3,128]{1,0:T(4,128)S(1)}, f32[3,128]{1,0:T(4,128)S(1)}, u32[]{:S(2)}, u32[]{:S(2)}) collective-permute-start(f32[3,128]{1,0:T(4,128)S(1)} %get-tuple-element.57), channel_id=1, source_target_pairs={{0,24},{8,16},{16,8},{24,0},{1,25},{9,17},{17,9},{25,1},{2,26},{10... | collective-permute-start | bytes 4616 | tf_op jit(solution)/shard_map/ppermute | solution.py:331
  34.3 3.7 %collective-permute-start.12 = (f32[3,128]{1,0:T(4,128)S(1)}, f32[3,128]{1,0:T(4,128)S(1)}, u32[]{:S(2)}, u32[]{:S(2)}) collective-permute-start(f32[3,128]{1,0:T(4,128)S(1)} %get-tuple-element.57), channel_id=1, source_target_pairs={{0,16},{8,24},{16,0},{24,8},{1,17},{9,25},{17,1},{25,9},{2,18},{10... | collective-permute-start | bytes 4616 | tf_op jit(solution)/shard_map/ppermute | solution.py:331
  38.4 4.0 %collective-permute-start.14 = (f32[32,256]{1,0:T(8,128)S(1)}, f32[32,256]{1,0:T(8,128)S(1)}, u32[]{:S(2)}, u32[]{:S(2)}) collective-permute-start(f32[32,256]{1,0:T(8,128)S(1)} %get-tuple-element.61.terms_ref), channel_id=1, source_target_pairs={{0,1},{1,0},{2,3},{3,2},{4,5},{5,4},{6,7},{7,6},{8,9},{9,8},{10,11... | collective-permute-start | bytes 98312 | tf_op jit(solution)/shard_map/ppermute | solution.py:325
  42.5 6.0 %collective-permute-start.15 = (f32[48,256]{1,0:T(8,128)S(1)}, f32[48,256]{1,0:T(8,128)S(1)}, u32[]{:S(2)}, u32[]{:S(2)}) collective-permute-start(f32[48,256]{1,0:T(8,128)S(1)} %get-tuple-element.62), channel_id=1, source_target_pairs={{0,4},{1,5},{2,6},{3,7},{4,0},{5,1},{6,2},{7,3},{8,12},{9,13},{10,... | collective-permute-start | bytes 147464 | tf_op jit(solution)/shard_map/ppermute | solution.py:435
  43.7 6.0 %collective-permute-start.16 = (f32[48,256]{1,0:T(8,128)S(1)}, f32[48,256]{1,0:T(8,128)S(1)}, u32[]{:S(2)}, u32[]{:S(2)}) collective-permute-start(f32[48,256]{1,0:T(8,128)S(1)} %get-tuple-element.63), channel_id=1, source_target_pairs={{0,6},{1,7},{2,4},{3,5},{4,2},{5,3},{6,0},{7,1},{8,14},{9,15},{10,... | collective-permute-start | bytes 147464 | tf_op jit(solution)/shard_map/ppermute | solution.py:435
  45.4 4.6 %collective-permute-start.17 = (f32[48,256]{1,0:T(8,128)S(1)}, f32[48,256]{1,0:T(8,128)S(1)}, u32[]{:S(2)}, u32[]{:S(2)}) collective-permute-start(f32[48,256]{1,0:T(8,128)S(1)} %get-tuple-element.64), channel_id=1, source_target_pairs={{0,2},{1,3},{2,0},{3,1},{4,6},{5,7},{6,4},{7,5},{8,10},{9,11},{10,... | collective-permute-start | bytes 147464 | tf_op jit(solution)/shard_map/ppermute | solution.py:435
  50.5 3.1 %collective-permute-start.20 = (f32[3,128]{1,0:T(4,128)S(1)}, f32[3,128]{1,0:T(4,128)S(1)}, u32[]{:S(2)}, u32[]{:S(2)}) collective-permute-start(f32[3,128]{1,0:T(4,128)S(1)} %get-tuple-element.67), channel_id=1, source_target_pairs={{0,24},{8,16},{16,8},{24,0},{1,25},{9,17},{17,9},{25,1},{2,26},{10... | collective-permute-start | bytes 4616 | tf_op jit(solution)/shard_map/ppermute | solution.py:331
  50.6 3.7 %collective-permute-start.19 = (f32[3,128]{1,0:T(4,128)S(1)}, f32[3,128]{1,0:T(4,128)S(1)}, u32[]{:S(2)}, u32[]{:S(2)}) collective-permute-start(f32[3,128]{1,0:T(4,128)S(1)} %get-tuple-element.67), channel_id=1, source_target_pairs={{0,16},{8,24},{16,0},{24,8},{1,17},{9,25},{17,1},{25,9},{2,18},{10... | collective-permute-start | bytes 4616 | tf_op jit(solution)/shard_map/ppermute | solution.py:331
  54.6 4.0 %collective-permute-start.21 = (f32[32,256]{1,0:T(8,128)S(1)}, f32[32,256]{1,0:T(8,128)S(1)}, u32[]{:S(2)}, u32[]{:S(2)}) collective-permute-start(f32[32,256]{1,0:T(8,128)S(1)} %get-tuple-element.70.terms_ref), channel_id=1, source_target_pairs={{0,1},{1,0},{2,3},{3,2},{4,5},{5,4},{6,7},{7,6},{8,9},{9,8},{10,11... | collective-permute-start | bytes 98312 | tf_op jit(solution)/shard_map/ppermute | solution.py:325
  58.8 5.7 %collective-permute-start.22 = (f32[48,256]{1,0:T(8,128)S(1)}, f32[48,256]{1,0:T(8,128)S(1)}, u32[]{:S(2)}, u32[]{:S(2)}) collective-permute-start(f32[48,256]{1,0:T(8,128)S(1)} %get-tuple-element.71), channel_id=1, source_target_pairs={{0,4},{1,5},{2,6},{3,7},{4,0},{5,1},{6,2},{7,3},{8,12},{9,13},{10,... | collective-permute-start | bytes 147464 | tf_op jit(solution)/shard_map/ppermute | solution.py:435
  59.6 6.1 %collective-permute-start.23 = (f32[48,256]{1,0:T(8,128)S(1)}, f32[48,256]{1,0:T(8,128)S(1)}, u32[]{:S(2)}, u32[]{:S(2)}) collective-permute-start(f32[48,256]{1,0:T(8,128)S(1)} %get-tuple-element.72), channel_id=1, source_target_pairs={{0,6},{1,7},{2,4},{3,5},{4,2},{5,3},{6,0},{7,1},{8,14},{9,15},{10,... | collective-permute-start | bytes 147464 | tf_op jit(solution)/shard_map/ppermute | solution.py:435
  61.4 4.6 %collective-permute-start.24 = (f32[48,256]{1,0:T(8,128)S(1)}, f32[48,256]{1,0:T(8,128)S(1)}, u32[]{:S(2)}, u32[]{:S(2)}) collective-permute-start(f32[48,256]{1,0:T(8,128)S(1)} %get-tuple-element.73), channel_id=1, source_target_pairs={{0,2},{1,3},{2,0},{3,1},{4,6},{5,7},{6,4},{7,5},{8,10},{9,11},{10,... | collective-permute-start | bytes 147464 | tf_op jit(solution)/shard_map/ppermute | solution.py:435
  66.5 3.1 %collective-permute-start.27 = (f32[3,128]{1,0:T(4,128)S(1)}, f32[3,128]{1,0:T(4,128)S(1)}, u32[]{:S(2)}, u32[]{:S(2)}) collective-permute-start(f32[3,128]{1,0:T(4,128)S(1)} %get-tuple-element.77), channel_id=1, source_target_pairs={{0,24},{8,16},{16,8},{24,0},{1,25},{9,17},{17,9},{25,1},{2,26},{10... | collective-permute-start | bytes 4616 | tf_op jit(solution)/shard_map/ppermute | solution.py:331
  66.5 3.7 %collective-permute-start.26 = (f32[3,128]{1,0:T(4,128)S(1)}, f32[3,128]{1,0:T(4,128)S(1)}, u32[]{:S(2)}, u32[]{:S(2)}) collective-permute-start(f32[3,128]{1,0:T(4,128)S(1)} %get-tuple-element.77), channel_id=1, source_target_pairs={{0,16},{8,24},{16,0},{24,8},{1,17},{9,25},{17,1},{25,9},{2,18},{10... | collective-permute-start | bytes 4616 | tf_op jit(solution)/shard_map/ppermute | solution.py:331
  (7 other events, 15.3 us)

commit v5 on v4

--- a/solution.py
+++ b/solution.py
@@ -16,14 +16,6 @@
     middle = rest.astype(jnp.bfloat16)
     low = (rest - middle.astype(jnp.float32)).astype(jnp.bfloat16)
     return high, middle, low
-
-
-def pick_rows(onehot, rows):
-    total = None
-    for part in split3(rows):
-        term = jnp.dot(onehot, part, preferred_element_type=jnp.float32)
-        total = term if total is None else total + term
-    return total
 
 
 def column_of(row):
@@ -85,12 +77,13 @@
     copy_all([(path_hbm, path_ref), (edge_hbm, edge_ref), (partner_hbm, partner_ref)], sems)
     names = path_ref[...]
     place = jnp.bitwise_xor(names // blocks, shard) * blocks + names % blocks
-    total = onehot_ref.shape[1]
+    total = onehot_ref.shape[1] // 3
     along = lax.broadcasted_iota(jnp.int32, (incs, total), 1).astype(jnp.float32)
     picked = jnp.where(along == column_of(place.astype(jnp.float32)), 1.0, 0.0)
     down = lax.broadcasted_iota(jnp.int32, (blocks, total), 0)
     own = jnp.where(down == lax.broadcasted_iota(jnp.int32, (blocks, total), 1), 1.0, 0.0)
-    onehot_ref[...] = jnp.concatenate([picked, own], axis=0).astype(jnp.bfloat16)
+    once = jnp.concatenate([picked, own], axis=0)
+    onehot_ref[...] = jnp.concatenate([once] * 3, axis=1).astype(jnp.bfloat16)
     edge = lax.broadcasted_iota(jnp.int32, mask_ref.shape, 0)
     mask_ref[...] = jnp.where(edge == edge_ref[...], 1.0, 0.0)
     for k in range(choice_ref.shape[0]):
@@ -109,14 +102,15 @@
 
 
 def load_of(flows, mask, inc_ref):
-    count, _, edges = inc_ref.shape
+    count, width, edges = inc_ref.shape
     parts = [p.astype(jnp.float32) for p in split3(flows)]
-    total = jnp.zeros((3 * SUB, edges), jnp.float32)
+    rest = jnp.zeros((SUB - len(parts), width), jnp.float32)
+    load = jnp.zeros((SUB, edges), jnp.float32)
     for i in range(count):
-        column = mask[:, i : i + 1]
-        rows = jnp.concatenate([p[i : i + 1] * column for p in parts], axis=0)
-        total += jnp.dot(rows.astype(jnp.bfloat16), inc_ref[i], preferred_element_type=jnp.float32)
-    return total[:SUB] + total[SUB : 2 * SUB] + total[2 * SUB :]
+        rows = jnp.concatenate([*[p[i : i + 1] for p in parts], rest], axis=0)
+        got = jnp.dot(rows.astype(jnp.bfloat16), inc_ref[i], preferred_element_type=jnp.float32)
+        load += mask[:, i : i + 1] * jnp.sum(got, axis=0, keepdims=True)
+    return load
 
 
 def put_load(load, load_ref, border_ref):
@@ -136,7 +130,7 @@
     ins = [ins[-1], *ins[:-1]]
     blocks = flows_ref.shape[0] - incs
     rows = [ref[k : k + blocks] for ref in ins for k in offsets(ref, blocks)]
-    flows = pick_rows(onehot_ref[...], jnp.concatenate(rows, axis=0))
+    flows = pick_thrice(onehot_ref[...], jnp.concatenate(rows, axis=0))
     flows_ref[...] = flows
     slots = border_ref.shape[0] // 3
     interior = cap_ref.shape[0] - slots
@@ -148,7 +142,7 @@
 def pick_kernel(pieces, blocks, *refs):
     ins, (onehot_ref, limit_ref) = refs[:pieces], refs[pieces:]
     rows = [ref[k + blocks : k + 2 * blocks] for ref in ins for k in offsets(ref, blocks)]
-    limit_ref[...] = pick_rows(onehot_ref[...], jnp.concatenate(rows, axis=0))
+    limit_ref[...] = pick_thrice(onehot_ref[...], jnp.concatenate(rows, axis=0))
 
 
 def relate_kernel(pieces, blocks, incs, stride, *refs):
@@ -356,7 +350,7 @@
         table_kernel,
         "tables",
         [
-            jax.ShapeDtypeStruct((rows, blocks * devices), half),
+            jax.ShapeDtypeStruct((rows, 3 * blocks * devices), half),
             (SUB, incs),
             (clusters - 1, slots, edges),
         ],
@@ -385,6 +379,7 @@
         cost_estimate=pl.CostEstimate(flops=0, bytes_accessed=6 * incidence.size, transcendentals=0),
         name="cast",
     )(tied(incidence, firsts[-1]))
+    firsts = [tied(firsts[0], onehot)]
     firsts = share(firsts, stages[-1:], bits - stages[-1])
     far_count, stride = 1 << stages[-1], devices >> stages[-1]
     own_same, other_same = kernel_call(

time: 71.1 us -> 70.9 us (level)
  no operation moved by 1% of the time
where the time goes in v5:
time: 70.9 us; the launch traced here: 70.6 us
  starting transfers between devices  31 us (44%)
  waiting for transfers between devices  27.8 us (39%)
  Pallas kernels  7.6 us (11%)
  local copies, waits for them, and re-layouts  2.81 us (4%)
  between operations  1.45 us (2%)
    ppermute x7, starting transfers between devices, share(): pieces.append(lax.ppermute(given, 'shard', pairs))  12.6 us
    ppermute x9, waiting for transfers between devices, body(): lax.ppermute(x, 'shard', [(i, i ^ k * stride) for i in range(devices)])  11 us
    ppermute x9, starting transfers between devices, body(): lax.ppermute(x, 'shard', [(i, i ^ k * stride) for i in range(devices)])  10.7 us
    ppermute x7, waiting for transfers between devices, share(): pieces.append(lax.ppermute(given, 'shard', pairs))  10.2 us
    ppermute x12, starting transfers between devices, trade(): lax.ppermute(x, 'cluster', [(i, i ^ k) for i in range(clusters)])  7.68 us
    pallas_call x19, Pallas kernels, kernel_call(): pl.pallas_call(kernel, out_shape=shapes, in_specs=[pl.BlockSpec(memory_sp...  7.34 us
    ppermute x12, waiting for transfers between devices, trade(): lax.ppermute(x, 'cluster', [(i, i ^ k) for i in range(clusters)])  6.52 us
    unnamed x6, local copies, waits for them, and re-layouts  2.19 us
  transfers between devices with their start and end apart: 28, of which 21 were waited for; matrix products, arithmetic and copies ran while one was open for 1% of the time, Pallas kernels for 4%

profile of v5, /device:TPU:0, one launch (start us, length us, event | category | flops | bytes accessed | tf_op | source)
XLA Modules:
  0.0 70.6 jit_solution(15759469031600035105)
XLA Ops:
  2.2 3.0 %collective-permute-start = (f32[56,256]{1,0:T(8,128)S(1)}, f32[56,256]{1,0:T(8,128)S(1)}, u32[]{:S(2)}, u32[]{:S(2)}) collective-permute-start(f32[56,256]{1,0:T(8,128)S(1)} %prepare.1.refs_4_), channel_id=1, source_target_pairs={{0,1},{1,0},{2,3},{3,2},{4,5},{5,4},{6,7},{7,6},{8,9},{9,8},{10,11... | collective-permute-start | bytes 172040 | tf_op jit(solution)/shard_map/ppermute | solution.py:319
  6.1 1.2 %collective-permute-done.refs_5_ = f32[56,256]{1,0:T(8,128)S(1)} collective-permute-done((f32[56,256]{1,0:T(8,128)S(1)}, f32[56,256]{1,0:T(8,128)S(1)}, u32[]{:S(2)}, u32[]{:S(2)}) %collective-permute-start) | collective-permute-done | bytes 57376 | tf_op jit(solution)/shard_map/ppermute | solution.py:319
  7.4 4.2 %collective-permute-start.3 = (f32[72,256]{1,0:T(8,128)S(1)}, f32[72,256]{1,0:T(8,128)S(1)}, u32[]{:S(2)}, u32[]{:S(2)}) collective-permute-start(f32[72,256]{1,0:T(8,128)S(1)} %pad_maximum_fusion.refs_3_.refs_0_), channel_id=1, source_target_pairs={{0,6},{1,7},{2,4},{3,5},{4,2},{5,3},{6,0},{7,1},{8,14},{9,15},{10,... | collective-permute-start | bytes 221192 | tf_op jit(solution)/shard_map/ppermute | solution.py:319
  12.2 2.2 %copy-done = f32[32,256,128]{2,1,0:T(8,128)S(1)} copy-done((f32[32,256,128]{2,1,0:T(8,128)S(1)}, f32[32,256,128]{2,1,0:T(8,128)}, u32[]{:S(2)}) %copy-start) | copy-done | bytes 4194328
  14.7 2.5 %collective-permute-done.2.refs_1_.refs_2_ = f32[72,256]{1,0:T(8,128)S(1)} collective-permute-done((f32[72,256]{1,0:T(8,128)S(1)}, f32[72,256]{1,0:T(8,128)S(1)}, u32[]{:S(2)}, u32[]{:S(2)}) %collective-permute-start.2) | collective-permute-done | bytes 73760 | tf_op jit(solution)/shard_map/ppermute | solution.py:319
  22.4 1.6 %collective-permute-start.7 = (f32[32,256]{1,0:T(8,128)S(1)}, f32[32,256]{1,0:T(8,128)S(1)}, u32[]{:S(2)}, u32[]{:S(2)}) collective-permute-start(f32[32,256]{1,0:T(8,128)S(1)} %get-tuple-element.51.terms_ref), channel_id=1, source_target_pairs={{0,1},{1,0},{2,3},{3,2},{4,5},{5,4},{6,7},{7,6},{8,9},{9,8},{10,11... | collective-permute-start | bytes 98312 | tf_op jit(solution)/shard_map/ppermute | solution.py:319
  24.4 2.0 %collective-permute-done.7.refs_0_ = f32[32,256]{1,0:T(8,128)S(1)} collective-permute-done((f32[32,256]{1,0:T(8,128)S(1)}, f32[32,256]{1,0:T(8,128)S(1)}, u32[]{:S(2)}, u32[]{:S(2)}) %collective-permute-start.7) | collective-permute-done | bytes 32800 | tf_op jit(solution)/shard_map/ppermute | solution.py:319
  26.6 1.3 %collective-permute-start.8 = (f32[48,256]{1,0:T(8,128)S(1)}, f32[48,256]{1,0:T(8,128)S(1)}, u32[]{:S(2)}, u32[]{:S(2)}) collective-permute-start(f32[48,256]{1,0:T(8,128)S(1)} %get-tuple-element.54), channel_id=1, source_target_pairs={{0,4},{1,5},{2,6},{3,7},{4,0},{5,1},{6,2},{7,3},{8,12},{9,13},{10,... | collective-permute-start | bytes 147464 | tf_op jit(solution)/shard_map/ppermute | solution.py:430
  30.3 1.9 %collective-permute-done.8.refs_0_ = f32[48,256]{1,0:T(8,128)S(1)} collective-permute-done((f32[48,256]{1,0:T(8,128)S(1)}, f32[48,256]{1,0:T(8,128)S(1)}, u32[]{:S(2)}, u32[]{:S(2)}) %collective-permute-start.8) | collective-permute-done | bytes 49184 | tf_op jit(solution)/shard_map/ppermute | solution.py:430
  32.1 1.6 %collective-permute-done.9.refs_1_ = f32[48,256]{1,0:T(8,128)S(1)} collective-permute-done((f32[48,256]{1,0:T(8,128)S(1)}, f32[48,256]{1,0:T(8,128)S(1)}, u32[]{:S(2)}, u32[]{:S(2)}) %collective-permute-start.9) | collective-permute-done | bytes 49184 | tf_op jit(solution)/shard_map/ppermute | solution.py:430
  34.2 1.5 %collective-permute-start.12 = (f32[3,128]{1,0:T(4,128)S(1)}, f32[3,128]{1,0:T(4,128)S(1)}, u32[]{:S(2)}, u32[]{:S(2)}) collective-permute-start(f32[3,128]{1,0:T(4,128)S(1)} %get-tuple-element.59), channel_id=1, source_target_pairs={{0,16},{8,24},{16,0},{24,8},{1,17},{9,25},{17,1},{25,9},{2,18},{10... | collective-permute-start | bytes 4616 | tf_op jit(solution)/shard_map/ppermute | solution.py:325
  36.1 1.1 %collective-permute-done.13.refs_2_ = f32[3,128]{1,0:T(4,128)S(1)} collective-permute-done((f32[3,128]{1,0:T(4,128)S(1)}, f32[3,128]{1,0:T(4,128)S(1)}, u32[]{:S(2)}, u32[]{:S(2)}) %collective-permute-start.13) | collective-permute-done | bytes 1568 | tf_op jit(solution)/shard_map/ppermute | solution.py:325
  38.3 1.6 %collective-permute-start.14 = (f32[32,256]{1,0:T(8,128)S(1)}, f32[32,256]{1,0:T(8,128)S(1)}, u32[]{:S(2)}, u32[]{:S(2)}) collective-permute-start(f32[32,256]{1,0:T(8,128)S(1)} %get-tuple-element.63.terms_ref), channel_id=1, source_target_pairs={{0,1},{1,0},{2,3},{3,2},{4,5},{5,4},{6,7},{7,6},{8,9},{9,8},{10,11... | collective-permute-start | bytes 98312 | tf_op jit(solution)/shard_map/ppermute | solution.py:319
  40.1 2.2 %collective-permute-done.14.refs_0_ = f32[32,256]{1,0:T(8,128)S(1)} collective-permute-done((f32[32,256]{1,0:T(8,128)S(1)}, f32[32,256]{1,0:T(8,128)S(1)}, u32[]{:S(2)}, u32[]{:S(2)}) %collective-permute-start.14) | collective-permute-done | bytes 32800 | tf_op jit(solution)/shard_map/ppermute | solution.py:319
  43.6 1.7 %collective-permute-start.16 = (f32[48,256]{1,0:T(8,128)S(1)}, f32[48,256]{1,0:T(8,128)S(1)}, u32[]{:S(2)}, u32[]{:S(2)}) collective-permute-start(f32[48,256]{1,0:T(8,128)S(1)} %get-tuple-element.65), channel_id=1, source_target_pairs={{0,6},{1,7},{2,4},{3,5},{4,2},{5,3},{6,0},{7,1},{8,14},{9,15},{10,... | collective-permute-start | bytes 147464 | tf_op jit(solution)/shard_map/ppermute | solution.py:430
  46.0 2.4 %collective-permute-done.15.refs_0_ = f32[48,256]{1,0:T(8,128)S(1)} collective-permute-done((f32[48,256]{1,0:T(8,128)S(1)}, f32[48,256]{1,0:T(8,128)S(1)}, u32[]{:S(2)}, u32[]{:S(2)}) %collective-permute-start.15) | collective-permute-done | bytes 49184 | tf_op jit(solution)/shard_map/ppermute | solution.py:430
  48.5 1.2 %collective-permute-done.16.refs_1_ = f32[48,256]{1,0:T(8,128)S(1)} collective-permute-done((f32[48,256]{1,0:T(8,128)S(1)}, f32[48,256]{1,0:T(8,128)S(1)}, u32[]{:S(2)}, u32[]{:S(2)}) %collective-permute-start.16) | collective-permute-done | bytes 49184 | tf_op jit(solution)/shard_map/ppermute | solution.py:430
  52.3 1.1 %collective-permute-done.20.refs_2_ = f32[3,128]{1,0:T(4,128)S(1)} collective-permute-done((f32[3,128]{1,0:T(4,128)S(1)}, f32[3,128]{1,0:T(4,128)S(1)}, u32[]{:S(2)}, u32[]{:S(2)}) %collective-permute-start.20) | collective-permute-done | bytes 1568 | tf_op jit(solution)/shard_map/ppermute | solution.py:325
  54.5 1.6 %collective-permute-start.21 = (f32[32,256]{1,0:T(8,128)S(1)}, f32[32,256]{1,0:T(8,128)S(1)}, u32[]{:S(2)}, u32[]{:S(2)}) collective-permute-start(f32[32,256]{1,0:T(8,128)S(1)} %get-tuple-element.72.terms_ref), channel_id=1, source_target_pairs={{0,1},{1,0},{2,3},{3,2},{4,5},{5,4},{6,7},{7,6},{8,9},{9,8},{10,11... | collective-permute-start | bytes 98312 | tf_op jit(solution)/shard_map/ppermute | solution.py:319
  56.3 2.2 %collective-permute-done.21.refs_0_ = f32[32,256]{1,0:T(8,128)S(1)} collective-permute-done((f32[32,256]{1,0:T(8,128)S(1)}, f32[32,256]{1,0:T(8,128)S(1)}, u32[]{:S(2)}, u32[]{:S(2)}) %collective-permute-start.21) | collective-permute-done | bytes 32800 | tf_op jit(solution)/shard_map/ppermute | solution.py:319
  59.4 1.8 %collective-permute-start.23 = (f32[48,256]{1,0:T(8,128)S(1)}, f32[48,256]{1,0:T(8,128)S(1)}, u32[]{:S(2)}, u32[]{:S(2)}) collective-permute-start(f32[48,256]{1,0:T(8,128)S(1)} %get-tuple-element.74), channel_id=1, source_target_pairs={{0,6},{1,7},{2,4},{3,5},{4,2},{5,3},{6,0},{7,1},{8,14},{9,15},{10,... | collective-permute-start | bytes 147464 | tf_op jit(solution)/shard_map/ppermute | solution.py:430
  62.2 2.1 %collective-permute-done.22.refs_0_ = f32[48,256]{1,0:T(8,128)S(1)} collective-permute-done((f32[48,256]{1,0:T(8,128)S(1)}, f32[48,256]{1,0:T(8,128)S(1)}, u32[]{:S(2)}, u32[]{:S(2)}) %collective-permute-start.22) | collective-permute-done | bytes 49184 | tf_op jit(solution)/shard_map/ppermute | solution.py:430
  64.3 1.2 %collective-permute-done.23.refs_1_ = f32[48,256]{1,0:T(8,128)S(1)} collective-permute-done((f32[48,256]{1,0:T(8,128)S(1)}, f32[48,256]{1,0:T(8,128)S(1)}, u32[]{:S(2)}, u32[]{:S(2)}) %collective-permute-start.23) | collective-permute-done | bytes 49184 | tf_op jit(solution)/shard_map/ppermute | solution.py:430
  66.4 1.5 %collective-permute-start.26 = (f32[3,128]{1,0:T(4,128)S(1)}, f32[3,128]{1,0:T(4,128)S(1)}, u32[]{:S(2)}, u32[]{:S(2)}) collective-permute-start(f32[3,128]{1,0:T(4,128)S(1)} %get-tuple-element.79), channel_id=1, source_target_pairs={{0,16},{8,24},{16,0},{24,8},{1,17},{9,25},{17,1},{25,9},{2,18},{10... | collective-permute-start | bytes 4616 | tf_op jit(solution)/shard_map/ppermute | solution.py:325
  (64 shorter events, 24.3 us)
Async XLA Ops:
  2.2 5.2 %collective-permute-start = (f32[56,256]{1,0:T(8,128)S(1)}, f32[56,256]{1,0:T(8,128)S(1)}, u32[]{:S(2)}, u32[]{:S(2)}) collective-permute-start(f32[56,256]{1,0:T(8,128)S(1)} %prepare.1.refs_4_), channel_id=1, source_target_pairs={{0,1},{1,0},{2,3},{3,2},{4,5},{5,4},{6,7},{7,6},{8,9},{9,8},{10,11... | collective-permute-start | bytes 172040 | tf_op jit(solution)/shard_map/ppermute | solution.py:319
  7.4 7.3 %collective-permute-start.3 = (f32[72,256]{1,0:T(8,128)S(1)}, f32[72,256]{1,0:T(8,128)S(1)}, u32[]{:S(2)}, u32[]{:S(2)}) collective-permute-start(f32[72,256]{1,0:T(8,128)S(1)} %pad_maximum_fusion.refs_3_.refs_0_), channel_id=1, source_target_pairs={{0,6},{1,7},{2,4},{3,5},{4,2},{5,3},{6,0},{7,1},{8,14},{9,15},{10,... | collective-permute-start | bytes 221192 | tf_op jit(solution)/shard_map/ppermute | solution.py:319
  11.6 5.6 %collective-permute-start.2 = (f32[72,256]{1,0:T(8,128)S(1)}, f32[72,256]{1,0:T(8,128)S(1)}, u32[]{:S(2)}, u32[]{:S(2)}) collective-permute-start(f32[72,256]{1,0:T(8,128)S(1)} %pad_maximum_fusion.refs_3_.refs_0_), channel_id=1, source_target_pairs={{0,4},{1,5},{2,6},{3,7},{4,0},{5,1},{6,2},{7,3},{8,12},{9,13},{10,... | collective-permute-start | bytes 221192 | tf_op jit(solution)/shard_map/ppermute | solution.py:319
  11.6 5.6 %collective-permute-start.1 = (f32[72,256]{1,0:T(8,128)S(1)}, f32[72,256]{1,0:T(8,128)S(1)}, u32[]{:S(2)}, u32[]{:S(2)}) collective-permute-start(f32[72,256]{1,0:T(8,128)S(1)} %pad_maximum_fusion.refs_3_.refs_0_), channel_id=1, source_target_pairs={{0,2},{1,3},{2,0},{3,1},{4,6},{5,7},{6,4},{7,5},{8,10},{9,11},{10,... | collective-permute-start | bytes 221192 | tf_op jit(solution)/shard_map/ppermute | solution.py:319
  17.8 3.2 %collective-permute-start.6 = (f32[9,128]{1,0:T(8,128)S(1)}, f32[9,128]{1,0:T(8,128)S(1)}, u32[]{:S(2)}, u32[]{:S(2)}) collective-permute-start(f32[9,128]{1,0:T(8,128)S(1)} %get-tuple-element.47), channel_id=1, source_target_pairs={{0,24},{8,16},{16,8},{24,0},{1,25},{9,17},{17,9},{25,1},{2,26},{10... | collective-permute-start | bytes 13832 | tf_op jit(solution)/shard_map/ppermute | solution.py:325
  18.3 3.7 %collective-permute-start.5 = (f32[9,128]{1,0:T(8,128)S(1)}, f32[9,128]{1,0:T(8,128)S(1)}, u32[]{:S(2)}, u32[]{:S(2)}) collective-permute-start(f32[9,128]{1,0:T(8,128)S(1)} %get-tuple-element.47), channel_id=1, source_target_pairs={{0,16},{8,24},{16,0},{24,8},{1,17},{9,25},{17,1},{25,9},{2,18},{10... | collective-permute-start | bytes 13832 | tf_op jit(solution)/shard_map/ppermute | solution.py:325
  22.4 4.0 %collective-permute-start.7 = (f32[32,256]{1,0:T(8,128)S(1)}, f32[32,256]{1,0:T(8,128)S(1)}, u32[]{:S(2)}, u32[]{:S(2)}) collective-permute-start(f32[32,256]{1,0:T(8,128)S(1)} %get-tuple-element.51.terms_ref), channel_id=1, source_target_pairs={{0,1},{1,0},{2,3},{3,2},{4,5},{5,4},{6,7},{7,6},{8,9},{9,8},{10,11... | collective-permute-start | bytes 98312 | tf_op jit(solution)/shard_map/ppermute | solution.py:319
  26.6 5.6 %collective-permute-start.8 = (f32[48,256]{1,0:T(8,128)S(1)}, f32[48,256]{1,0:T(8,128)S(1)}, u32[]{:S(2)}, u32[]{:S(2)}) collective-permute-start(f32[48,256]{1,0:T(8,128)S(1)} %get-tuple-element.54), channel_id=1, source_target_pairs={{0,4},{1,5},{2,6},{3,7},{4,0},{5,1},{6,2},{7,3},{8,12},{9,13},{10,... | collective-permute-start | bytes 147464 | tf_op jit(solution)/shard_map/ppermute | solution.py:430
  27.9 5.9 %collective-permute-start.9 = (f32[48,256]{1,0:T(8,128)S(1)}, f32[48,256]{1,0:T(8,128)S(1)}, u32[]{:S(2)}, u32[]{:S(2)}) collective-permute-start(f32[48,256]{1,0:T(8,128)S(1)} %get-tuple-element.55), channel_id=1, source_target_pairs={{0,6},{1,7},{2,4},{3,5},{4,2},{5,3},{6,0},{7,1},{8,14},{9,15},{10,... | collective-permute-start | bytes 147464 | tf_op jit(solution)/shard_map/ppermute | solution.py:430
  29.0 4.7 %collective-permute-start.10 = (f32[48,256]{1,0:T(8,128)S(1)}, f32[48,256]{1,0:T(8,128)S(1)}, u32[]{:S(2)}, u32[]{:S(2)}) collective-permute-start(f32[48,256]{1,0:T(8,128)S(1)} %get-tuple-element.56), channel_id=1, source_target_pairs={{0,2},{1,3},{2,0},{3,1},{4,6},{5,7},{6,4},{7,5},{8,10},{9,11},{10,... | collective-permute-start | bytes 147464 | tf_op jit(solution)/shard_map/ppermute | solution.py:430
  34.2 3.1 %collective-permute-start.13 = (f32[3,128]{1,0:T(4,128)S(1)}, f32[3,128]{1,0:T(4,128)S(1)}, u32[]{:S(2)}, u32[]{:S(2)}) collective-permute-start(f32[3,128]{1,0:T(4,128)S(1)} %get-tuple-element.59), channel_id=1, source_target_pairs={{0,24},{8,16},{16,8},{24,0},{1,25},{9,17},{17,9},{25,1},{2,26},{10... | collective-permute-start | bytes 4616 | tf_op jit(solution)/shard_map/ppermute | solution.py:325
  34.2 3.7 %collective-permute-start.12 = (f32[3,128]{1,0:T(4,128)S(1)}, f32[3,128]{1,0:T(4,128)S(1)}, u32[]{:S(2)}, u32[]{:S(2)}) collective-permute-start(f32[3,128]{1,0:T(4,128)S(1)} %get-tuple-element.59), channel_id=1, source_target_pairs={{0,16},{8,24},{16,0},{24,8},{1,17},{9,25},{17,1},{25,9},{2,18},{10... | collective-permute-start | bytes 4616 | tf_op jit(solution)/shard_map/ppermute | solution.py:325
  38.3 4.0 %collective-permute-start.14 = (f32[32,256]{1,0:T(8,128)S(1)}, f32[32,256]{1,0:T(8,128)S(1)}, u32[]{:S(2)}, u32[]{:S(2)}) collective-permute-start(f32[32,256]{1,0:T(8,128)S(1)} %get-tuple-element.63.terms_ref), channel_id=1, source_target_pairs={{0,1},{1,0},{2,3},{3,2},{4,5},{5,4},{6,7},{7,6},{8,9},{9,8},{10,11... | collective-permute-start | bytes 98312 | tf_op jit(solution)/shard_map/ppermute | solution.py:319
  42.5 6.0 %collective-permute-start.15 = (f32[48,256]{1,0:T(8,128)S(1)}, f32[48,256]{1,0:T(8,128)S(1)}, u32[]{:S(2)}, u32[]{:S(2)}) collective-permute-start(f32[48,256]{1,0:T(8,128)S(1)} %get-tuple-element.64), channel_id=1, source_target_pairs={{0,4},{1,5},{2,6},{3,7},{4,0},{5,1},{6,2},{7,3},{8,12},{9,13},{10,... | collective-permute-start | bytes 147464 | tf_op jit(solution)/shard_map/ppermute | solution.py:430
  43.6 6.0 %collective-permute-start.16 = (f32[48,256]{1,0:T(8,128)S(1)}, f32[48,256]{1,0:T(8,128)S(1)}, u32[]{:S(2)}, u32[]{:S(2)}) collective-permute-start(f32[48,256]{1,0:T(8,128)S(1)} %get-tuple-element.65), channel_id=1, source_target_pairs={{0,6},{1,7},{2,4},{3,5},{4,2},{5,3},{6,0},{7,1},{8,14},{9,15},{10,... | collective-permute-start | bytes 147464 | tf_op jit(solution)/shard_map/ppermute | solution.py:430
  45.3 4.6 %collective-permute-start.17 = (f32[48,256]{1,0:T(8,128)S(1)}, f32[48,256]{1,0:T(8,128)S(1)}, u32[]{:S(2)}, u32[]{:S(2)}) collective-permute-start(f32[48,256]{1,0:T(8,128)S(1)} %get-tuple-element.66), channel_id=1, source_target_pairs={{0,2},{1,3},{2,0},{3,1},{4,6},{5,7},{6,4},{7,5},{8,10},{9,11},{10,... | collective-permute-start | bytes 147464 | tf_op jit(solution)/shard_map/ppermute | solution.py:430
  50.4 3.1 %collective-permute-start.20 = (f32[3,128]{1,0:T(4,128)S(1)}, f32[3,128]{1,0:T(4,128)S(1)}, u32[]{:S(2)}, u32[]{:S(2)}) collective-permute-start(f32[3,128]{1,0:T(4,128)S(1)} %get-tuple-element.69), channel_id=1, source_target_pairs={{0,24},{8,16},{16,8},{24,0},{1,25},{9,17},{17,9},{25,1},{2,26},{10... | collective-permute-start | bytes 4616 | tf_op jit(solution)/shard_map/ppermute | solution.py:325
  50.4 3.7 %collective-permute-start.19 = (f32[3,128]{1,0:T(4,128)S(1)}, f32[3,128]{1,0:T(4,128)S(1)}, u32[]{:S(2)}, u32[]{:S(2)}) collective-permute-start(f32[3,128]{1,0:T(4,128)S(1)} %get-tuple-element.69), channel_id=1, source_target_pairs={{0,16},{8,24},{16,0},{24,8},{1,17},{9,25},{17,1},{25,9},{2,18},{10... | collective-permute-start | bytes 4616 | tf_op jit(solution)/shard_map/ppermute | solution.py:325
  54.5 4.0 %collective-permute-start.21 = (f32[32,256]{1,0:T(8,128)S(1)}, f32[32,256]{1,0:T(8,128)S(1)}, u32[]{:S(2)}, u32[]{:S(2)}) collective-permute-start(f32[32,256]{1,0:T(8,128)S(1)} %get-tuple-element.72.terms_ref), channel_id=1, source_target_pairs={{0,1},{1,0},{2,3},{3,2},{4,5},{5,4},{6,7},{7,6},{8,9},{9,8},{10,11... | collective-permute-start | bytes 98312 | tf_op jit(solution)/shard_map/ppermute | solution.py:319
  58.7 5.7 %collective-permute-start.22 = (f32[48,256]{1,0:T(8,128)S(1)}, f32[48,256]{1,0:T(8,128)S(1)}, u32[]{:S(2)}, u32[]{:S(2)}) collective-permute-start(f32[48,256]{1,0:T(8,128)S(1)} %get-tuple-element.73), channel_id=1, source_target_pairs={{0,4},{1,5},{2,6},{3,7},{4,0},{5,1},{6,2},{7,3},{8,12},{9,13},{10,... | collective-permute-start | bytes 147464 | tf_op jit(solution)/shard_map/ppermute | solution.py:430
  59.4 6.1 %collective-permute-start.23 = (f32[48,256]{1,0:T(8,128)S(1)}, f32[48,256]{1,0:T(8,128)S(1)}, u32[]{:S(2)}, u32[]{:S(2)}) collective-permute-start(f32[48,256]{1,0:T(8,128)S(1)} %get-tuple-element.74), channel_id=1, source_target_pairs={{0,6},{1,7},{2,4},{3,5},{4,2},{5,3},{6,0},{7,1},{8,14},{9,15},{10,... | collective-permute-start | bytes 147464 | tf_op jit(solution)/shard_map/ppermute | solution.py:430
  61.3 4.6 %collective-permute-start.24 = (f32[48,256]{1,0:T(8,128)S(1)}, f32[48,256]{1,0:T(8,128)S(1)}, u32[]{:S(2)}, u32[]{:S(2)}) collective-permute-start(f32[48,256]{1,0:T(8,128)S(1)} %get-tuple-element.75), channel_id=1, source_target_pairs={{0,2},{1,3},{2,0},{3,1},{4,6},{5,7},{6,4},{7,5},{8,10},{9,11},{10,... | collective-permute-start | bytes 147464 | tf_op jit(solution)/shard_map/ppermute | solution.py:430
  66.3 3.1 %collective-permute-start.27 = (f32[3,128]{1,0:T(4,128)S(1)}, f32[3,128]{1,0:T(4,128)S(1)}, u32[]{:S(2)}, u32[]{:S(2)}) collective-permute-start(f32[3,128]{1,0:T(4,128)S(1)} %get-tuple-element.79), channel_id=1, source_target_pairs={{0,24},{8,16},{16,8},{24,0},{1,25},{9,17},{17,9},{25,1},{2,26},{10... | collective-permute-start | bytes 4616 | tf_op jit(solution)/shard_map/ppermute | solution.py:325
  66.4 3.7 %collective-permute-start.26 = (f32[3,128]{1,0:T(4,128)S(1)}, f32[3,128]{1,0:T(4,128)S(1)}, u32[]{:S(2)}, u32[]{:S(2)}) collective-permute-start(f32[3,128]{1,0:T(4,128)S(1)} %get-tuple-element.79), channel_id=1, source_target_pairs={{0,16},{8,24},{16,0},{24,8},{1,17},{9,25},{17,1},{25,9},{2,18},{10... | collective-permute-start | bytes 4616 | tf_op jit(solution)/shard_map/ppermute | solution.py:325
  (7 other events, 31.2 us)

commit v6 on v5

--- a/solution.py
+++ b/solution.py
@@ -176,11 +176,12 @@
     out_ref[...] = pick_thrice(own_ref[...], rows)
 
 
-def sum_kernel(pieces, skip, *refs):
+def sum_kernel(pieces, skip, first, *refs):
     ins, (others_ref, part_ref), outs = refs[:pieces], refs[pieces : pieces + 2], refs[pieces + 2 :]
     terms = jnp.concatenate([ref[...] for ref in ins], axis=0)[skip:]
-    total = part_ref[...] + pick_thrice(others_ref[...], terms)
     rows = outs[0].shape[0]
+    place = slice(first * rows, (first + len(outs)) * rows)
+    total = part_ref[place] + pick_thrice(others_ref[place], terms)
     for k, out in enumerate(outs):
         out[...] = total[k * rows : (k + 1) * rows]
 
@@ -423,12 +424,16 @@
         else:
             skip = incs
         sums = kernel_call(
-            lambda *refs: sum_kernel(len(near), skip, *refs), "sums", [(rows, width)] * far_count,
-            [*near, other_same, part],
+            lambda *refs: sum_kernel(len(near), skip, 1, *refs), "sums",
+            [(rows, width)] * (far_count - 1), [*near, other_same, part],
         )
-        far = [sums[0]] + [
+        (mine,) = kernel_call(
+            lambda *refs: sum_kernel(len(near), skip, 0, *refs), "own_rows",
+            [(rows, width)], [*near, other_same, tied(part, sums[0])],
+        )
+        far = [mine] + [
             lax.ppermute(x, "shard", [(i, i ^ (k * stride)) for i in range(devices)])
-            for k, x in enumerate(sums) if k > 0
+            for k, x in enumerate(sums, 1)
         ]
         flows, load, out = kernel_call(
             lambda *refs: flow_kernel(len(far), step_size, *refs), "flows", load_shapes,

time: 70.9 us -> 70.9 us (level)
    pallas_call x19 -> x22, Pallas kernels: 7.34 us -> 7.72 us  [kernel_call(): pl.pallas_call(kernel, out_shape=shapes, in_specs=[pl.BlockSpec(memory_sp...]
where the time goes in v6:
time: 70.9 us; the launch traced here: 70.6 us
  starting transfers between devices  31 us (44%)
  waiting for transfers between devices  27.4 us (39%)
  Pallas kernels  7.97 us (11%)
  local copies, waits for them, and re-layouts  2.81 us (4%)
  between operations  1.45 us (2%)
    ppermute x7, starting transfers between devices, share(): pieces.append(lax.ppermute(given, 'shard', pairs))  12.6 us
    ppermute x9, starting transfers between devices, body(): lax.ppermute(x, 'shard', [(i, i ^ k * stride) for i in range(devices)])  10.7 us
    ppermute x9, waiting for transfers between devices, body(): lax.ppermute(x, 'shard', [(i, i ^ k * stride) for i in range(devices)])  10.6 us
    ppermute x7, waiting for transfers between devices, share(): pieces.append(lax.ppermute(given, 'shard', pairs))  10.2 us
    pallas_call x22, Pallas kernels, kernel_call(): pl.pallas_call(kernel, out_shape=shapes, in_specs=[pl.BlockSpec(memory_sp...  7.72 us
    ppermute x12, starting transfers between devices, trade(): lax.ppermute(x, 'cluster', [(i, i ^ k) for i in range(clusters)])  7.68 us
    ppermute x12, waiting for transfers between devices, trade(): lax.ppermute(x, 'cluster', [(i, i ^ k) for i in range(clusters)])  6.52 us
    unnamed x6, local copies, waits for them, and re-layouts  2.19 us
  transfers between devices with their start and end apart: 28, of which 21 were waited for; matrix products, arithmetic and copies ran while one was open for 1% of the time, Pallas kernels for 4%

profile of v6, /device:TPU:0, one launch (start us, length us, event | category | flops | bytes accessed | tf_op | source)
XLA Modules:
  0.0 70.6 jit_solution(8721587101048141211)
XLA Ops:
  2.2 3.0 %collective-permute-start = (f32[56,256]{1,0:T(8,128)S(1)}, f32[56,256]{1,0:T(8,128)S(1)}, u32[]{:S(2)}, u32[]{:S(2)}) collective-permute-start(f32[56,256]{1,0:T(8,128)S(1)} %prepare.1.refs_4_), channel_id=1, source_target_pairs={{0,1},{1,0},{2,3},{3,2},{4,5},{5,4},{6,7},{7,6},{8,9},{9,8},{10,11... | collective-permute-start | bytes 172040 | tf_op jit(solution)/shard_map/ppermute | solution.py:320
  6.1 1.2 %collective-permute-done.refs_5_ = f32[56,256]{1,0:T(8,128)S(1)} collective-permute-done((f32[56,256]{1,0:T(8,128)S(1)}, f32[56,256]{1,0:T(8,128)S(1)}, u32[]{:S(2)}, u32[]{:S(2)}) %collective-permute-start) | collective-permute-done | bytes 57376 | tf_op jit(solution)/shard_map/ppermute | solution.py:320
  7.4 4.2 %collective-permute-start.3 = (f32[72,256]{1,0:T(8,128)S(1)}, f32[72,256]{1,0:T(8,128)S(1)}, u32[]{:S(2)}, u32[]{:S(2)}) collective-permute-start(f32[72,256]{1,0:T(8,128)S(1)} %pad_maximum_fusion.refs_3_.refs_0_), channel_id=1, source_target_pairs={{0,6},{1,7},{2,4},{3,5},{4,2},{5,3},{6,0},{7,1},{8,14},{9,15},{10,... | collective-permute-start | bytes 221192 | tf_op jit(solution)/shard_map/ppermute | solution.py:320
  12.2 2.2 %copy-done = f32[32,256,128]{2,1,0:T(8,128)S(1)} copy-done((f32[32,256,128]{2,1,0:T(8,128)S(1)}, f32[32,256,128]{2,1,0:T(8,128)}, u32[]{:S(2)}) %copy-start) | copy-done | bytes 4194328
  14.7 2.5 %collective-permute-done.2.refs_1_.refs_2_ = f32[72,256]{1,0:T(8,128)S(1)} collective-permute-done((f32[72,256]{1,0:T(8,128)S(1)}, f32[72,256]{1,0:T(8,128)S(1)}, u32[]{:S(2)}, u32[]{:S(2)}) %collective-permute-start.2) | collective-permute-done | bytes 73760 | tf_op jit(solution)/shard_map/ppermute | solution.py:320
  22.4 1.6 %collective-permute-start.7 = (f32[32,256]{1,0:T(8,128)S(1)}, f32[32,256]{1,0:T(8,128)S(1)}, u32[]{:S(2)}, u32[]{:S(2)}) collective-permute-start(f32[32,256]{1,0:T(8,128)S(1)} %get-tuple-element.51.terms_ref), channel_id=1, source_target_pairs={{0,1},{1,0},{2,3},{3,2},{4,5},{5,4},{6,7},{7,6},{8,9},{9,8},{10,11... | collective-permute-start | bytes 98312 | tf_op jit(solution)/shard_map/ppermute | solution.py:320
  24.4 2.0 %collective-permute-done.7.refs_0_ = f32[32,256]{1,0:T(8,128)S(1)} collective-permute-done((f32[32,256]{1,0:T(8,128)S(1)}, f32[32,256]{1,0:T(8,128)S(1)}, u32[]{:S(2)}, u32[]{:S(2)}) %collective-permute-start.7) | collective-permute-done | bytes 32800 | tf_op jit(solution)/shard_map/ppermute | solution.py:320
  26.6 1.3 %collective-permute-start.8 = (f32[48,256]{1,0:T(8,128)S(1)}, f32[48,256]{1,0:T(8,128)S(1)}, u32[]{:S(2)}, u32[]{:S(2)}) collective-permute-start(f32[48,256]{1,0:T(8,128)S(1)} %get-tuple-element.54), channel_id=1, source_target_pairs={{0,4},{1,5},{2,6},{3,7},{4,0},{5,1},{6,2},{7,3},{8,12},{9,13},{10,... | collective-permute-start | bytes 147464 | tf_op jit(solution)/shard_map/ppermute | solution.py:435
  30.4 1.7 %collective-permute-done.8.refs_0_ = f32[48,256]{1,0:T(8,128)S(1)} collective-permute-done((f32[48,256]{1,0:T(8,128)S(1)}, f32[48,256]{1,0:T(8,128)S(1)}, u32[]{:S(2)}, u32[]{:S(2)}) %collective-permute-start.8) | collective-permute-done | bytes 49184 | tf_op jit(solution)/shard_map/ppermute | solution.py:435
  32.1 1.6 %collective-permute-done.9.refs_1_ = f32[48,256]{1,0:T(8,128)S(1)} collective-permute-done((f32[48,256]{1,0:T(8,128)S(1)}, f32[48,256]{1,0:T(8,128)S(1)}, u32[]{:S(2)}, u32[]{:S(2)}) %collective-permute-start.9) | collective-permute-done | bytes 49184 | tf_op jit(solution)/shard_map/ppermute | solution.py:435
  34.2 1.5 %collective-permute-start.12 = (f32[3,128]{1,0:T(4,128)S(1)}, f32[3,128]{1,0:T(4,128)S(1)}, u32[]{:S(2)}, u32[]{:S(2)}) collective-permute-start(f32[3,128]{1,0:T(4,128)S(1)} %get-tuple-element.59), channel_id=1, source_target_pairs={{0,16},{8,24},{16,0},{24,8},{1,17},{9,25},{17,1},{25,9},{2,18},{10... | collective-permute-start | bytes 4616 | tf_op jit(solution)/shard_map/ppermute | solution.py:326
  36.1 1.1 %collective-permute-done.13.refs_2_ = f32[3,128]{1,0:T(4,128)S(1)} collective-permute-done((f32[3,128]{1,0:T(4,128)S(1)}, f32[3,128]{1,0:T(4,128)S(1)}, u32[]{:S(2)}, u32[]{:S(2)}) %collective-permute-start.13) | collective-permute-done | bytes 1568 | tf_op jit(solution)/shard_map/ppermute | solution.py:326
  38.3 1.6 %collective-permute-start.14 = (f32[32,256]{1,0:T(8,128)S(1)}, f32[32,256]{1,0:T(8,128)S(1)}, u32[]{:S(2)}, u32[]{:S(2)}) collective-permute-start(f32[32,256]{1,0:T(8,128)S(1)} %get-tuple-element.63.terms_ref), channel_id=1, source_target_pairs={{0,1},{1,0},{2,3},{3,2},{4,5},{5,4},{6,7},{7,6},{8,9},{9,8},{10,11... | collective-permute-start | bytes 98312 | tf_op jit(solution)/shard_map/ppermute | solution.py:320
  40.1 2.2 %collective-permute-done.14.refs_0_ = f32[32,256]{1,0:T(8,128)S(1)} collective-permute-done((f32[32,256]{1,0:T(8,128)S(1)}, f32[32,256]{1,0:T(8,128)S(1)}, u32[]{:S(2)}, u32[]{:S(2)}) %collective-permute-start.14) | collective-permute-done | bytes 32800 | tf_op jit(solution)/shard_map/ppermute | solution.py:320
  42.5 1.1 %collective-permute-start.15 = (f32[48,256]{1,0:T(8,128)S(1)}, f32[48,256]{1,0:T(8,128)S(1)}, u32[]{:S(2)}, u32[]{:S(2)}) collective-permute-start(f32[48,256]{1,0:T(8,128)S(1)} %get-tuple-element.64), channel_id=1, source_target_pairs={{0,4},{1,5},{2,6},{3,7},{4,0},{5,1},{6,2},{7,3},{8,12},{9,13},{10,... | collective-permute-start | bytes 147464 | tf_op jit(solution)/shard_map/ppermute | solution.py:435
  43.6 1.7 %collective-permute-start.16 = (f32[48,256]{1,0:T(8,128)S(1)}, f32[48,256]{1,0:T(8,128)S(1)}, u32[]{:S(2)}, u32[]{:S(2)}) collective-permute-start(f32[48,256]{1,0:T(8,128)S(1)} %get-tuple-element.65), channel_id=1, source_target_pairs={{0,6},{1,7},{2,4},{3,5},{4,2},{5,3},{6,0},{7,1},{8,14},{9,15},{10,... | collective-permute-start | bytes 147464 | tf_op jit(solution)/shard_map/ppermute | solution.py:435
  46.1 2.3 %collective-permute-done.15.refs_0_ = f32[48,256]{1,0:T(8,128)S(1)} collective-permute-done((f32[48,256]{1,0:T(8,128)S(1)}, f32[48,256]{1,0:T(8,128)S(1)}, u32[]{:S(2)}, u32[]{:S(2)}) %collective-permute-start.15) | collective-permute-done | bytes 49184 | tf_op jit(solution)/shard_map/ppermute | solution.py:435
  48.4 1.2 %collective-permute-done.16.refs_1_ = f32[48,256]{1,0:T(8,128)S(1)} collective-permute-done((f32[48,256]{1,0:T(8,128)S(1)}, f32[48,256]{1,0:T(8,128)S(1)}, u32[]{:S(2)}, u32[]{:S(2)}) %collective-permute-start.16) | collective-permute-done | bytes 49184 | tf_op jit(solution)/shard_map/ppermute | solution.py:435
  52.3 1.1 %collective-permute-done.20.refs_2_ = f32[3,128]{1,0:T(4,128)S(1)} collective-permute-done((f32[3,128]{1,0:T(4,128)S(1)}, f32[3,128]{1,0:T(4,128)S(1)}, u32[]{:S(2)}, u32[]{:S(2)}) %collective-permute-start.20) | collective-permute-done | bytes 1568 | tf_op jit(solution)/shard_map/ppermute | solution.py:326
  54.5 1.6 %collective-permute-start.21 = (f32[32,256]{1,0:T(8,128)S(1)}, f32[32,256]{1,0:T(8,128)S(1)}, u32[]{:S(2)}, u32[]{:S(2)}) collective-permute-start(f32[32,256]{1,0:T(8,128)S(1)} %get-tuple-element.72.terms_ref), channel_id=1, source_target_pairs={{0,1},{1,0},{2,3},{3,2},{4,5},{5,4},{6,7},{7,6},{8,9},{9,8},{10,11... | collective-permute-start | bytes 98312 | tf_op jit(solution)/shard_map/ppermute | solution.py:320
  56.3 2.2 %collective-permute-done.21.refs_0_ = f32[32,256]{1,0:T(8,128)S(1)} collective-permute-done((f32[32,256]{1,0:T(8,128)S(1)}, f32[32,256]{1,0:T(8,128)S(1)}, u32[]{:S(2)}, u32[]{:S(2)}) %collective-permute-start.21) | collective-permute-done | bytes 32800 | tf_op jit(solution)/shard_map/ppermute | solution.py:320
  59.4 1.8 %collective-permute-start.23 = (f32[48,256]{1,0:T(8,128)S(1)}, f32[48,256]{1,0:T(8,128)S(1)}, u32[]{:S(2)}, u32[]{:S(2)}) collective-permute-start(f32[48,256]{1,0:T(8,128)S(1)} %get-tuple-element.74), channel_id=1, source_target_pairs={{0,6},{1,7},{2,4},{3,5},{4,2},{5,3},{6,0},{7,1},{8,14},{9,15},{10,... | collective-permute-start | bytes 147464 | tf_op jit(solution)/shard_map/ppermute | solution.py:435
  62.3 2.0 %collective-permute-done.22.refs_0_ = f32[48,256]{1,0:T(8,128)S(1)} collective-permute-done((f32[48,256]{1,0:T(8,128)S(1)}, f32[48,256]{1,0:T(8,128)S(1)}, u32[]{:S(2)}, u32[]{:S(2)}) %collective-permute-start.22) | collective-permute-done | bytes 49184 | tf_op jit(solution)/shard_map/ppermute | solution.py:435
  66.3 1.5 %collective-permute-start.26 = (f32[3,128]{1,0:T(4,128)S(1)}, f32[3,128]{1,0:T(4,128)S(1)}, u32[]{:S(2)}, u32[]{:S(2)}) collective-permute-start(f32[3,128]{1,0:T(4,128)S(1)} %get-tuple-element.79), channel_id=1, source_target_pairs={{0,16},{8,24},{16,0},{24,8},{1,17},{9,25},{17,1},{25,9},{2,18},{10... | collective-permute-start | bytes 4616 | tf_op jit(solution)/shard_map/ppermute | solution.py:326
  (67 shorter events, 24.7 us)
Async XLA Ops:
  2.2 5.2 %collective-permute-start = (f32[56,256]{1,0:T(8,128)S(1)}, f32[56,256]{1,0:T(8,128)S(1)}, u32[]{:S(2)}, u32[]{:S(2)}) collective-permute-start(f32[56,256]{1,0:T(8,128)S(1)} %prepare.1.refs_4_), channel_id=1, source_target_pairs={{0,1},{1,0},{2,3},{3,2},{4,5},{5,4},{6,7},{7,6},{8,9},{9,8},{10,11... | collective-permute-start | bytes 172040 | tf_op jit(solution)/shard_map/ppermute | solution.py:320
  7.4 7.3 %collective-permute-start.3 = (f32[72,256]{1,0:T(8,128)S(1)}, f32[72,256]{1,0:T(8,128)S(1)}, u32[]{:S(2)}, u32[]{:S(2)}) collective-permute-start(f32[72,256]{1,0:T(8,128)S(1)} %pad_maximum_fusion.refs_3_.refs_0_), channel_id=1, source_target_pairs={{0,6},{1,7},{2,4},{3,5},{4,2},{5,3},{6,0},{7,1},{8,14},{9,15},{10,... | collective-permute-start | bytes 221192 | tf_op jit(solution)/shard_map/ppermute | solution.py:320
  11.6 5.6 %collective-permute-start.2 = (f32[72,256]{1,0:T(8,128)S(1)}, f32[72,256]{1,0:T(8,128)S(1)}, u32[]{:S(2)}, u32[]{:S(2)}) collective-permute-start(f32[72,256]{1,0:T(8,128)S(1)} %pad_maximum_fusion.refs_3_.refs_0_), channel_id=1, source_target_pairs={{0,4},{1,5},{2,6},{3,7},{4,0},{5,1},{6,2},{7,3},{8,12},{9,13},{10,... | collective-permute-start | bytes 221192 | tf_op jit(solution)/shard_map/ppermute | solution.py:320
  11.6 5.6 %collective-permute-start.1 = (f32[72,256]{1,0:T(8,128)S(1)}, f32[72,256]{1,0:T(8,128)S(1)}, u32[]{:S(2)}, u32[]{:S(2)}) collective-permute-start(f32[72,256]{1,0:T(8,128)S(1)} %pad_maximum_fusion.refs_3_.refs_0_), channel_id=1, source_target_pairs={{0,2},{1,3},{2,0},{3,1},{4,6},{5,7},{6,4},{7,5},{8,10},{9,11},{10,... | collective-permute-start | bytes 221192 | tf_op jit(solution)/shard_map/ppermute | solution.py:320
  17.8 3.2 %collective-permute-start.6 = (f32[9,128]{1,0:T(8,128)S(1)}, f32[9,128]{1,0:T(8,128)S(1)}, u32[]{:S(2)}, u32[]{:S(2)}) collective-permute-start(f32[9,128]{1,0:T(8,128)S(1)} %get-tuple-element.47), channel_id=1, source_target_pairs={{0,24},{8,16},{16,8},{24,0},{1,25},{9,17},{17,9},{25,1},{2,26},{10... | collective-permute-start | bytes 13832 | tf_op jit(solution)/shard_map/ppermute | solution.py:326
  18.3 3.7 %collective-permute-start.5 = (f32[9,128]{1,0:T(8,128)S(1)}, f32[9,128]{1,0:T(8,128)S(1)}, u32[]{:S(2)}, u32[]{:S(2)}) collective-permute-start(f32[9,128]{1,0:T(8,128)S(1)} %get-tuple-element.47), channel_id=1, source_target_pairs={{0,16},{8,24},{16,0},{24,8},{1,17},{9,25},{17,1},{25,9},{2,18},{10... | collective-permute-start | bytes 13832 | tf_op jit(solution)/shard_map/ppermute | solution.py:326
  22.4 4.0 %collective-permute-start.7 = (f32[32,256]{1,0:T(8,128)S(1)}, f32[32,256]{1,0:T(8,128)S(1)}, u32[]{:S(2)}, u32[]{:S(2)}) collective-permute-start(f32[32,256]{1,0:T(8,128)S(1)} %get-tuple-element.51.terms_ref), channel_id=1, source_target_pairs={{0,1},{1,0},{2,3},{3,2},{4,5},{5,4},{6,7},{7,6},{8,9},{9,8},{10,11... | collective-permute-start | bytes 98312 | tf_op jit(solution)/shard_map/ppermute | solution.py:320
  26.6 5.6 %collective-permute-start.8 = (f32[48,256]{1,0:T(8,128)S(1)}, f32[48,256]{1,0:T(8,128)S(1)}, u32[]{:S(2)}, u32[]{:S(2)}) collective-permute-start(f32[48,256]{1,0:T(8,128)S(1)} %get-tuple-element.54), channel_id=1, source_target_pairs={{0,4},{1,5},{2,6},{3,7},{4,0},{5,1},{6,2},{7,3},{8,12},{9,13},{10,... | collective-permute-start | bytes 147464 | tf_op jit(solution)/shard_map/ppermute | solution.py:435
  27.9 5.9 %collective-permute-start.9 = (f32[48,256]{1,0:T(8,128)S(1)}, f32[48,256]{1,0:T(8,128)S(1)}, u32[]{:S(2)}, u32[]{:S(2)}) collective-permute-start(f32[48,256]{1,0:T(8,128)S(1)} %get-tuple-element.55), channel_id=1, source_target_pairs={{0,6},{1,7},{2,4},{3,5},{4,2},{5,3},{6,0},{7,1},{8,14},{9,15},{10,... | collective-permute-start | bytes 147464 | tf_op jit(solution)/shard_map/ppermute | solution.py:435
  29.0 4.7 %collective-permute-start.10 = (f32[48,256]{1,0:T(8,128)S(1)}, f32[48,256]{1,0:T(8,128)S(1)}, u32[]{:S(2)}, u32[]{:S(2)}) collective-permute-start(f32[48,256]{1,0:T(8,128)S(1)} %get-tuple-element.56), channel_id=1, source_target_pairs={{0,2},{1,3},{2,0},{3,1},{4,6},{5,7},{6,4},{7,5},{8,10},{9,11},{10,... | collective-permute-start | bytes 147464 | tf_op jit(solution)/shard_map/ppermute | solution.py:435
  34.2 3.1 %collective-permute-start.13 = (f32[3,128]{1,0:T(4,128)S(1)}, f32[3,128]{1,0:T(4,128)S(1)}, u32[]{:S(2)}, u32[]{:S(2)}) collective-permute-start(f32[3,128]{1,0:T(4,128)S(1)} %get-tuple-element.59), channel_id=1, source_target_pairs={{0,24},{8,16},{16,8},{24,0},{1,25},{9,17},{17,9},{25,1},{2,26},{10... | collective-permute-start | bytes 4616 | tf_op jit(solution)/shard_map/ppermute | solution.py:326
  34.2 3.7 %collective-permute-start.12 = (f32[3,128]{1,0:T(4,128)S(1)}, f32[3,128]{1,0:T(4,128)S(1)}, u32[]{:S(2)}, u32[]{:S(2)}) collective-permute-start(f32[3,128]{1,0:T(4,128)S(1)} %get-tuple-element.59), channel_id=1, source_target_pairs={{0,16},{8,24},{16,0},{24,8},{1,17},{9,25},{17,1},{25,9},{2,18},{10... | collective-permute-start | bytes 4616 | tf_op jit(solution)/shard_map/ppermute | solution.py:326
  38.3 4.0 %collective-permute-start.14 = (f32[32,256]{1,0:T(8,128)S(1)}, f32[32,256]{1,0:T(8,128)S(1)}, u32[]{:S(2)}, u32[]{:S(2)}) collective-permute-start(f32[32,256]{1,0:T(8,128)S(1)} %get-tuple-element.63.terms_ref), channel_id=1, source_target_pairs={{0,1},{1,0},{2,3},{3,2},{4,5},{5,4},{6,7},{7,6},{8,9},{9,8},{10,11... | collective-permute-start | bytes 98312 | tf_op jit(solution)/shard_map/ppermute | solution.py:320
  42.5 6.0 %collective-permute-start.15 = (f32[48,256]{1,0:T(8,128)S(1)}, f32[48,256]{1,0:T(8,128)S(1)}, u32[]{:S(2)}, u32[]{:S(2)}) collective-permute-start(f32[48,256]{1,0:T(8,128)S(1)} %get-tuple-element.64), channel_id=1, source_target_pairs={{0,4},{1,5},{2,6},{3,7},{4,0},{5,1},{6,2},{7,3},{8,12},{9,13},{10,... | collective-permute-start | bytes 147464 | tf_op jit(solution)/shard_map/ppermute | solution.py:435
  43.6 6.0 %collective-permute-start.16 = (f32[48,256]{1,0:T(8,128)S(1)}, f32[48,256]{1,0:T(8,128)S(1)}, u32[]{:S(2)}, u32[]{:S(2)}) collective-permute-start(f32[48,256]{1,0:T(8,128)S(1)} %get-tuple-element.65), channel_id=1, source_target_pairs={{0,6},{1,7},{2,4},{3,5},{4,2},{5,3},{6,0},{7,1},{8,14},{9,15},{10,... | collective-permute-start | bytes 147464 | tf_op jit(solution)/shard_map/ppermute | solution.py:435
  45.3 4.6 %collective-permute-start.17 = (f32[48,256]{1,0:T(8,128)S(1)}, f32[48,256]{1,0:T(8,128)S(1)}, u32[]{:S(2)}, u32[]{:S(2)}) collective-permute-start(f32[48,256]{1,0:T(8,128)S(1)} %get-tuple-element.66), channel_id=1, source_target_pairs={{0,2},{1,3},{2,0},{3,1},{4,6},{5,7},{6,4},{7,5},{8,10},{9,11},{10,... | collective-permute-start | bytes 147464 | tf_op jit(solution)/shard_map/ppermute | solution.py:435
  50.4 3.1 %collective-permute-start.20 = (f32[3,128]{1,0:T(4,128)S(1)}, f32[3,128]{1,0:T(4,128)S(1)}, u32[]{:S(2)}, u32[]{:S(2)}) collective-permute-start(f32[3,128]{1,0:T(4,128)S(1)} %get-tuple-element.69), channel_id=1, source_target_pairs={{0,24},{8,16},{16,8},{24,0},{1,25},{9,17},{17,9},{25,1},{2,26},{10... | collective-permute-start | bytes 4616 | tf_op jit(solution)/shard_map/ppermute | solution.py:326
  50.4 3.7 %collective-permute-start.19 = (f32[3,128]{1,0:T(4,128)S(1)}, f32[3,128]{1,0:T(4,128)S(1)}, u32[]{:S(2)}, u32[]{:S(2)}) collective-permute-start(f32[3,128]{1,0:T(4,128)S(1)} %get-tuple-element.69), channel_id=1, source_target_pairs={{0,16},{8,24},{16,0},{24,8},{1,17},{9,25},{17,1},{25,9},{2,18},{10... | collective-permute-start | bytes 4616 | tf_op jit(solution)/shard_map/ppermute | solution.py:326
  54.5 4.0 %collective-permute-start.21 = (f32[32,256]{1,0:T(8,128)S(1)}, f32[32,256]{1,0:T(8,128)S(1)}, u32[]{:S(2)}, u32[]{:S(2)}) collective-permute-start(f32[32,256]{1,0:T(8,128)S(1)} %get-tuple-element.72.terms_ref), channel_id=1, source_target_pairs={{0,1},{1,0},{2,3},{3,2},{4,5},{5,4},{6,7},{7,6},{8,9},{9,8},{10,11... | collective-permute-start | bytes 98312 | tf_op jit(solution)/shard_map/ppermute | solution.py:320
  58.6 5.7 %collective-permute-start.22 = (f32[48,256]{1,0:T(8,128)S(1)}, f32[48,256]{1,0:T(8,128)S(1)}, u32[]{:S(2)}, u32[]{:S(2)}) collective-permute-start(f32[48,256]{1,0:T(8,128)S(1)} %get-tuple-element.73), channel_id=1, source_target_pairs={{0,4},{1,5},{2,6},{3,7},{4,0},{5,1},{6,2},{7,3},{8,12},{9,13},{10,... | collective-permute-start | bytes 147464 | tf_op jit(solution)/shard_map/ppermute | solution.py:435
  59.4 6.0 %collective-permute-start.23 = (f32[48,256]{1,0:T(8,128)S(1)}, f32[48,256]{1,0:T(8,128)S(1)}, u32[]{:S(2)}, u32[]{:S(2)}) collective-permute-start(f32[48,256]{1,0:T(8,128)S(1)} %get-tuple-element.74), channel_id=1, source_target_pairs={{0,6},{1,7},{2,4},{3,5},{4,2},{5,3},{6,0},{7,1},{8,14},{9,15},{10,... | collective-permute-start | bytes 147464 | tf_op jit(solution)/shard_map/ppermute | solution.py:435
  61.2 4.6 %collective-permute-start.24 = (f32[48,256]{1,0:T(8,128)S(1)}, f32[48,256]{1,0:T(8,128)S(1)}, u32[]{:S(2)}, u32[]{:S(2)}) collective-permute-start(f32[48,256]{1,0:T(8,128)S(1)} %get-tuple-element.75), channel_id=1, source_target_pairs={{0,2},{1,3},{2,0},{3,1},{4,6},{5,7},{6,4},{7,5},{8,10},{9,11},{10,... | collective-permute-start | bytes 147464 | tf_op jit(solution)/shard_map/ppermute | solution.py:435
  66.3 3.1 %collective-permute-start.27 = (f32[3,128]{1,0:T(4,128)S(1)}, f32[3,128]{1,0:T(4,128)S(1)}, u32[]{:S(2)}, u32[]{:S(2)}) collective-permute-start(f32[3,128]{1,0:T(4,128)S(1)} %get-tuple-element.79), channel_id=1, source_target_pairs={{0,24},{8,16},{16,8},{24,0},{1,25},{9,17},{17,9},{25,1},{2,26},{10... | collective-permute-start | bytes 4616 | tf_op jit(solution)/shard_map/ppermute | solution.py:326
  66.3 3.7 %collective-permute-start.26 = (f32[3,128]{1,0:T(4,128)S(1)}, f32[3,128]{1,0:T(4,128)S(1)}, u32[]{:S(2)}, u32[]{:S(2)}) collective-permute-start(f32[3,128]{1,0:T(4,128)S(1)} %get-tuple-element.79), channel_id=1, source_target_pairs={{0,16},{8,24},{16,0},{24,8},{1,17},{9,25},{17,1},{25,9},{2,18},{10... | collective-permute-start | bytes 4616 | tf_op jit(solution)/shard_map/ppermute | solution.py:326
  (7 other events, 31.2 us)
